TPU v7x, 32 devices: a whole 2x2x4 slice. The times are simulated.
32 devices in a mesh: dp: 8 (over y, x, core), fsdp: 4 (over z).
Axes of the slice: x: 2, y: 2, z: 4, core: 2. Of those that a mesh axis runs over, the one named last changes fastest.
Arguments:
- token_ids: int32 [32, 512], P(('dp', 'fsdp')), may hold values from 0 to 7999
- targets: int32 [32, 512], P(('dp', 'fsdp')), may hold values from 0 to 7999
- target_counts: int32 [32], P(('dp', 'fsdp')), may hold values from 1 to 512, as said below
- memory: bfloat16 [32, 512, 1024], P(('dp', 'fsdp')), may hold values from -8 to 8
- value_routes: int32 [32, 1024, 4, 2], P(('dp', 'fsdp')), may hold values from 0 to 4, as said below
- value_slots: int32 [32, 1024, 4, 2], P(('dp', 'fsdp')), may hold values from 0 to 512, as said below
- output_routes: int32 [32, 512, 4, 2], P(('dp', 'fsdp')), may hold values from 0 to 4, as said below
- output_slots: int32 [32, 512, 4, 2], P(('dp', 'fsdp')), may hold values from 0 to 256, as said below
- embedding: float32 [8000, 1024], P('fsdp', 'dp')
- momentum_embedding: float32 [8000, 1024], P('fsdp', 'dp'), may hold values from -2.670288e-05 to 2.670288e-05
- average_embedding: float32 [8000, 1024], P('fsdp', 'dp'), may hold values from -0.1875 to 0.1875
- projector: float32 [1024, 936], P(('dp', 'fsdp')), may hold values from -0.15625 to 0.15625
- momentum_projector: float32 [1024, 936], P(('dp', 'fsdp')), may hold values from -2.670288e-05 to 2.670288e-05
- average_projector: float32 [1024, 936], P(('dp', 'fsdp')), may hold values from -0.15625 to 0.15625
- position: float32 [1024, 448], P(('dp', 'fsdp')), may hold values from -0.25 to 0.25
- momentum_position: float32 [1024, 448], P(('dp', 'fsdp')), may hold values from -2.670288e-05 to 2.670288e-05
- average_position: float32 [1024, 448], P(('dp', 'fsdp')), may hold values from -0.25 to 0.25
- values: float32 [1024, 2240], P(('dp', 'fsdp')), may hold values from -0.1875 to 0.1875
- momentum_values: float32 [1024, 2240], P(('dp', 'fsdp')), may hold values from -2.670288e-05 to 2.670288e-05
- average_values: float32 [1024, 2240], P(('dp', 'fsdp')), may hold values from -0.1875 to 0.1875
- outputs: float32 [2240, 1024], P(None, ('dp', 'fsdp')), may hold values from -3 to 3
- momentum_outputs: float32 [2240, 1024], P(None, ('dp', 'fsdp')), may hold values from -7.1525574e-07 to 7.1525574e-07
- average_outputs: float32 [2240, 1024], P(None, ('dp', 'fsdp')), may hold values from -3 to 3
- expand: float32 [1024, 4096], P(('dp', 'fsdp')), may hold values from -0.1875 to 0.1875
- momentum_expand: float32 [1024, 4096], P(('dp', 'fsdp')), may hold values from -2.670288e-05 to 2.670288e-05
- average_expand: float32 [1024, 4096], P(('dp', 'fsdp')), may hold values from -0.1875 to 0.1875
- contract: float32 [4096, 1024], P(None, ('dp', 'fsdp')), may hold values from -0.125 to 0.125
- momentum_contract: float32 [4096, 1024], P(None, ('dp', 'fsdp')), may hold values from -2.670288e-05 to 2.670288e-05
- average_contract: float32 [4096, 1024], P(None, ('dp', 'fsdp')), may hold values from -0.125 to 0.125
- vectors: float32 [4, 1024], P(None, ('dp', 'fsdp'))
- momentum_vectors: float32 [4, 1024], P(None, ('dp', 'fsdp')), may hold values from -2.670288e-05 to 2.670288e-05
- average_vectors: float32 [4, 1024], P(None, ('dp', 'fsdp')), may hold values from 0.5 to 1.5
- biases: float32 [4992], replicated, may hold values from -3 to 3
- momentum_biases: float32 [4992], replicated, may hold values from -2.670288e-05 to 2.670288e-05
- average_biases: float32 [4992], replicated, may hold values from -3 to 3
Outputs:
- loss_total: float32 [], replicated
- token_count: float32 [], replicated
- gradient_norm: float32 [], replicated
- velocity_embedding: float32 [8000, 1024], P('fsdp', 'dp')
- updated_embedding: float32 [8000, 1024], P('fsdp', 'dp')
- smoothed_embedding: float32 [8000, 1024], P('fsdp', 'dp')
- velocity_projector: float32 [1024, 936], P(('dp', 'fsdp'))
- updated_projector: float32 [1024, 936], P(('dp', 'fsdp'))
- smoothed_projector: float32 [1024, 936], P(('dp', 'fsdp'))
- velocity_position: float32 [1024, 448], P(('dp', 'fsdp'))
- updated_position: float32 [1024, 448], P(('dp', 'fsdp'))
- smoothed_position: float32 [1024, 448], P(('dp', 'fsdp'))
- velocity_values: float32 [1024, 2240], P(('dp', 'fsdp'))
- updated_values: float32 [1024, 2240], P(('dp', 'fsdp'))
- smoothed_values: float32 [1024, 2240], P(('dp', 'fsdp'))
- velocity_outputs: float32 [2240, 1024], P(None, ('dp', 'fsdp'))
- updated_outputs: float32 [2240, 1024], P(None, ('dp', 'fsdp'))
- smoothed_outputs: float32 [2240, 1024], P(None, ('dp', 'fsdp'))
- velocity_expand: float32 [1024, 4096], P(('dp', 'fsdp'))
- updated_expand: float32 [1024, 4096], P(('dp', 'fsdp'))
- smoothed_expand: float32 [1024, 4096], P(('dp', 'fsdp'))
- velocity_contract: float32 [4096, 1024], P(None, ('dp', 'fsdp'))
- updated_contract: float32 [4096, 1024], P(None, ('dp', 'fsdp'))
- smoothed_contract: float32 [4096, 1024], P(None, ('dp', 'fsdp'))
- velocity_vectors: float32 [4, 1024], P(None, ('dp', 'fsdp'))
- updated_vectors: float32 [4, 1024], P(None, ('dp', 'fsdp'))
- smoothed_vectors: float32 [4, 1024], P(None, ('dp', 'fsdp'))
- velocity_biases: float32 [4992], replicated
- updated_biases: float32 [4992], replicated
- smoothed_biases: float32 [4992], replicated
Inputs may be any that keep to these rules, and one draw needn't show every extreme that they name: Each segment counts its first target_counts positions; the last segment counts all 512. `value_routes`: the two experts of one position and head differ. `value_slots`: within one segment and head, the routes to one expert are numbered 0, 1, 2, ... over all first choices in position order and then all second choices; a route numbered 512 or more carries 512 and is dropped; in every segment and head some expert drops routes. `output_routes`: the two experts of one position and head differ. `output_slots`: within one segment and head, the routes to one expert are numbered 0, 1, 2, ... over all first choices in position order and then all second choices; a route numbered 256 or more carries 256 and is dropped; in every segment and head some expert drops routes.
All inputs are finite; a program needn't handle non-finite values.
Results may differ from a plain program's by a relative error of at most 0.0084.
Values may be sent and summed in bfloat16 or wider, within the bound.
No kernel may reach another device: no remote copies, remote signals or barrier semaphores. Data moves between devices by JAX's collectives and lax.ppermute only.
A program may use at most 384 MiB of HBM per device.

v0:
```python
import functools
import math

import jax
import jax.numpy as jnp
from jax import lax
from jax.experimental import pallas as pl
from jax.experimental.pallas import tpu as pltpu
from jax.sharding import PartitionSpec as P

D = 1024
H = 4
DH = 112
NE = 5
FF = 4096
V = 8000
SEG = 512
MEM = 512
STEP = 8
SPAN = 1024
CAPV = 512
CAPO = 256
HD = H * DH
QUERIES = 2 * HD
VALUE_ROW = 0
OUTPUT_ROW = 2240
QUERY_ROW = 4480
POSITION_ROW = 5376
GATE_ROW = 5824
GATES = 2 * H * NE
LAST_ROWS = 64
PARAMS = 22594432

eps = 1e-05
clip_norm = 0.02
momentum_decay = 0.9
rate_base = 10.0
rate_factors = (1.0, 1.0, 1.0, 1.0, 500.0, 1.0, 1.0, 1.0, 8.0)
masked = -1e30
scale = DH ** (-0.5)
bfloat = jnp.bfloat16
single = jnp.float32
DP, FSDP = "dp", "fsdp"
BOTH = (DP, FSDP)
vmem_bytes = 56 * 1024 * 1024
params = pltpu.CompilerParams(vmem_limit_bytes=vmem_bytes)
light = pl.CostEstimate(flops=10**7, bytes_accessed=10**5, transcendentals=0)


def dot(left, right, left_dim, right_dim):
    return lax.dot_general(
        left, right, (((left_dim,), (right_dim,)), ((), ())), preferred_element_type=single
    )


class Grid:
    def __init__(self):
        self.n_dp = lax.axis_size(DP)
        self.n_fsdp = lax.axis_size(FSDP)
        self.count = self.n_dp * self.n_fsdp
        assert self.count & (self.count - 1) == 0
        self.dp_index = lax.axis_index(DP)
        self.fsdp_index = lax.axis_index(FSDP)
        inner = []
        bit = 2
        while bit < self.n_dp:
            inner.append(bit)
            bit *= 2
        self.layout = ([1] if self.n_dp > 1 else []) + inner[::-1]

        self.sent, self.before = [], ()
        self.summed = []

    def swap(self, part, dp_bits, fsdp_bits=0):
        flip = dp_bits * self.n_fsdp + fsdp_bits
        return lax.ppermute(part, BOTH, [(i, i ^ flip) for i in range(self.count)])

    def queued(self, part, dp_bits, fsdp_bits=0):
        self.sent.append(self.swap(after(part, *self.before), dp_bits, fsdp_bits))
        return self.sent[-1]

    def step(self, *ties):
        self.before, self.sent = tuple(self.sent) + ties, []

    def relative_blocks(self):
        found = [0]
        for bit in self.layout:
            found = [f + b for f in found for b in (0, bit)]
        return found


def after(value, *others):
    return lax.optimization_barrier((value,) + others)[0]


def turn_kernel(in_ref, out_ref):
    out_ref[...] = in_ref[...].T


def turned_block(block):
    rows, columns = block.shape
    return pl.pallas_call(
        turn_kernel,
        grid=(2,),
        in_specs=[pl.BlockSpec((rows, columns // 2), lambda i: (0, i))],
        out_specs=pl.BlockSpec((columns // 2, rows), lambda i: (i, 0)),
        out_shape=jax.ShapeDtypeStruct((columns, rows), block.dtype),
        compiler_params=params,
        cost_estimate=light,
    )(block)


class Gather:
    def __init__(self, grid, shard, turned=False):
        self.grid, self.shard, self.turned = grid, shard, turned

    def direct_line(self):
        grid = self.grid
        self.pieces = [self.shard] + [grid.queued(self.shard, 0, k) for k in range(1, grid.n_fsdp)]
        self.finish_line()

    def first_line(self):
        grid = self.grid
        self.pieces = [self.shard, grid.queued(self.shard, 0, 1)] if grid.n_fsdp > 1 else [self.shard]

    def second_line(self):
        grid = self.grid
        height = self.shard.shape[0]
        bit = 2
        while bit < grid.n_fsdp:
            away = grid.queued(jnp.concatenate(self.pieces, axis=0), 0, bit)
            self.pieces += [away[i * height : (i + 1) * height] for i in range(bit)]
            bit *= 2
        self.finish_line()

    def finish_line(self):
        grid, pieces = self.grid, self.pieces
        bit = 1
        while bit < grid.n_fsdp:
            odd = (grid.fsdp_index & bit) != 0
            pieces = [jnp.where(odd, pieces[i ^ bit], pieces[i]) for i in range(grid.n_fsdp)]
            bit *= 2
        self.line = jnp.concatenate(pieces, axis=0)
        if self.turned:
            self.line = turned_block(self.line)

    def neighbours(self, *ties):
        grid, block = self.grid, after(self.line, *ties)
        self.line = block
        inner = grid.layout[1:]
        self.pieces = [block]
        if len(inner) == 2:
            outer, near = inner
            self.pieces += [grid.queued(block, near), grid.queued(block, outer)]
        else:
            for bit in inner[::-1]:
                self.pieces = [jnp.concatenate(self.pieces, axis=0)]
                self.pieces.append(grid.queued(self.pieces[0], bit))

    def opposite(self, *ties):
        grid = self.grid
        inner = grid.layout[1:]
        if len(inner) == 2:
            outer, near = inner
            middle = self.line.shape[0] // 32 * 16
            self.pieces += [
                grid.queued(after(self.pieces[1][:middle], *ties), outer),
                grid.queued(after(self.pieces[2][middle:], *ties), near),
            ]
        self.own = jnp.concatenate(self.pieces, axis=0)

    def pair(self):
        self.other = self.grid.queued(self.own, 1)

    def rows(self):
        return jnp.concatenate([self.own, self.other], axis=0)

    def by_block(self):
        sides = [side.reshape(-1, *self.line.shape) for side in (self.own, self.other)]
        if self.line.shape[1] % 128:
            sides = [jnp.concatenate(list(side), axis=1)[None] for side in sides]
        return tuple(sides)

    def columns(self):
        count = self.line.shape[0]
        return jnp.concatenate(
            [
                side[i : i + count]
                for side in (self.own, self.other)
                for i in range(0, side.shape[0], count)
            ],
            axis=1,
        )


def opposite_and_neighbours(one, two):
    grid = one.grid
    inner = grid.layout[1:]
    if len(inner) != 2:
        one.opposite()
        two.neighbours()
        return
    outer, near = inner
    middle = one.line.shape[0] // 32 * 16
    first = jnp.concatenate([one.pieces[1][:middle], two.line], axis=0)
    second = jnp.concatenate([one.pieces[2][middle:], two.line], axis=0)
    first, second = grid.queued(first, outer), grid.queued(second, near)
    one.pieces += [first[:middle], second[: one.line.shape[0] - middle]]
    one.own = jnp.concatenate(one.pieces, axis=0)
    two.pieces = [two.line, second[one.line.shape[0] - middle :], first[middle:]]


class Reduce:
    def __init__(self, grid, low, high, columns=False, turned=False):
        self.grid, self.low, self.high = grid, low, high
        self.columns, self.turned = columns, turned

    def pair(self, *ties):
        self.high = self.high(ties).astype(bfloat)
        self.came = self.grid.queued(self.high, 1)
        return self.high

    def opposite(self, *ties):
        grid = self.grid
        total = (self.low(ties) + self.came.astype(single)).astype(bfloat)
        if self.columns:
            width = D // grid.n_dp
            self.blocks = [total[:, i : i + width] for i in range(0, total.shape[1], width)]
        else:
            height = total.shape[0] // (grid.n_dp // 2)
            self.blocks = [total[i : i + height] for i in range(0, total.shape[0], height)]
        inner = grid.layout[1:]
        if len(inner) == 2:
            outer, near = inner
            self.middle = self.blocks[3].shape[0] // 32 * 16
            one, two = self.blocks[3][: self.middle], self.blocks[3][self.middle :]
            self.first, self.second = grid.queued(one, outer), grid.queued(two, near)
            self.met = (self.first, self.second)
            return one, two
        self.met = ()
        return (total,)

    def neighbours(self):
        grid = self.grid
        inner = grid.layout[1:]
        self.sums = []
        if len(inner) == 2:
            outer, near = inner
            rows, middle = self.blocks[0].shape[0], self.middle
            first, second = self.first.astype(single), self.second.astype(single)
            to_near = self.blocks[1].astype(single) + jnp.pad(first, ((0, rows - middle), (0, 0)))
            to_outer = self.blocks[2].astype(single) + jnp.pad(second, ((middle, 0), (0, 0)))
            one, two = to_near.astype(bfloat), to_outer.astype(bfloat)
            self.sums = [grid.queued(one, near), grid.queued(two, outer)]
            total = self.blocks[0].astype(single)
            for part in self.sums:
                total = total + part.astype(single)
            self.block = total.astype(bfloat)
            return one, two
        total = jnp.stack(self.blocks)
        for bit in inner:
            middle = total.shape[0] // 2
            away = grid.queued(total[middle:], bit)
            total = (total[:middle].astype(single) + away.astype(single)).astype(bfloat)
        self.block = total[0]
        return (total,)

    def along_line(self):
        block = self.block.T if self.turned else self.block
        if self.grid.summed:
            block = after(block, self.grid.summed[-1])
        self.shard = lax.psum_scatter(block, FSDP, scatter_dimension=0, tiled=True)
        self.grid.summed.append(self.shard)

    def value(self):
        return self.shard.astype(single)


def total_everywhere(grid, part):
    bit = 1
    while bit < grid.n_dp:
        part = part + grid.swap(part, bit)
        bit *= 2
    bit = 1
    while bit < grid.n_fsdp:
        part = part + grid.swap(part, 0, bit)
        bit *= 2
    return part


def normalised(values):
    centred = values - jnp.mean(values, axis=-1, keepdims=True)
    spread = lax.rsqrt(jnp.mean(centred * centred, axis=-1, keepdims=True) + eps)
    return centred * spread, spread


def norm_gradient(grad, normal, spread, gain):
    scaled = grad * gain
    mean_one = jnp.mean(scaled, axis=-1, keepdims=True)
    mean_two = jnp.mean(scaled * normal, axis=-1, keepdims=True)
    return spread * (scaled - mean_one - normal * mean_two), jnp.sum(grad * normal, axis=0)


def gelu_exact(values):
    return jax.nn.gelu(values, approximate=False)


def positions(length, features):
    distances = jnp.arange(length, dtype=single)[::-1]
    freqs = jnp.exp(jnp.arange(features // 2, dtype=single) * (-2.0 * math.log(10000.0) / features))
    angles = distances[:, None] * freqs[None, :]
    return jnp.concatenate([jnp.sin(angles), jnp.cos(angles)], axis=1)


def lanes(*sides):
    return jnp.concatenate([side[i] for side in sides for i in range(side.shape[0])], axis=1)


def sums_of_experts(gates, blocks):
    return sum(gates[e : e + 1] * blocks[e * DH : (e + 1) * DH] for e in range(NE))


def each_expert(gates, block):
    return jnp.concatenate([gates[e : e + 1] * block for e in range(NE)], axis=0).astype(bfloat)


def expert_products(blocks, block):
    sums = [
        jnp.sum(blocks[e * DH : (e + 1) * DH].astype(single) * block, axis=0, keepdims=True)
        for e in range(NE)
    ]
    return jnp.concatenate(sums + [jnp.zeros_like(sums[0])] * (8 - NE), axis=0)


def mix_kernel(*refs):
    normed, rel, *sides = refs[:12]
    content_ref, position_ref, value_gate, output_gate = refs[12:16]
    qa_ref, qb_ref, k_ref, r_ref, v_ref, o_ref, p_ref, every_ref, gated_ref, out_ref = refs[16:]
    query, key, far, value, output = (lanes(*sides[i : i + 2]) for i in range(0, 10, 2))
    queries = dot(query, normed[MEM:, :], 1, 1)
    qa_ref[0] = (queries + content_ref[0]).astype(bfloat)
    qb_ref[0] = (queries + position_ref[0]).astype(bfloat)
    k_ref[0] = dot(key, normed[...], 1, 1).astype(bfloat)
    r_ref[0] = dot(far, rel[...], 1, 1).astype(bfloat)
    every = dot(value, normed[...], 1, 1)
    every_ref[0] = every.astype(bfloat)
    v_ref[0] = sums_of_experts(value_gate[0], every).astype(bfloat)
    bias = dot(qb_ref[0], r_ref[0], 0, 0)
    bias = pltpu.roll(bias, SPAN - SEG + 1, 1, stride=1, stride_axis=0)
    row = lax.broadcasted_iota(jnp.int32, (SEG, SPAN), 0)
    column = lax.broadcasted_iota(jnp.int32, (SEG, SPAN), 1)
    scores = (dot(qa_ref[0], k_ref[0], 0, 0) + bias) * scale
    scores = jnp.where(column <= MEM + row, scores, masked)
    powers = jnp.exp(scores - jnp.max(scores, axis=1, keepdims=True))
    weights = powers / jnp.sum(powers, axis=1, keepdims=True)
    p_ref[0] = weights
    attended = dot(v_ref[0], weights.astype(bfloat), 1, 1).astype(bfloat)
    o_ref[0] = attended
    gated = each_expert(output_gate[0], attended.astype(single))
    gated_ref[0] = gated

    @pl.when(pl.program_id(0) == 0)
    def _():
        out_ref[...] = jnp.zeros_like(out_ref)

    out_ref[...] += dot(gated, output, 0, 0)


def mix_back_kernel(*refs):
    grad_ref, *sides = refs[:9]
    qa_ref, qb_ref, k_ref, r_ref, v_ref, o_ref, p_ref, every_ref, value_gate, output_gate = refs[9:19]
    dq_ref, dk_ref, dr_ref, dv_ref, dzv_ref, dzo_ref, du_ref, dw_ref, out_ref = refs[19:]
    query, key, value, output = (lanes(*sides[i : i + 2]) for i in range(0, 8, 2))
    back = dot(output, grad_ref[...], 1, 1)
    gate = output_gate[0]
    dzo_ref[0] = expert_products(back, o_ref[0].astype(single)) * gate * (1.0 - gate)
    grad_out = sums_of_experts(gate, back).astype(bfloat)
    weights = p_ref[0]
    grad_mixed = dot(grad_out, weights.astype(bfloat), 1, 0).astype(bfloat).astype(single)
    grad = dot(grad_out, v_ref[0], 0, 0).astype(bfloat).astype(single)
    grad = weights * (grad - jnp.sum(grad * weights, axis=1, keepdims=True)) * scale
    low = grad.astype(bfloat)
    grad_qa = dot(k_ref[0], low, 1, 1).astype(bfloat).astype(single)
    grad_key = dot(qa_ref[0], low, 1, 0).astype(bfloat)
    row = lax.broadcasted_iota(jnp.int32, (SEG, SEG), 0)
    column = lax.broadcasted_iota(jnp.int32, (SEG, SEG), 1)
    turn = jnp.where(row + column == SEG - 1, 1.0, 0.0).astype(bfloat)
    far = pltpu.roll(dot(turn, low, 1, 0), 0, 1, stride=1, stride_axis=0).astype(bfloat)
    dr_ref[0] = dot(dot(qb_ref[0], turn, 1, 0).astype(bfloat), far, 1, 0).astype(bfloat)
    grad_qb = dot(dot(r_ref[0], far, 1, 1).astype(bfloat), turn, 1, 0)
    du_ref[0] = jnp.sum(grad_qa, axis=1, keepdims=True)
    dw_ref[0] = jnp.sum(grad_qb, axis=1, keepdims=True)
    grad_query = (grad_qa + grad_qb).astype(bfloat)
    dq_ref[0, :, :MEM] = jnp.zeros((DH, MEM), bfloat)
    dq_ref[0, :, MEM:] = grad_query
    dk_ref[0] = grad_key
    gate = value_gate[0]
    dzv_ref[0] = expert_products(every_ref[0], grad_mixed) * gate * (1.0 - gate)
    grad_value = each_expert(gate, grad_mixed)
    dv_ref[0] = grad_value

    @pl.when(pl.program_id(0) == 0)
    def _():
        out_ref[...] = jnp.zeros_like(out_ref)

    out_ref[...] += dot(grad_key, key, 0, 0) + dot(grad_value, value, 0, 0)
    out_ref[MEM:, :] += dot(grad_query, query, 0, 0)


def head_rows(rows, columns, dtype=bfloat):
    block = pl.BlockSpec((1, rows, columns), lambda h: (h, 0, 0))
    return block, jax.ShapeDtypeStruct((H, rows, columns), dtype)


def weight_blocks(sides, start, rows):
    blocks, _, width = sides[0].shape
    return [pl.BlockSpec((blocks, rows, width), lambda h: (0, start // rows + h, 0))] * 2


def fixed(rows, columns):
    return pl.BlockSpec((rows, columns), lambda *_: (0, 0))


EXPERT = NE * DH


def mix(normed, rel, sides, content, position, value_gates, output_gates):
    outs = [
        head_rows(DH, SEG),
        head_rows(DH, SEG),
        head_rows(DH, SPAN),
        head_rows(DH, SPAN),
        head_rows(DH, SPAN),
        head_rows(DH, SEG),
        head_rows(SEG, SPAN, single),
        head_rows(EXPERT, SPAN),
        head_rows(EXPERT, SEG),
        (fixed(SEG, D), jax.ShapeDtypeStruct((SEG, D), single)),
    ]
    return pl.pallas_call(
        mix_kernel,
        grid=(H,),
        in_specs=[fixed(SPAN, D), fixed(SPAN, D)]
        + weight_blocks(sides, QUERY_ROW, DH)
        + weight_blocks(sides, QUERY_ROW + HD, DH)
        + weight_blocks(sides, POSITION_ROW, DH)
        + weight_blocks(sides, VALUE_ROW, EXPERT)
        + weight_blocks(sides, OUTPUT_ROW, EXPERT)
        + [head_rows(DH, 1)[0]] * 2
        + [head_rows(8, SPAN)[0], head_rows(8, SEG)[0]],
        out_specs=[spec for spec, _ in outs],
        out_shape=[shape for _, shape in outs],
        compiler_params=params,
        cost_estimate=light,
    )(normed, rel, *(sides * 5), content, position, value_gates, output_gates)


def mix_back(grad, sides, stored, value_gates, output_gates):
    outs = [
        head_rows(DH, SPAN),
        head_rows(DH, SPAN),
        head_rows(DH, SPAN),
        head_rows(EXPERT, SPAN),
        head_rows(8, SPAN, single),
        head_rows(8, SEG, single),
        head_rows(DH, 1, single),
        head_rows(DH, 1, single),
        (fixed(SPAN, D), jax.ShapeDtypeStruct((SPAN, D), single)),
    ]
    return pl.pallas_call(
        mix_back_kernel,
        grid=(H,),
        in_specs=[fixed(SEG, D)]
        + weight_blocks(sides, QUERY_ROW, DH)
        + weight_blocks(sides, QUERY_ROW + HD, DH)
        + weight_blocks(sides, VALUE_ROW, EXPERT)
        + weight_blocks(sides, OUTPUT_ROW, EXPERT)
        + [head_rows(*array.shape[1:])[0] for array in stored]
        + [head_rows(8, SPAN)[0], head_rows(8, SEG)[0]],
        out_specs=[spec for spec, _ in outs],
        out_shape=[shape for _, shape in outs],
        compiler_params=params,
        cost_estimate=light,
    )(grad, *(sides * 4), *stored, value_gates, output_gates)


ff_tile = 512
ff_columns = pl.BlockSpec((SEG, ff_tile), lambda i: (0, i))
ff_weights = pl.BlockSpec((D // 2, ff_tile), lambda i: (0, i))
ff_bias = pl.BlockSpec((1, ff_tile), lambda i: (0, i))


def expand_kernel(in_ref, own_ref, other_ref, bias_ref, act_ref, slope_ref):
    hidden = dot(in_ref[:, : D // 2], own_ref[...], 1, 0) + bias_ref[...]
    hidden = hidden + dot(in_ref[:, D // 2 :], other_ref[...], 1, 0)
    share = 0.5 + 0.5 * lax.erf(hidden * math.sqrt(0.5))
    act_ref[...] = (hidden * share).astype(bfloat)
    density = jnp.exp(hidden * hidden * -0.5) * (1.0 / math.sqrt(2.0 * math.pi))
    slope_ref[...] = (share + hidden * density).astype(bfloat)


def expand_forward(normed, sides, bias):
    wide = jax.ShapeDtypeStruct((SEG, FF), bfloat)
    return pl.pallas_call(
        expand_kernel,
        grid=(FF // ff_tile,),
        in_specs=[fixed(SEG, D), ff_weights, ff_weights, ff_bias],
        out_specs=[ff_columns, ff_columns],
        out_shape=[wide, wide],
        compiler_params=params,
        cost_estimate=light,
    )(normed, *sides, bias)


def contract_kernel(act_ref, own_ref, other_ref, out_ref):
    @pl.when(pl.program_id(0) == 0)
    def _():
        out_ref[...] = jnp.zeros_like(out_ref)

    out_ref[:, : D // 2] += dot(act_ref[...], own_ref[...], 1, 1)
    out_ref[:, D // 2 :] += dot(act_ref[...], other_ref[...], 1, 1)


def contract_forward(active, sides):
    return pl.pallas_call(
        contract_kernel,
        grid=(FF // ff_tile,),
        in_specs=[ff_columns, ff_weights, ff_weights],
        out_specs=fixed(SEG, D),
        out_shape=jax.ShapeDtypeStruct((SEG, D), single),
        compiler_params=params,
        cost_estimate=light,
    )(active, *sides)


def ff_back_kernel(
    in_ref, slope_ref, own_down, other_down, own_up, other_up, grad_ref, bias_ref, out_ref, total
):
    tile = pl.program_id(0)

    @pl.when(tile == 0)
    def _():
        total[...] = jnp.zeros_like(total)

    grad = dot(in_ref[:, : D // 2], own_down[...], 1, 0)
    grad = grad + dot(in_ref[:, D // 2 :], other_down[...], 1, 0)
    grad = grad.astype(bfloat).astype(single) * slope_ref[...].astype(single)
    low = grad.astype(bfloat)
    grad_ref[...] = low
    bias_ref[...] = jnp.sum(low.astype(single), axis=0, keepdims=True)
    total[:, : D // 2] += dot(low, own_up[...], 1, 1)
    total[:, D // 2 :] += dot(low, other_up[...], 1, 1)

    @pl.when(tile == pl.num_programs(0) - 1)
    def _():
        out_ref[...] = total[...].astype(bfloat)


def ff_back(grad, slope, down, up):
    return pl.pallas_call(
        ff_back_kernel,
        grid=(FF // ff_tile,),
        in_specs=[fixed(SEG, D), ff_columns] + [ff_weights] * 4,
        out_specs=[ff_columns, ff_bias, fixed(SEG, D)],
        out_shape=[
            jax.ShapeDtypeStruct((SEG, FF), bfloat),
            jax.ShapeDtypeStruct((1, FF), single),
            jax.ShapeDtypeStruct((SEG, D), bfloat),
        ],
        scratch_shapes=[pltpu.VMEM((SEG, D), single)],
        compiler_params=params,
        cost_estimate=light,
    )(grad, slope, *down, *up)


def lookup_kernel(first, ids_ref, own_ref, other_ref, out_ref):
    tile = pl.program_id(0)
    rows = own_ref.shape[1]
    place = first + tile * rows + lax.broadcasted_iota(jnp.int32, (SEG, rows), 1)
    chosen = jnp.where(ids_ref[...] == place, 1.0, 0.0).astype(bfloat)
    found = dot(chosen, lanes(own_ref, other_ref), 1, 0)

    @pl.when(tile == 0)
    def _():
        out_ref[...] = found

    @pl.when(tile > 0)
    def _():
        out_ref[...] += found


def lookup(ids, own, other, first):
    blocks, rows, width = own.shape
    tile = 1024
    side = pl.BlockSpec((blocks, tile, width), lambda i: (0, i, 0))
    return pl.pallas_call(
        functools.partial(lookup_kernel, first),
        grid=(rows // tile,),
        in_specs=[pl.BlockSpec((SEG, 1), lambda i: (0, 0)), side, side],
        out_specs=pl.BlockSpec((SEG, D), lambda i: (0, 0)),
        out_shape=jax.ShapeDtypeStruct((SEG, D), single),
        compiler_params=params,
        cost_estimate=light,
    )(ids, own, other)


head_tile = 512


def head_kernel(
    shard_rows,
    shard_half,
    hf_ref,
    goal_ref,
    counted_ref,
    own_zero,
    other_zero,
    own_one,
    other_one,
    grad_ref,
    back_ref,
    loss_ref,
    logits,
    total,
    highest,
    summed,
    picked,
):
    tiles = pl.num_programs(0) // 2
    step = pl.program_id(0)
    tile = lax.rem(step, tiles)
    at = pl.multiple_of(tile * head_tile, head_tile)
    place = at + lax.broadcasted_iota(jnp.int32, (SEG, head_tile), 1)
    hits = place == goal_ref[...]

    def each_table(use):
        @pl.when(tile < tiles // 2)
        def _():
            use(lanes(own_zero, other_zero), 0)

        @pl.when(tile >= tiles // 2)
        def _():
            use(lanes(own_one, other_one), shard_half)

    def groups(values):
        return [values[:, i : i + 128] for i in range(0, head_tile, 128)]

    @pl.when(step == 0)
    def _():
        highest[...] = jnp.full_like(highest, masked)
        summed[...] = jnp.zeros_like(summed)
        picked[...] = jnp.zeros_like(picked)
        total[...] = jnp.zeros_like(total)

    @pl.when(step < tiles)
    def _():
        def use(rows, late):
            scores = dot(hf_ref[...], rows, 1, 1)
            scores = jnp.where(lax.rem(place, shard_half) + late < shard_rows, scores, masked)
            logits[:, pl.ds(at, head_tile)] = scores
            parts = groups(scores)
            top = functools.reduce(jnp.maximum, parts, highest[...])
            powers = sum(jnp.exp(part - top) for part in parts)
            summed[...] = summed[...] * jnp.exp(highest[...] - top) + powers
            highest[...] = top
            picked[...] += sum(groups(jnp.where(hits, scores, 0.0)))

        each_table(use)

    @pl.when(step == tiles)
    def _():
        top = jnp.max(highest[...], axis=1, keepdims=True)
        powers = jnp.sum(summed[...] * jnp.exp(highest[...] - top), axis=1, keepdims=True)
        whole = top + jnp.log(powers)
        loss_ref[...] = (whole - jnp.sum(picked[...], axis=1, keepdims=True)) * counted_ref[...]
        highest[...] = jnp.broadcast_to(whole, highest.shape)

    @pl.when(step >= tiles)
    def _():
        def use(rows, late):
            shares = jnp.exp(logits[:, pl.ds(at, head_tile)] - highest[:, :1])
            grad = ((shares - jnp.where(hits, 1.0, 0.0)) * counted_ref[...]).astype(bfloat)
            grad_ref[...] = grad
            total[...] += dot(grad, rows, 1, 0)

        each_table(use)

    @pl.when(step == 2 * tiles - 1)
    def _():
        back_ref[...] = total[...].astype(bfloat)


def head(hf, goals, counted, parts, shard_rows, shard_half):
    blocks, rows, width = parts[0][0].shape
    half_tiles = rows // head_tile
    tiles = 2 * half_tiles

    def side(part):
        def index(i):
            return 0, jnp.clip(lax.rem(i, tiles) - part * half_tiles, 0, half_tiles - 1), 0

        return pl.BlockSpec((blocks, head_tile, width), index)

    column = pl.BlockSpec((SEG, 1), lambda i: (0, 0))
    whole = pl.BlockSpec((SEG, D), lambda i: (0, 0))
    return pl.pallas_call(
        functools.partial(head_kernel, shard_rows, shard_half),
        grid=(2 * tiles,),
        in_specs=[whole, column, column, side(0), side(0), side(1), side(1)],
        out_specs=[
            pl.BlockSpec((SEG, head_tile), lambda i: (0, jnp.maximum(i - tiles, 0))),
            whole,
            column,
        ],
        out_shape=[
            jax.ShapeDtypeStruct((SEG, 2 * rows), bfloat),
            jax.ShapeDtypeStruct((SEG, D), bfloat),
            jax.ShapeDtypeStruct((SEG, 1), single),
        ],
        scratch_shapes=[
            pltpu.VMEM((SEG, 2 * rows), single),
            pltpu.VMEM((SEG, D), single),
            pltpu.VMEM((SEG, 128), single),
            pltpu.VMEM((SEG, 128), single),
            pltpu.VMEM((SEG, 128), single),
        ],
        compiler_params=params,
        cost_estimate=light,
    )(hf, goals, counted, *parts[0], *parts[1])


def chosen_experts(routes, slots, capacity):
    experts = jnp.arange(NE, dtype=jnp.int32)[None, :, None, None]
    turned = jnp.transpose(routes, (1, 2, 0))[:, None]
    kept = jnp.transpose(slots, (1, 2, 0))[:, None] < capacity
    return jnp.sum(((turned == experts) & kept).astype(single), axis=2)


def advance(weight, velocity, average, grad, factor, step_rate):
    clipped = grad * factor
    velocity_next = momentum_decay * velocity + clipped
    updated = weight - step_rate * (clipped + momentum_decay * velocity_next)
    return (velocity_next, updated, average + (updated - average) / (STEP + 1))


def table_shape(grid):
    rows = V // grid.n_fsdp
    return rows, -(-rows // 256) * 128


def table_place(grid, ids):
    rows, part = table_shape(grid)
    owner, row = ids // rows, ids % rows
    return (row // part) * (grid.n_fsdp * part) + owner * part + row % part


def body(
    token_ids,
    targets,
    target_counts,
    memory,
    value_routes,
    value_slots,
    output_routes,
    output_slots,
    *states,
):
    masters, moments, averages = states[0::3], states[1::3], states[2::3]
    embedding, projector, position, values, outputs, expand, contract, vectors, biases = masters
    grid = Grid()
    ids = table_place(grid, token_ids[0])
    goals = table_place(grid, targets[0])
    half = D // 2
    chunk = D // grid.count

    shard_rows, shard_half = table_shape(grid)
    part_rows = shard_half * grid.n_fsdp
    table_shard = jnp.pad(embedding.astype(bfloat), ((0, 2 * shard_half - shard_rows), (0, 0)))
    expanding = Gather(grid, expand.astype(bfloat))
    contracting = Gather(grid, contract.T.astype(bfloat))
    tables = [Gather(grid, table_shard[i : i + shard_half]) for i in (0, shard_half)]
    attention_shard = jnp.concatenate(
        [
            values.astype(bfloat),
            outputs.T.astype(bfloat),
            projector[:, :QUERIES].astype(bfloat),
            position.astype(bfloat),
            projector[:, QUERIES:].astype(bfloat),
            vectors.T.astype(bfloat),
            jnp.zeros((chunk, LAST_ROWS - GATES - 4), bfloat),
        ],
        axis=1,
    )
    attending = Gather(grid, attention_shard, True)
    distances = jnp.array(grid.relative_blocks(), jnp.int32)
    width = D // grid.n_dp
    true_columns = (
        (distances[:, None] ^ grid.dp_index) * width + jnp.arange(width, dtype=jnp.int32)[None, :]
    ).reshape(D)
    to_order = (jnp.arange(D, dtype=jnp.int32)[:, None] == true_columns[None, :]).astype(bfloat)
    memory_rows = dot(memory[0], to_order, 1, 0)
    rel_table = dot(positions(SPAN, D).astype(bfloat), to_order, 1, 0).astype(bfloat)

    tables[0].direct_line()
    grid.step(memory_rows, rel_table)
    tables[0].neighbours()
    tables[1].direct_line()
    grid.step()
    opposite_and_neighbours(tables[0], tables[1])
    attending.direct_line()
    grid.step()
    middle = expand.shape[1]
    lines = lax.all_gather(
        after(jnp.concatenate([expanding.shard, contracting.shard], axis=1), *grid.before),
        FSDP,
        axis=0,
        tiled=True,
    )
    expanding.line, contracting.line = lines[:, :middle], lines[:, middle:]
    tables[1].opposite()
    tables[0].pair()
    attending.neighbours()
    grid.step()
    attending.opposite()
    expanding.neighbours()
    tables[1].pair()
    tables_by_block = [part.by_block() for part in tables]
    found = [lookup(ids[:, None], *tables_by_block[0], 0)]
    grid.step(found[0])
    attending.pair()
    expanding.opposite()
    contracting.neighbours()
    found.append(lookup(ids[:, None], *tables_by_block[1], part_rows))
    embedded = (found[0] + found[1]) * D**0.5
    grid.step(embedded)
    contracting.opposite()
    expanding.pair()
    grid.step()
    contracting.pair()
    attention = attending.by_block()
    last_rows = jnp.concatenate(
        [side[i, GATE_ROW:] for side in attention for i in range(side.shape[0])], axis=1
    )
    gains = last_rows[GATES : GATES + 4].astype(single)

    stream = jnp.concatenate([memory_rows, embedded], axis=0)
    normal_in, spread_in = normalised(stream)
    normed = (normal_in * gains[0]).astype(bfloat)
    logits = jax.nn.sigmoid(dot(last_rows, normed, 1, 1)[:GATES])

    def gates_of(shares, routes, slots, capacity):
        kept = shares.reshape(H, NE, -1) * chosen_experts(routes, slots, capacity)
        return jnp.pad(kept, ((0, 0), (0, 8 - NE), (0, 0)))

    value_gates = gates_of(logits[: H * NE], value_routes[0], value_slots[0], CAPV)
    output_gates = gates_of(logits[H * NE :, MEM:], output_routes[0], output_slots[0], CAPO)
    *stored, gated, mixed = mix(
        normed,
        rel_table,
        attention,
        biases[:HD].reshape(H, DH, 1),
        biases[HD : 2 * HD].reshape(H, DH, 1),
        value_gates,
        output_gates,
    )
    gated = gated.reshape(H * EXPERT, SEG)
    residual = embedded + mixed
    normal_mid, spread_mid = normalised(residual)
    normed_mid = (normal_mid * gains[1]).astype(bfloat)
    up, down = (expanding.own, expanding.other), (contracting.own, contracting.other)
    active, slope = expand_forward(normed_mid, up, biases[None, 2 * HD :])
    final = residual + contract_forward(active, down) + gains[3]
    normal_out, spread_out = normalised(final)
    normed_out = (normal_out * gains[2]).astype(bfloat)

    counted = (jnp.arange(SEG, dtype=jnp.int32) < target_counts[0]).astype(single)
    grad_logits, grad_out, losses = head(
        normed_out, goals[:, None], counted[:, None], tables_by_block, shard_rows, shard_half
    )
    loss = jnp.sum(losses)

    grad_final, grad_gain_out = norm_gradient(
        grad_out.astype(single), normal_out, spread_out, gains[2]
    )
    grad_branch = grad_final.astype(bfloat)
    grad_bias_down = jnp.sum(grad_branch.astype(single), axis=0)

    def summing(wide, other, wide_dim, other_dim):
        def part(start):
            side = lax.slice_in_dim(wide, start, start + half, axis=1)
            return lambda ties: dot(after(side, *ties), other, wide_dim, other_dim)

        return Reduce(grid, part(0), part(half))

    def summing_turned(wide, other):
        def part(start):
            side = lax.slice_in_dim(wide, start, start + half, axis=1)
            return lambda ties: dot(other, after(side, *ties), 1, 0)

        return Reduce(grid, part(0), part(half), True, True)

    grid.step()
    contracting = summing(grad_branch, active, 0, 0)
    tie = contracting.pair()
    grad_hidden, grad_bias_up, grad_mid = ff_back(after(grad_branch, tie), slope, down, up)
    expanding = summing(normed_mid, grad_hidden, 0, 0)
    tie = expanding.pair()
    tie_two = contracting.opposite()
    grad_mid = after(grad_mid, tie, *tie_two)
    grad_residual, grad_gain_mid = norm_gradient(
        grad_mid.astype(single), normal_mid, spread_mid, gains[1]
    )
    grad_residual = grad_residual + grad_final
    low_residual = grad_residual.astype(bfloat)
    outputting = summing_turned(low_residual, gated)
    tie = outputting.pair()
    tie_two = expanding.opposite()
    tie_three = contracting.neighbours()
    tie_four = outputting.opposite()
    (
        grad_queries,
        grad_keys,
        grad_rel,
        grad_values,
        grad_value_gates,
        grad_output_gates,
        grad_content,
        grad_position,
        grad_normed,
    ) = mix_back(
        after(low_residual, *tie_two, *tie_three, *tie_four),
        attention,
        stored,
        value_gates,
        output_gates,
    )
    tie = expanding.neighbours()
    grad_values = grad_values.reshape(H * EXPERT, SPAN)
    grad_gates = jnp.concatenate(
        [
            grad_value_gates[:, :NE].reshape(H * NE, SPAN),
            jnp.pad(grad_output_gates[:, :NE].reshape(H * NE, SEG), ((0, 0), (MEM, 0))),
            jnp.zeros((LAST_ROWS - GATES, SPAN), single),
        ],
        axis=0,
    ).astype(bfloat)
    contracting.along_line()
    tie = outputting.neighbours()
    grad_normed = (grad_normed + dot(grad_gates, last_rows, 0, 0)).astype(bfloat)
    grad_normed = after(grad_normed, *expanding.sums)
    expanding.along_line()
    grad_stream, grad_gain_in = norm_gradient(
        grad_normed.astype(single), normal_in, spread_in, gains[0]
    )
    grad_embedded = (grad_residual + grad_stream[MEM:]).astype(bfloat)
    nothing = jnp.zeros((D,), single)
    grad_vectors = jnp.stack(
        [nothing] * GATES
        + [grad_gain_in, grad_gain_mid, grad_gain_out, grad_bias_down]
        + [nothing] * (LAST_ROWS - GATES - 4)
    )

    tokens = jnp.arange(2 * part_rows, dtype=jnp.int32)[None, :]
    looked = (ids[:, None] == tokens).astype(bfloat)
    table_left = jnp.concatenate([grad_logits, looked], axis=0)
    table_right = jnp.concatenate([normed_out, grad_embedded * bfloat(D**0.5)], axis=0)

    def table_summing(start):
        side = table_left[:, start : start + part_rows]

        def part(column):
            right = table_right[:, column : column + half]
            return lambda ties: dot(side, after(right, *ties), 0, 0)

        return Reduce(grid, part(0), part(half), columns=True)

    tables = [table_summing(i) for i in (0, part_rows)]
    valuing = summing_turned(normed, grad_values)

    def small_half(start):
        def compute(ties):
            stop = start + half
            side = after(normed[:, start:stop], *ties)
            return jnp.concatenate(
                [
                    dot(grad_queries.reshape(HD, SPAN), side, 1, 0),
                    dot(grad_keys.reshape(HD, SPAN), side, 1, 0),
                    dot(grad_rel.reshape(HD, SPAN), rel_table[:, start:stop], 1, 0),
                    dot(grad_gates, side, 1, 0) + grad_vectors[:, start:stop],
                ],
                axis=0,
            )

        return compute

    smalling = Reduce(grid, small_half(0), small_half(half), True, True)
    tie = tables[0].pair(contracting.shard)
    tie = tables[1].pair(tie)
    outputting.along_line()
    tie = tables[0].opposite(tie, *outputting.sums, expanding.shard)
    tie = (valuing.pair(*tie),)
    tie = tables[1].opposite(*tie)
    tie = tables[0].neighbours() + tie
    tie = (smalling.pair(*tie, outputting.shard),)
    tie = valuing.opposite(*tie, *tables[1].met)
    tie = tables[1].neighbours() + tie
    tables[0].along_line()
    tie = smalling.opposite(*tie)
    valuing.neighbours()
    tables[1].along_line()
    smalling.neighbours()
    valuing.along_line()
    smalling.along_line()
    sum_contract, sum_expand, sum_outputs, sum_values, sum_small = (
        part.value() for part in (contracting, expanding, outputting, valuing, smalling)
    )
    sum_table = jnp.concatenate([part.value() for part in tables], axis=0)[:shard_rows]

    shard_grads = [
        sum_table,
        jnp.concatenate([sum_small[:, :QUERIES], sum_small[:, 3 * HD : 3 * HD + GATES]], axis=1),
        sum_small[:, QUERIES : 3 * HD],
        sum_values,
        sum_outputs.T,
        sum_expand,
        sum_contract.T,
        sum_small[:, 3 * HD + GATES : 3 * HD + GATES + 4].T,
    ]
    most_tokens = grid.count * SEG
    local_squares = jnp.zeros((), single)
    for grad in shard_grads:
        scaled = grad * (1.0 / most_tokens)
        local_squares = local_squares + jnp.sum(scaled * scaled)
    shared = jnp.concatenate(
        [
            grad_content.reshape(HD),
            grad_position.reshape(HD),
            grad_bias_up.reshape(FF),
            jnp.stack([loss, target_counts[0].astype(single), local_squares]),
        ]
    )
    shared = total_everywhere(grid, shared)
    bias_grad, loss_total, token_count, squares = shared[:-3], shared[-3], shared[-2], shared[-1]
    scaled = bias_grad * (1.0 / most_tokens)
    gradient_norm = jnp.sqrt(squares + jnp.sum(scaled * scaled)) * (most_tokens / token_count)
    factor = jnp.minimum(1.0, clip_norm / (gradient_norm + 1e-06))
    inverse = 1.0 / token_count
    shard_grads = [grad * inverse for grad in shard_grads]
    bias_grad = bias_grad * inverse
    step_rate = rate_base * (PARAMS / D) ** 0.5
    results = (loss_total, token_count, gradient_norm)
    for weight, velocity, average, grad, multiplier in zip(
        masters, moments, averages, shard_grads + [bias_grad], rate_factors
    ):
        results += advance(weight, velocity, average, grad, factor, step_rate * multiplier)
    return results


def solution(mesh):
    batch = P(BOTH)
    rows, columns, whole = P(BOTH, None), P(None, BOTH), P()
    kinds = (P(FSDP, DP), rows, rows, rows, columns, rows, columns, columns, whole)
    triples = tuple(kind for kind in kinds for _ in range(3))
    return jax.shard_map(
        body,
        mesh=mesh,
        in_specs=(batch,) * 8 + triples,
        out_specs=(whole,) * 3 + triples,
        check_vma=False,
    )
```

profile of v0, /device:TPU:0, one launch (start us, length us, event | category | flops | bytes accessed | tf_op | source)
XLA Modules:
  0.0 871.5 jit_solution(4962055427169552547)
XLA Ops:
  8.7 5.1 collective-permute-start
  14.6 8.1 fusion.24
  22.8 3.7 fusion.35.refs_1_
  29.2 6.9 collective-permute-done.1
  41.3 6.0 collective-permute-done.5
  47.2 12.0 %collective-permute-done.6 = bf16[1024,128]{1,0:T(8,128)(2,1)S(1)} collective-permute-done((bf16[1024,128]{1,0:T(8,128)(2,1)S(1)}, bf16[1024,128]{1,0:T(8,128)(2,1)S(1)}, u32[]{:S(2)}, u32[]{:S(2)}) %collective-permute-start.6) | collective-permute-done | bytes 262176 | tf_op jit(solution)/shard_map/ppermute | solution.py:76
  71.7 15.4 %collective-permute-done.4 = bf16[4096,128]{1,0:T(8,128)(2,1)S(1)} collective-permute-done((bf16[4096,128]{1,0:T(8,128)(2,1)S(1)}, bf16[4096,128]{1,0:T(8,128)(2,1)S(1)}, u32[]{:S(2)}, u32[]{:S(2)}) %collective-permute-start.4) | collective-permute-done | bytes 1048608 | tf_op jit(solution)/shard_map/ppermute | solution.py:76
  87.1 5.0 collective-permute-done.3
  108.2 21.0 %collective-permute-done.8 = bf16[6144,128]{1,0:T(8,128)(2,1)S(1)} collective-permute-done((bf16[6144,128]{1,0:T(8,128)(2,1)}, bf16[6144,128]{1,0:T(8,128)(2,1)S(1)}, u32[]{:S(2)}, u32[]{:S(2)}) %collective-permute-start.8) | collective-permute-done | bytes 1572896 | tf_op jit(solution)/shard_map/ppermute | solution.py:76
  146.4 40.3 %collective-permute-done.14 = bf16[2048,128]{1,0:T(8,128)(2,1)S(1)} collective-permute-done((bf16[2048,128]{1,0:T(8,128)(2,1)}, bf16[2048,128]{1,0:T(8,128)(2,1)S(1)}, u32[]{:S(2)}, u32[]{:S(2)}) %collective-permute-start.14) | collective-permute-done | bytes 524320 | tf_op jit(solution)/shard_map/ppermute | solution.py:76
  205.2 8.9 %shard_map.571 = f32[512,1024]{1,0:T(8,128)} custom-call(s32[512,1]{1,0:T(8,128)} %fusion.93.ids_ref, bf16[4,4096,128]{2,1,0:T(8,128)(2,1)} %bitcast.6.own_ref.own_zero, bf16[4,4096,128]{2,1,0:T(8,128)(2,1)} %bitcast.9.other_ref.other_zero), custom_call_target="tpu_custom_call" | custom-call | flops 10000000 | bytes 100000 | tf_op jit(solution)/shard_map/pallas_call | solution.py:596
  217.1 24.0 %collective-permute-done.20 = bf16[2944,128]{1,0:T(8,128)(2,1)S(1)} collective-permute-done((bf16[2944,128]{1,0:T(8,128)(2,1)S(1)}, bf16[2944,128]{1,0:T(8,128)(2,1)S(1)}, u32[]{:S(2)}, u32[]{:S(2)}) %collective-permute-start.20) | collective-permute-done | bytes 753696 | tf_op jit(solution)/shard_map/ppermute | solution.py:76
  250.5 9.0 %shard_map.573 = f32[512,1024]{1,0:T(8,128)} custom-call(s32[512,1]{1,0:T(8,128)} %fusion.93.ids_ref, bf16[4,4096,128]{2,1,0:T(8,128)(2,1)} %bitcast.177, bf16[4,4096,128]{2,1,0:T(8,128)(2,1)} %bitcast.11.other_ref.other_one), custom_call_target="tpu_custom_call" | custom-call | flops 10000000 | bytes 100000 | tf_op jit(solution)/shard_map/pallas_call | solution.py:596
  263.5 21.3 %collective-permute-done.25 = bf16[64,4096]{1,0:T(8,128)(2,1)} collective-permute-done((bf16[64,4096]{1,0:T(8,128)(2,1)}, bf16[64,4096]{1,0:T(8,128)(2,1)}, u32[]{:S(2)}, u32[]{:S(2)}) %collective-permute-start.25) | collective-permute-done | bytes 524320 | tf_op jit(solution)/shard_map/ppermute | solution.py:76
  306.6 10.8 %collective-permute-done.29 = bf16[64,4096]{1,0:T(8,128)(2,1)S(1)} collective-permute-done((bf16[64,4096]{1,0:T(8,128)(2,1)S(1)}, bf16[64,4096]{1,0:T(8,128)(2,1)S(1)}, u32[]{:S(2)}, u32[]{:S(2)}) %collective-permute-start.29) | collective-permute-done | bytes 524320 | tf_op jit(solution)/shard_map/ppermute | solution.py:76
  329.7 29.6 %shard_map.574 = (bf16[4,112,512]{2,1,0:T(8,128)(2,1)}, bf16[4,112,512]{2,1,0:T(8,128)(2,1)}, bf16[4,112,1024]{2,1,0:T(8,128)(2,1)}, bf16[4,112,1024]{2,1,0:T(8,...) custom-call(bf16[1024,1024]{1,0:T(8,128)(2,1)} %copy-done.4, ...), custom_call_target="tpu_custom_call" | custom-call | flops 10000000 | bytes 100000 | tf_op jit(solution)/shard_map/pallas_call | solution.py:440
  362.9 13.2 %shard_map.575 = (bf16[512,4096]{1,0:T(8,128)(2,1)}, bf16[512,4096]{1,0:T(8,128)(2,1)}) custom-call(bf16[512,1024]{1,0:T(8,128)(2,1)} %multiply_convert_fusion.2.in_ref, bf16[512,4096]{1,0:T(8,128)(2,1)} %constant_dynamic-update-slice_fusion.30.own_ref.own_up, bf16[512,4096]{1,0:T(8,128)(2,1)} %collective-permute-done.28.other_ref.other_up, f32[1,4096]{1,0:T(1,128)} %bitcast.186), custom_call_target="tpu_custom_call" | custom-call | flops 10000000 | bytes 100000 | tf_op jit(solution)/shard_map/pallas_call | solution.py:504
  376.0 11.0 %shard_map.576 = f32[512,1024]{1,0:T(8,128)} custom-call(bf16[512,4096]{1,0:T(8,128)(2,1)} %get-tuple-element.152.act_ref, bf16[512,4096]{1,0:T(8,128)(2,1)} %constant_dynamic-update-slice_fusion.35.own_ref.own_down, bf16[512,4096]{1,0:T(8,128)(2,1)} %collective-permute-done.31.other_ref.other_down), custom_call_target="tpu_custom_call" | custom-call | flops 10000000 | bytes 100000 | tf_op jit(solution)/shard_map/pallas_call | solution.py:525
  390.6 42.8 %shard_map.577 = (bf16[512,8192]{1,0:T(8,128)(2,1)}, bf16[512,1024]{1,0:T(8,128)(2,1)}, f32[512,1]{1,0:T(8,128)}) custom-call(bf16[512,1024]{1,0:T(8,128)(2,1)} %multiply_convert_fusion.1.hf_ref, s32[512,1]{1,0:T(8,128)} %fusion.97.goal_ref, f32[512,1]{1,0:T(8,128)} %fusion.107.counted_ref, bf16[4,4096,128]{2,1,0:T(8,128)(2,1)} %bitcast.6.own_ref.own_zero, ...), custom_call_target="tpu_custom_call" | custom-call | flops 10000000 | bytes 100000 | tf_op jit(solution)/shard_map/pallas_call | solution.py:706
  438.2 4.3 convolution_convert_fusion.3
  443.1 16.4 %shard_map.578 = (bf16[512,4096]{1,0:T(8,128)(2,1)}, f32[1,4096]{1,0:T(1,128)}, bf16[512,1024]{1,0:T(8,128)(2,1)}) custom-call(bf16[512,1024]{1,0:T(8,128)(2,1)} %copy-done.14, bf16[512,4096]{1,0:T(8,128)(2,1)} %get-tuple-element.158.slope_ref, bf16[512,4096]{1,0:T(8,128)(2,1)} %constant_dynamic-update-slice_fusion.35.own_ref.own_down, ...), custom_call_target="tpu_custom_call" | custom-call | flops 10000000 | bytes 100000 | tf_op jit(solution)/shard_map/pallas_call | solution.py:560
  459.6 4.7 convolution_convert_fusion.2
  464.5 4.8 add_convert_fusion.3
  483.9 5.2 collective-permute-done.37
  493.0 7.3 collective-permute-done.34
  503.4 6.5 fusion
  509.9 35.8 %collective-permute-done.41 = bf16[128,4096]{1,0:T(8,128)(2,1)S(1)} collective-permute-done((bf16[128,4096]{1,0:T(8,128)(2,1)S(1)}, bf16[128,4096]{1,0:T(8,128)(2,1)S(1)}, u32[]{:S(2)}, u32[]{:S(2)}) %collective-permute-start.41) | collective-permute-done | bytes 1048608 | tf_op jit(solution)/shard_map/ppermute | solution.py:76
  547.3 3.4 add_convert_fusion.11
  550.7 3.9 fusion.3
  557.9 33.5 %shard_map.579 = (bf16[4,112,1024]{2,1,0:T(8,128)(2,1)}, bf16[4,112,1024]{2,1,0:T(8,128)(2,1)}, bf16[4,112,1024]{2,1,0:T(8,128)(2,1)}, bf16[4,560,1024]{2,1,0:T(...) custom-call(bf16[512,1024]{1,0:T(8,128)(2,1)} %copy-done.10, ...), custom_call_target="tpu_custom_call" | custom-call | flops 10000000 | bytes 100000 | tf_op jit(solution)/shard_map/pallas_call | solution.py:470
  601.5 8.9 %convolution_convert_fusion.1 = bf16[4096,512]{1,0:T(8,128)(2,1)} fusion(bf16[1024,512]{1,0:T(8,128)(2,1)S(1)} %get-tuple-element.193, bf16[512,8192]{1,0:T(8,128)(2,1)} %get-tuple-element.181, bf16[512,8192]{1,0:T(8,128)(2,1)} %fusion), kind=kOutput, calls=%fused_computation.11 | convolution fusion | flops 4313841664 | bytes 22020096 | tf_op jit(solution)/shard_map/dot_general | solution.py:51
  614.7 12.4 %collective-permute-done.46 = bf16[2240,128]{1,0:T(8,128)(2,1)S(1)} collective-permute-done((bf16[2240,128]{1,0:T(8,128)(2,1)S(1)}, bf16[2240,128]{1,0:T(8,128)(2,1)S(1)}, u32[]{:S(2)}, u32[]{:S(2)}) %collective-permute-start.46) | collective-permute-done | bytes 573472 | tf_op jit(solution)/shard_map/ppermute | solution.py:76
  630.5 10.4 %convolution_convert_fusion = bf16[4096,512]{1,0:T(8,128)(2,1)} fusion(bf16[1024,512]{1,0:T(8,128)(2,1)} %copy-done.54, bf16[512,8192]{1,0:T(8,128)(2,1)} %fusion, bf16[512,8192]{1,0:T(8,128)(2,1)} %get-tuple-element.181), kind=kOutput, calls=%fused_computation.10 | convolution fusion | flops 4313841664 | bytes 22020096 | tf_op jit(solution)/shard_map/dot_general | solution.py:51
  652.7 7.9 add_convert_fusion.1
  663.8 6.2 convolution_convert_fusion.4
  670.0 9.2 %add_convert_fusion = bf16[4096,512]{1,0:T(8,128)(2,1)S(1)} fusion(bf16[4096,512]{1,0:T(8,128)(2,1)} %collective-permute-done.52, bf16[1024,512]{1,0:T(8,128)(2,1)S(1)} %copy-done.52, bf16[512,8192]{1,0:T(8,128)(2,1)} %fusion, bf16[512,8192]{1,0:T(8,128)(2,1)} %get-tuple-element.181), kind=kOutput, calls=%fused_computation.6 | convolution fusion | flops 4318035968 | bytes 26214400 | tf_op jit(solution)/shard_map/dot_general | solution.py:51
  684.0 10.3 %collective-permute-done.55 = bf16[2048,128]{1,0:T(8,128)(2,1)S(1)} collective-permute-done((bf16[2048,128]{1,0:T(8,128)(2,1)S(1)}, bf16[2048,128]{1,0:T(8,128)(2,1)S(1)}, u32[]{:S(2)}, u32[]{:S(2)}) %collective-permute-start.55) | collective-permute-done | bytes 524320 | tf_op jit(solution)/shard_map/ppermute | solution.py:76
  700.5 16.3 %collective-permute-done.49 = bf16[4096,128]{1,0:T(8,128)(2,1)S(1)} collective-permute-done((bf16[4096,128]{1,0:T(8,128)(2,1)S(1)}, bf16[4096,128]{1,0:T(8,128)(2,1)S(1)}, u32[]{:S(2)}, u32[]{:S(2)}) %collective-permute-start.49) | collective-permute-done | bytes 1048608 | tf_op jit(solution)/shard_map/ppermute | solution.py:76
  719.1 17.4 %collective-permute-done.54 = bf16[4096,128]{1,0:T(8,128)(2,1)} collective-permute-done((bf16[4096,128]{1,0:T(8,128)(2,1)}, bf16[4096,128]{1,0:T(8,128)(2,1)}, u32[]{:S(2)}, u32[]{:S(2)}) %collective-permute-start.54) | collective-permute-done | bytes 1048608 | tf_op jit(solution)/shard_map/ppermute | solution.py:76
  740.0 5.7 fusion.2
  755.1 3.4 collective-permute-done.61
  761.4 3.4 collective-permute-done.65
  768.3 4.2 collective-permute-done.60
  775.1 5.6 collective-permute-done.64
  788.8 10.2 %reduce-scatter.26.cloned.1.call-done = bf16[32,1408]{1,0:T(8,128)(2,1)} async-done(((bf16[128,1408]{1,0:T(8,128)(2,1)}), bf16[32,1408]{1,0:T(8,128)(2,1)}) %reduce-scatter.26.cloned.1.call-update) | async-done | bytes 90128 | tf_op jit(solution)/shard_map/reduce_scatter | solution.py:272
  806.3 15.9 %reduce-scatter.24.cloned.1.call-done = bf16[32,2240]{1,0:T(8,128)(2,1)} async-done(((bf16[128,2240]{1,0:T(8,128)(2,1)}), bf16[32,2240]{1,0:T(8,128)(2,1)}) %reduce-scatter.24.cloned.1.call-update) | async-done | bytes 143376 | tf_op jit(solution)/shard_map/reduce_scatter | solution.py:272
  836.5 3.8 collective-permute-done.70
  841.5 3.5 collective-permute-done.71
  (601 shorter events, 271.1 us)
Async XLA Ops:
  7.2 190.7 %all-gather.2.cloned.1.call-start = ((), (), s32[]{:S(2)}) async-start(), calls=%async_computation.7 | async-start | bytes 2621440 | tf_op jit(solution)/shard_map/all_gather | solution.py:813
  13.8 22.3 %collective-permute-start.1 = (bf16[1024,128]{1,0:T(8,128)(2,1)S(1)}, bf16[1024,128]{1,0:T(8,128)(2,1)S(1)}, u32[]{:S(2)}, u32[]{:S(2)}) collective-permute-start(bf16[1024,128]{1,0:T(8,128)(2,1)S(1)} %get-tuple-element.496), channel_id=1, source_target_pairs={{0,2},{1,3},{2,0},{3,1},{4,6},{5,7},{6,4},{7,5},{8,10},{9,11},{10,... | collective-permute-start | bytes 786440 | tf_op jit(solution)/shard_map/ppermute | solution.py:76
  13.8 22.3 %collective-permute-start.2 = (bf16[1024,128]{1,0:T(8,128)(2,1)S(1)}, bf16[1024,128]{1,0:T(8,128)(2,1)S(1)}, u32[]{:S(2)}, u32[]{:S(2)}) collective-permute-start(bf16[1024,128]{1,0:T(8,128)(2,1)S(1)} %get-tuple-element.496), channel_id=1, source_target_pairs={{0,1},{1,0},{2,3},{3,2},{4,5},{5,4},{6,7},{7,6},{8,9},{9,8},{10,11... | collective-permute-start | bytes 786440 | tf_op jit(solution)/shard_map/ppermute | solution.py:76
  64.1 23.0 %collective-permute-start.4 = (bf16[4096,128]{1,0:T(8,128)(2,1)S(1)}, bf16[4096,128]{1,0:T(8,128)(2,1)S(1)}, u32[]{:S(2)}, u32[]{:S(2)}) collective-permute-start(bf16[4096,128]{1,0:T(8,128)(2,1)S(1)} %pad_maximum_fusion.9), channel_id=1, source_target_pairs={{0,16},{1,17},{2,18},{3,19},{4,20},{5,21},{6,22},{7,23},{8,24},{9,... | collective-permute-start | bytes 3145736 | tf_op jit(solution)/shard_map/ppermute | solution.py:76
  69.5 22.6 %collective-permute-start.3 = (bf16[4096,128]{1,0:T(8,128)(2,1)S(1)}, bf16[4096,128]{1,0:T(8,128)(2,1)S(1)}, u32[]{:S(2)}, u32[]{:S(2)}) collective-permute-start(bf16[4096,128]{1,0:T(8,128)(2,1)S(1)} %pad_maximum_fusion.9), channel_id=1, source_target_pairs={{0,8},{1,9},{2,10},{3,11},{4,12},{5,13},{6,14},{7,15},{8,0},{9,1},... | collective-permute-start | bytes 3145736 | tf_op jit(solution)/shard_map/ppermute | solution.py:76
  96.1 33.1 %collective-permute-start.8 = (bf16[6144,128]{1,0:T(8,128)(2,1)}, bf16[6144,128]{1,0:T(8,128)(2,1)S(1)}, u32[]{:S(2)}, u32[]{:S(2)}) collective-permute-start(bf16[6144,128]{1,0:T(8,128)(2,1)} %get-tuple-element.134), channel_id=1, source_target_pairs={{0,16},{1,17},{2,18},{3,19},{4,20},{5,21},{6,22},{7,23},{8,24},{9,... | collective-permute-start | bytes 4718600 | tf_op jit(solution)/shard_map/ppermute | solution.py:76
  99.1 33.1 %collective-permute-start.9 = (bf16[6144,128]{1,0:T(8,128)(2,1)}, bf16[6144,128]{1,0:T(8,128)(2,1)S(1)}, u32[]{:S(2)}, u32[]{:S(2)}) collective-permute-start(bf16[6144,128]{1,0:T(8,128)(2,1)} %copy-done.81), channel_id=1, source_target_pairs={{0,8},{1,9},{2,10},{3,11},{4,12},{5,13},{6,14},{7,15},{8,0},{9,1},... | collective-permute-start | bytes 4718600 | tf_op jit(solution)/shard_map/ppermute | solution.py:76
  101.7 32.7 %collective-permute-start.10 = (bf16[32,5888]{1,0:T(8,128)(2,1)S(1)}, bf16[32,5888]{1,0:T(8,128)(2,1)S(1)}, u32[]{:S(2)}, u32[]{:S(2)}) collective-permute-start(bf16[32,5888]{1,0:T(8,128)(2,1)S(1)} %concatenate.79), channel_id=1, source_target_pairs={{0,1},{1,0},{2,3},{3,2},{4,5},{5,4},{6,7},{7,6},{8,9},{9,8},{10,11... | collective-permute-start | bytes 1130504 | tf_op jit(solution)/shard_map/ppermute | solution.py:76
  101.7 32.7 %collective-permute-start.11 = (bf16[32,5888]{1,0:T(8,128)(2,1)S(1)}, bf16[32,5888]{1,0:T(8,128)(2,1)S(1)}, u32[]{:S(2)}, u32[]{:S(2)}) collective-permute-start(bf16[32,5888]{1,0:T(8,128)(2,1)S(1)} %concatenate.79), channel_id=1, source_target_pairs={{0,2},{1,3},{2,0},{3,1},{4,6},{5,7},{6,4},{7,5},{8,10},{9,11},{10,... | collective-permute-start | bytes 1130504 | tf_op jit(solution)/shard_map/ppermute | solution.py:76
  104.8 29.7 %collective-permute-start.12 = (bf16[32,5888]{1,0:T(8,128)(2,1)S(1)}, bf16[32,5888]{1,0:T(8,128)(2,1)S(1)}, u32[]{:S(2)}, u32[]{:S(2)}) collective-permute-start(bf16[32,5888]{1,0:T(8,128)(2,1)S(1)} %concatenate.79), channel_id=1, source_target_pairs={{0,3},{1,2},{2,1},{3,0},{4,7},{5,6},{6,5},{7,4},{8,11},{9,10},{10,... | collective-permute-start | bytes 1130504 | tf_op jit(solution)/shard_map/ppermute | solution.py:76
  134.5 54.0 %collective-permute-start.13 = (bf16[16384,128]{1,0:T(8,128)(2,1)}, bf16[16384,128]{1,0:T(8,128)(2,1)}, u32[]{:S(2)}, u32[]{:S(2)}) collective-permute-start(bf16[16384,128]{1,0:T(8,128)(2,1)} %get-tuple-element.137), channel_id=1, source_target_pairs={{0,4},{1,5},{2,6},{3,7},{4,0},{5,1},{6,2},{7,3},{8,12},{9,13},{10,... | collective-permute-start | bytes 12582920 | tf_op jit(solution)/shard_map/ppermute | solution.py:76
  138.7 49.8 %collective-permute-start.16 = (bf16[5888,128]{1,0:T(8,128)(2,1)}, bf16[5888,128]{1,0:T(8,128)(2,1)}, u32[]{:S(2)}, u32[]{:S(2)}) collective-permute-start(bf16[5888,128]{1,0:T(8,128)(2,1)} %shard_map.572), channel_id=1, source_target_pairs={{0,8},{1,9},{2,10},{3,11},{4,12},{5,13},{6,14},{7,15},{8,0},{9,1},... | collective-permute-start | bytes 4521992 | tf_op jit(solution)/shard_map/ppermute | solution.py:76
  140.2 48.3 %collective-permute-start.17 = (bf16[5888,128]{1,0:T(8,128)(2,1)}, bf16[5888,128]{1,0:T(8,128)(2,1)}, u32[]{:S(2)}, u32[]{:S(2)}) collective-permute-start(bf16[5888,128]{1,0:T(8,128)(2,1)} %shard_map.572), channel_id=1, source_target_pairs={{0,16},{1,17},{2,18},{3,19},{4,20},{5,21},{6,22},{7,23},{8,24},{9,... | collective-permute-start | bytes 4521992 | tf_op jit(solution)/shard_map/ppermute | solution.py:76
  141.5 45.2 %collective-permute-start.14 = (bf16[2048,128]{1,0:T(8,128)(2,1)}, bf16[2048,128]{1,0:T(8,128)(2,1)S(1)}, u32[]{:S(2)}, u32[]{:S(2)}) collective-permute-start(bf16[2048,128]{1,0:T(8,128)(2,1)} %get-tuple-element.138), channel_id=1, source_target_pairs={{0,16},{1,17},{2,18},{3,19},{4,20},{5,21},{6,22},{7,23},{8,24},{9,... | collective-permute-start | bytes 1572872 | tf_op jit(solution)/shard_map/ppermute | solution.py:76
  142.2 45.4 %collective-permute-start.15 = (bf16[2048,128]{1,0:T(8,128)(2,1)}, bf16[2048,128]{1,0:T(8,128)(2,1)S(1)}, u32[]{:S(2)}, u32[]{:S(2)}) collective-permute-start(bf16[2048,128]{1,0:T(8,128)(2,1)} %get-tuple-element.139), channel_id=1, source_target_pairs={{0,8},{1,9},{2,10},{3,11},{4,12},{5,13},{6,14},{7,15},{8,0},{9,1},... | collective-permute-start | bytes 1572872 | tf_op jit(solution)/shard_map/ppermute | solution.py:76
  142.8 458.6 %reduce-scatter.14.cloned.1.call-start = ((), (), s32[]{:S(2)}) async-start(), calls=%async_computation.8 | async-start | bytes 1310720 | tf_op jit(solution)/shard_map/reduce_scatter | solution.py:272
  188.5 53.6 %collective-permute-start.18 = (bf16[16384,128]{1,0:T(8,128)(2,1)}, bf16[16384,128]{1,0:T(8,128)(2,1)}, u32[]{:S(2)}, u32[]{:S(2)}) collective-permute-start(bf16[16384,128]{1,0:T(8,128)(2,1)} %constant_dynamic-update-slice_fusion.11), channel_id=1, source_target_pairs={{0,4},{1,5},{2,6},{3,7},{4,0},{5,1},{6,2},{7,3},{8,12},{9,13},{10,... | collective-permute-start | bytes 12582920 | tf_op jit(solution)/shard_map/ppermute | solution.py:76
  199.7 42.4 %collective-permute-start.21 = (bf16[128,4096]{1,0:T(8,128)(2,1)S(1)}, bf16[128,4096]{1,0:T(8,128)(2,1)S(1)}, u32[]{:S(2)}, u32[]{:S(2)}) collective-permute-start(bf16[128,4096]{1,0:T(8,128)(2,1)S(1)} %get-tuple-element.145), channel_id=1, source_target_pairs={{0,8},{1,9},{2,10},{3,11},{4,12},{5,13},{6,14},{7,15},{8,0},{9,1},... | collective-permute-start | bytes 3145736 | tf_op jit(solution)/shard_map/ppermute | solution.py:76
  200.3 41.8 %collective-permute-start.22 = (bf16[128,4096]{1,0:T(8,128)(2,1)S(1)}, bf16[128,4096]{1,0:T(8,128)(2,1)S(1)}, u32[]{:S(2)}, u32[]{:S(2)}) collective-permute-start(bf16[128,4096]{1,0:T(8,128)(2,1)S(1)} %get-tuple-element.145), channel_id=1, source_target_pairs={{0,16},{1,17},{2,18},{3,19},{4,20},{5,21},{6,22},{7,23},{8,24},{9,... | collective-permute-start | bytes 3145736 | tf_op jit(solution)/shard_map/ppermute | solution.py:76
  201.0 40.2 %collective-permute-start.20 = (bf16[2944,128]{1,0:T(8,128)(2,1)S(1)}, bf16[2944,128]{1,0:T(8,128)(2,1)S(1)}, u32[]{:S(2)}, u32[]{:S(2)}) collective-permute-start(bf16[2944,128]{1,0:T(8,128)(2,1)S(1)} %slice.460), channel_id=1, source_target_pairs={{0,8},{1,9},{2,10},{3,11},{4,12},{5,13},{6,14},{7,15},{8,0},{9,1},... | collective-permute-start | bytes 2261000 | tf_op jit(solution)/shard_map/ppermute | solution.py:76
  242.1 45.6 %collective-permute-start.23 = (bf16[23552,128]{1,0:T(8,128)(2,1)}, bf16[23552,128]{1,0:T(8,128)(2,1)}, u32[]{:S(2)}, u32[]{:S(2)}) collective-permute-start(bf16[23552,128]{1,0:T(8,128)(2,1)} %constant_dynamic-update-slice_fusion.17), channel_id=1, source_target_pairs={{0,4},{1,5},{2,6},{3,7},{4,0},{5,1},{6,2},{7,3},{8,12},{9,13},{10,... | collective-permute-start | bytes 18087944 | tf_op jit(solution)/shard_map/ppermute | solution.py:76
  247.1 39.5 %collective-permute-start.27 = (bf16[128,4096]{1,0:T(8,128)(2,1)S(1)}, bf16[128,4096]{1,0:T(8,128)(2,1)S(1)}, u32[]{:S(2)}, u32[]{:S(2)}) collective-permute-start(bf16[128,4096]{1,0:T(8,128)(2,1)S(1)} %get-tuple-element.150), channel_id=1, source_target_pairs={{0,16},{1,17},{2,18},{3,19},{4,20},{5,21},{6,22},{7,23},{8,24},{9,... | collective-permute-start | bytes 3145736 | tf_op jit(solution)/shard_map/ppermute | solution.py:76
  248.4 38.2 %collective-permute-start.26 = (bf16[128,4096]{1,0:T(8,128)(2,1)S(1)}, bf16[128,4096]{1,0:T(8,128)(2,1)S(1)}, u32[]{:S(2)}, u32[]{:S(2)}) collective-permute-start(bf16[128,4096]{1,0:T(8,128)(2,1)S(1)} %get-tuple-element.150), channel_id=1, source_target_pairs={{0,8},{1,9},{2,10},{3,11},{4,12},{5,13},{6,14},{7,15},{8,0},{9,1},... | collective-permute-start | bytes 3145736 | tf_op jit(solution)/shard_map/ppermute | solution.py:76
  249.0 35.8 %collective-permute-start.25 = (bf16[64,4096]{1,0:T(8,128)(2,1)}, bf16[64,4096]{1,0:T(8,128)(2,1)}, u32[]{:S(2)}, u32[]{:S(2)}) collective-permute-start(bf16[64,4096]{1,0:T(8,128)(2,1)} %slice.477), channel_id=1, source_target_pairs={{0,8},{1,9},{2,10},{3,11},{4,12},{5,13},{6,14},{7,15},{8,0},{9,1},... | collective-permute-start | bytes 1572872 | tf_op jit(solution)/shard_map/ppermute | solution.py:76
  288.6 31.2 %collective-permute-start.28 = (bf16[512,4096]{1,0:T(8,128)(2,1)}, bf16[512,4096]{1,0:T(8,128)(2,1)}, u32[]{:S(2)}, u32[]{:S(2)}) collective-permute-start(bf16[512,4096]{1,0:T(8,128)(2,1)} %constant_dynamic-update-slice_fusion.30.own_ref.own_up), channel_id=1, source_target_pairs={{0,4},{1,5},{2,6},{3,7},{4,0},{5,1},{6,2},{7,3},{8,12},{9,13},{10,... | collective-permute-start | bytes 12582920 | tf_op jit(solution)/shard_map/ppermute | solution.py:76
  319.8 56.2 %collective-permute-start.31 = (bf16[512,4096]{1,0:T(8,128)(2,1)}, bf16[512,4096]{1,0:T(8,128)(2,1)}, u32[]{:S(2)}, u32[]{:S(2)}) collective-permute-start(bf16[512,4096]{1,0:T(8,128)(2,1)} %constant_dynamic-update-slice_fusion.35.own_ref.own_down), channel_id=1, source_target_pairs={{0,4},{1,5},{2,6},{3,7},{4,0},{5,1},{6,2},{7,3},{8,12},{9,13},{10,... | collective-permute-start | bytes 12582920 | tf_op jit(solution)/shard_map/ppermute | solution.py:76
  442.5 21.9 %collective-permute-start.32 = (bf16[512,4096]{1,0:T(8,128)(2,1)}, bf16[512,4096]{1,0:T(8,128)(2,1)}, u32[]{:S(2)}, u32[]{:S(2)}) collective-permute-start(bf16[512,4096]{1,0:T(8,128)(2,1)} %convolution_convert_fusion.3), channel_id=1, source_target_pairs={{0,4},{1,5},{2,6},{3,7},{4,0},{5,1},{6,2},{7,3},{8,12},{9,13},{10,... | collective-permute-start | bytes 12582920 | tf_op jit(solution)/shard_map/ppermute | solution.py:76
  481.7 69.0 %collective-permute-start.36 = (bf16[2240,512]{1,0:T(8,128)(2,1)}, bf16[2240,512]{1,0:T(8,128)(2,1)}, u32[]{:S(2)}, u32[]{:S(2)}) collective-permute-start(bf16[2240,512]{1,0:T(8,128)(2,1)} %convolution_convert_fusion.5), channel_id=1, source_target_pairs={{0,4},{1,5},{2,6},{3,7},{4,0},{5,1},{6,2},{7,3},{8,12},{9,13},{10,... | collective-permute-start | bytes 6881288 | tf_op jit(solution)/shard_map/ppermute | solution.py:76
  491.7 55.5 %collective-permute-start.40 = (bf16[128,4096]{1,0:T(8,128)(2,1)}, bf16[128,4096]{1,0:T(8,128)(2,1)}, u32[]{:S(2)}, u32[]{:S(2)}) collective-permute-start(bf16[128,4096]{1,0:T(8,128)(2,1)} %get-tuple-element.188), channel_id=1, source_target_pairs={{0,16},{1,17},{2,18},{3,19},{4,20},{5,21},{6,22},{7,23},{8,24},{9,... | collective-permute-start | bytes 3145736 | tf_op jit(solution)/shard_map/ppermute | solution.py:76
  492.5 54.8 %collective-permute-start.38 = (bf16[128,4096]{1,0:T(8,128)(2,1)S(1)}, bf16[128,4096]{1,0:T(8,128)(2,1)}, u32[]{:S(2)}, u32[]{:S(2)}) collective-permute-start(bf16[128,4096]{1,0:T(8,128)(2,1)S(1)} %get-tuple-element.186), channel_id=1, source_target_pairs={{0,8},{1,9},{2,10},{3,11},{4,12},{5,13},{6,14},{7,15},{8,0},{9,1},... | collective-permute-start | bytes 3145736 | tf_op jit(solution)/shard_map/ppermute | solution.py:76
  502.0 43.7 %collective-permute-start.41 = (bf16[128,4096]{1,0:T(8,128)(2,1)S(1)}, bf16[128,4096]{1,0:T(8,128)(2,1)S(1)}, u32[]{:S(2)}, u32[]{:S(2)}) collective-permute-start(bf16[128,4096]{1,0:T(8,128)(2,1)S(1)} %get-tuple-element.190), channel_id=1, source_target_pairs={{0,8},{1,9},{2,10},{3,11},{4,12},{5,13},{6,14},{7,15},{8,0},{9,1},... | collective-permute-start | bytes 3145736 | tf_op jit(solution)/shard_map/ppermute | solution.py:76
  502.6 43.1 %collective-permute-start.42 = (bf16[128,4096]{1,0:T(8,128)(2,1)S(1)}, bf16[128,4096]{1,0:T(8,128)(2,1)S(1)}, u32[]{:S(2)}, u32[]{:S(2)}) collective-permute-start(bf16[128,4096]{1,0:T(8,128)(2,1)S(1)} %get-tuple-element.191), channel_id=1, source_target_pairs={{0,16},{1,17},{2,18},{3,19},{4,20},{5,21},{6,22},{7,23},{8,24},{9,... | collective-permute-start | bytes 3145736 | tf_op jit(solution)/shard_map/ppermute | solution.py:76
  547.2 82.2 %reduce-scatter.16.cloned.1.call-start = ((), (), s32[]{:S(2)}) async-start(), calls=%async_computation.9 | async-start | bytes 1310720 | tf_op jit(solution)/shard_map/reduce_scatter | solution.py:272
  556.8 53.5 %collective-permute-start.43 = (bf16[1120,128]{1,0:T(8,128)(2,1)}, bf16[1120,128]{1,0:T(8,128)(2,1)}, u32[]{:S(2)}, u32[]{:S(2)}) collective-permute-start(bf16[1120,128]{1,0:T(8,128)(2,1)} %get-tuple-element.194), channel_id=1, source_target_pairs={{0,16},{1,17},{2,18},{3,19},{4,20},{5,21},{6,22},{7,23},{8,24},{9,... | collective-permute-start | bytes 860168 | tf_op jit(solution)/shard_map/ppermute | solution.py:76
  557.4 53.0 %collective-permute-start.45 = (bf16[1120,128]{1,0:T(8,128)(2,1)}, bf16[1120,128]{1,0:T(8,128)(2,1)}, u32[]{:S(2)}, u32[]{:S(2)}) collective-permute-start(bf16[1120,128]{1,0:T(8,128)(2,1)} %get-tuple-element.196), channel_id=1, source_target_pairs={{0,8},{1,9},{2,10},{3,11},{4,12},{5,13},{6,14},{7,15},{8,0},{9,1},... | collective-permute-start | bytes 860168 | tf_op jit(solution)/shard_map/ppermute | solution.py:76
  601.4 51.3 %reduce-scatter.22.cloned.1.call-start = ((), (), s32[]{:S(2)}) async-start(), calls=%async_computation.12 | async-start | bytes 737280 | tf_op jit(solution)/shard_map/reduce_scatter | solution.py:272
  610.4 42.4 %collective-permute-start.47 = (bf16[4096,512]{1,0:T(8,128)(2,1)}, bf16[4096,512]{1,0:T(8,128)(2,1)}, u32[]{:S(2)}, u32[]{:S(2)}) collective-permute-start(bf16[4096,512]{1,0:T(8,128)(2,1)} %convolution_convert_fusion.1), channel_id=1, source_target_pairs={{0,4},{1,5},{2,6},{3,7},{4,0},{5,1},{6,2},{7,3},{8,12},{9,13},{10,... | collective-permute-start | bytes 12582920 | tf_op jit(solution)/shard_map/ppermute | solution.py:76
  630.5 120.4 %reduce-scatter.18.cloned.1.call-start = ((), (), s32[]{:S(2)}) async-start(), calls=%async_computation.10 | async-start | bytes 1310720 | tf_op jit(solution)/shard_map/reduce_scatter | solution.py:272
  640.9 29.1 %collective-permute-start.52 = (bf16[4096,512]{1,0:T(8,128)(2,1)}, bf16[4096,512]{1,0:T(8,128)(2,1)}, u32[]{:S(2)}, u32[]{:S(2)}) collective-permute-start(bf16[4096,512]{1,0:T(8,128)(2,1)} %convolution_convert_fusion), channel_id=1, source_target_pairs={{0,4},{1,5},{2,6},{3,7},{4,0},{5,1},{6,2},{7,3},{8,12},{9,13},{10,... | collective-permute-start | bytes 12582920 | tf_op jit(solution)/shard_map/ppermute | solution.py:76
  680.6 59.4 %collective-permute-start.57 = (bf16[2240,512]{1,0:T(8,128)(2,1)}, bf16[2240,512]{1,0:T(8,128)(2,1)}, u32[]{:S(2)}, u32[]{:S(2)}) collective-permute-start(bf16[2240,512]{1,0:T(8,128)(2,1)} %convolution_convert_fusion.4), channel_id=1, source_target_pairs={{0,4},{1,5},{2,6},{3,7},{4,0},{5,1},{6,2},{7,3},{8,12},{9,13},{10,... | collective-permute-start | bytes 6881288 | tf_op jit(solution)/shard_map/ppermute | solution.py:76
  681.0 35.8 %collective-permute-start.49 = (bf16[4096,128]{1,0:T(8,128)(2,1)S(1)}, bf16[4096,128]{1,0:T(8,128)(2,1)S(1)}, u32[]{:S(2)}, u32[]{:S(2)}) collective-permute-start(bf16[4096,128]{1,0:T(8,128)(2,1)S(1)} %get-tuple-element.202), channel_id=1, source_target_pairs={{0,8},{1,9},{2,10},{3,11},{4,12},{5,13},{6,14},{7,15},{8,0},{9,1},... | collective-permute-start | bytes 3145736 | tf_op jit(solution)/shard_map/ppermute | solution.py:76
  682.5 34.8 %collective-permute-start.51 = (bf16[4096,128]{1,0:T(8,128)(2,1)S(1)}, bf16[4096,128]{1,0:T(8,128)(2,1)S(1)}, u32[]{:S(2)}, u32[]{:S(2)}) collective-permute-start(bf16[4096,128]{1,0:T(8,128)(2,1)S(1)} %get-tuple-element.204), channel_id=1, source_target_pairs={{0,16},{1,17},{2,18},{3,19},{4,20},{5,21},{6,22},{7,23},{8,24},{9,... | collective-permute-start | bytes 3145736 | tf_op jit(solution)/shard_map/ppermute | solution.py:76
  698.3 38.1 %collective-permute-start.54 = (bf16[4096,128]{1,0:T(8,128)(2,1)}, bf16[4096,128]{1,0:T(8,128)(2,1)}, u32[]{:S(2)}, u32[]{:S(2)}) collective-permute-start(bf16[4096,128]{1,0:T(8,128)(2,1)} %get-tuple-element.212), channel_id=1, source_target_pairs={{0,8},{1,9},{2,10},{3,11},{4,12},{5,13},{6,14},{7,15},{8,0},{9,1},... | collective-permute-start | bytes 3145736 | tf_op jit(solution)/shard_map/ppermute | solution.py:76
  699.9 36.8 %collective-permute-start.56 = (bf16[4096,128]{1,0:T(8,128)(2,1)S(1)}, bf16[4096,128]{1,0:T(8,128)(2,1)}, u32[]{:S(2)}, u32[]{:S(2)}) collective-permute-start(bf16[4096,128]{1,0:T(8,128)(2,1)S(1)} %get-tuple-element.214), channel_id=1, source_target_pairs={{0,16},{1,17},{2,18},{3,19},{4,20},{5,21},{6,22},{7,23},{8,24},{9,... | collective-permute-start | bytes 3145736 | tf_op jit(solution)/shard_map/ppermute | solution.py:76
  716.8 32.0 %collective-permute-start.58 = (bf16[1408,512]{1,0:T(8,128)(2,1)S(1)}, bf16[1408,512]{1,0:T(8,128)(2,1)}, u32[]{:S(2)}, u32[]{:S(2)}) collective-permute-start(bf16[1408,512]{1,0:T(8,128)(2,1)S(1)} %pad_maximum_fusion.3), channel_id=1, source_target_pairs={{0,4},{1,5},{2,6},{3,7},{4,0},{5,1},{6,2},{7,3},{8,12},{9,13},{10,... | collective-permute-start | bytes 4325384 | tf_op jit(solution)/shard_map/ppermute | solution.py:76
  718.8 64.7 %reduce-scatter.20.cloned.1.call-start = ((), (), s32[]{:S(2)}) async-start(), calls=%async_computation.11 | async-start | bytes 1310720 | tf_op jit(solution)/shard_map/reduce_scatter | solution.py:272
  750.9 48.1 %reduce-scatter.26.cloned.1.call-start = ((), (), s32[]{:S(2)}) async-start(), calls=%async_computation.14 | async-start | bytes 450560 | tf_op jit(solution)/shard_map/reduce_scatter | solution.py:272
  775.1 47.1 %reduce-scatter.24.cloned.1.call-start = ((), (), s32[]{:S(2)}) async-start(), calls=%async_computation.13 | async-start | bytes 737280 | tf_op jit(solution)/shard_map/reduce_scatter | solution.py:272
  (145 other events, 1998.9 us)
Sparse Core Ops, SparseCore 0:
  142.9 46.5 all-gather.1
  547.3 26.2 reduce-scatter.13
  601.5 27.7 reduce-scatter.15
  632.1 20.6 reduce-scatter.21
  718.9 24.6 reduce-scatter.17
  751.0 26.1 reduce-scatter.19
  780.0 18.9 reduce-scatter.25
  801.9 20.2 reduce-scatter.23
where the time goes:
time: 882 us; the launch traced here: 872 us
  waiting for transfers between devices  343 us (39%)
  Pallas kernels  167 us (19%)
  other arithmetic  96.6 us (11%)
  matrix products  88.4 us (10%)
  local copies, waits for them, and re-layouts  85.3 us (10%)
  starting transfers between devices  65.3 us (7%)
  between operations  26.2 us (3%)
    ppermute x72, waiting for transfers between devices, swap(): return lax.ppermute(part, BOTH, [(i, i ^ flip) for i in range(self.count)])  313 us
    dot_general x24, matrix products, dot(): lax.dot_general(left, right, (((left_dim,), (right_dim,)), ((), ())), pre...  88.4 us
    ppermute x72, starting transfers between devices, swap(): return lax.ppermute(part, BOTH, [(i, i ^ flip) for i in range(self.count)])  64.6 us
    unnamed x263, local copies, waits for them, and re-layouts  52.7 us
    pallas_call x1, Pallas kernels, head(): pl.pallas_call(functools.partial(head_kernel, shard_rows, shard_half), gr...  42.8 us
    pallas_call x1, Pallas kernels, mix_back(): pl.pallas_call(mix_back_kernel, grid=(H,), in_specs=[fixed(SEG, D)] + wei...  33.5 us
    pallas_call x1, Pallas kernels, mix(): pl.pallas_call(mix_kernel, grid=(H,), in_specs=[fixed(SPAN, D), fixed(SPA...  29.6 us
    reduce_scatter x7, waiting for transfers between devices, along_line(): self.shard = lax.psum_scatter(block, FSDP, scatter_dimension=0, tiled=True)  29 us
  transfers between devices with their start and end apart: 80, of which 44 were waited for; matrix products, arithmetic and copies ran while one was open for 25% of the time, Pallas kernels for 13%

commit v1 on v0

--- a/solution.py
+++ b/solution.py
@@ -53,6 +53,15 @@
     )
 
 
+class Sent:
+    def __init__(self, value):
+        self.value = value
+
+
+def came(*parts):
+    return [part.value if isinstance(part, Sent) else part for part in parts]
+
+
 class Grid:
     def __init__(self):
         self.n_dp = lax.axis_size(DP)
@@ -76,11 +85,14 @@
         return lax.ppermute(part, BOTH, [(i, i ^ flip) for i in range(self.count)])
 
     def queued(self, part, dp_bits, fsdp_bits=0):
-        self.sent.append(self.swap(after(part, *self.before), dp_bits, fsdp_bits))
+        self.sent.append(Sent(self.swap(after(part, *self.before), dp_bits, fsdp_bits)))
         return self.sent[-1]
 
     def step(self, *ties):
-        self.before, self.sent = tuple(self.sent) + ties, []
+        came = lax.optimization_barrier(tuple(one.value for one in self.sent))
+        for one, value in zip(self.sent, came):
+            one.value = value
+        self.before, self.sent = came + ties, []
 
     def relative_blocks(self):
         found = [0]
@@ -113,28 +125,16 @@
 class Gather:
     def __init__(self, grid, shard, turned=False):
         self.grid, self.shard, self.turned = grid, shard, turned
+        self.line = None
 
     def direct_line(self):
         grid = self.grid
         self.pieces = [self.shard] + [grid.queued(self.shard, 0, k) for k in range(1, grid.n_fsdp)]
-        self.finish_line()
-
-    def first_line(self):
-        grid = self.grid
-        self.pieces = [self.shard, grid.queued(self.shard, 0, 1)] if grid.n_fsdp > 1 else [self.shard]
-
-    def second_line(self):
-        grid = self.grid
-        height = self.shard.shape[0]
-        bit = 2
-        while bit < grid.n_fsdp:
-            away = grid.queued(jnp.concatenate(self.pieces, axis=0), 0, bit)
-            self.pieces += [away[i * height : (i + 1) * height] for i in range(bit)]
-            bit *= 2
-        self.finish_line()
 
     def finish_line(self):
-        grid, pieces = self.grid, self.pieces
+        if self.line is not None:
+            return
+        grid, pieces = self.grid, came(*self.pieces)
         bit = 1
         while bit < grid.n_fsdp:
             odd = (grid.fsdp_index & bit) != 0
@@ -144,9 +144,9 @@
         if self.turned:
             self.line = turned_block(self.line)
 
-    def neighbours(self, *ties):
-        grid, block = self.grid, after(self.line, *ties)
-        self.line = block
+    def neighbours(self):
+        self.finish_line()
+        grid, block = self.grid, self.line
         inner = grid.layout[1:]
         self.pieces = [block]
         if len(inner) == 2:
@@ -154,43 +154,33 @@
             self.pieces += [grid.queued(block, near), grid.queued(block, outer)]
         else:
             for bit in inner[::-1]:
-                self.pieces = [jnp.concatenate(self.pieces, axis=0)]
+                self.pieces = [jnp.concatenate(came(*self.pieces), axis=0)]
                 self.pieces.append(grid.queued(self.pieces[0], bit))
 
-    def opposite(self, *ties):
+    def opposite(self):
         grid = self.grid
         inner = grid.layout[1:]
         if len(inner) == 2:
             outer, near = inner
             middle = self.line.shape[0] // 32 * 16
+            by_near, by_outer = came(*self.pieces[1:3])
             self.pieces += [
-                grid.queued(after(self.pieces[1][:middle], *ties), outer),
-                grid.queued(after(self.pieces[2][middle:], *ties), near),
+                grid.queued(by_near[:middle], outer),
+                grid.queued(by_outer[middle:], near),
             ]
-        self.own = jnp.concatenate(self.pieces, axis=0)
 
     def pair(self):
+        self.own = jnp.concatenate(came(*self.pieces), axis=0)
         self.other = self.grid.queued(self.own, 1)
 
-    def rows(self):
-        return jnp.concatenate([self.own, self.other], axis=0)
+    def sides(self):
+        return came(self.own, self.other)
 
     def by_block(self):
-        sides = [side.reshape(-1, *self.line.shape) for side in (self.own, self.other)]
+        sides = [side.reshape(-1, *self.line.shape) for side in self.sides()]
         if self.line.shape[1] % 128:
             sides = [jnp.concatenate(list(side), axis=1)[None] for side in sides]
         return tuple(sides)
-
-    def columns(self):
-        count = self.line.shape[0]
-        return jnp.concatenate(
-            [
-                side[i : i + count]
-                for side in (self.own, self.other)
-                for i in range(0, side.shape[0], count)
-            ],
-            axis=1,
-        )
 
 
 def opposite_and_neighbours(one, two):
@@ -200,29 +190,31 @@
         one.opposite()
         two.neighbours()
         return
+    two.finish_line()
     outer, near = inner
-    middle = one.line.shape[0] // 32 * 16
-    first = jnp.concatenate([one.pieces[1][:middle], two.line], axis=0)
-    second = jnp.concatenate([one.pieces[2][middle:], two.line], axis=0)
-    first, second = grid.queued(first, outer), grid.queued(second, near)
-    one.pieces += [first[:middle], second[: one.line.shape[0] - middle]]
-    one.own = jnp.concatenate(one.pieces, axis=0)
-    two.pieces = [two.line, second[one.line.shape[0] - middle :], first[middle:]]
+    height = one.line.shape[0]
+    middle = height // 32 * 16
+    by_near, by_outer = came(*one.pieces[1:3])
+    first = grid.queued(jnp.concatenate([by_near[:middle], two.line], axis=0), outer)
+    second = grid.queued(jnp.concatenate([by_outer[middle:], two.line], axis=0), near)
+    grid.step()
+    one.pieces += [first.value[:middle], second.value[: height - middle]]
+    two.pieces = [two.line, second.value[height - middle :], first.value[middle:]]
 
 
 class Reduce:
-    def __init__(self, grid, low, high, columns=False, turned=False):
-        self.grid, self.low, self.high = grid, low, high
+    def __init__(self, grid, part, columns=False, turned=False):
+        self.grid, self.part = grid, part
+        self.met = self.sums = ()
         self.columns, self.turned = columns, turned
 
     def pair(self, *ties):
-        self.high = self.high(ties).astype(bfloat)
-        self.came = self.grid.queued(self.high, 1)
-        return self.high
+        self.high = self.part(1, ties=ties)
+        self.arrived = self.grid.queued(self.high, 1)
 
     def opposite(self, *ties):
         grid = self.grid
-        total = (self.low(ties) + self.came.astype(single)).astype(bfloat)
+        total = self.total = self.part(0, (self.arrived.value,), ties)
         if self.columns:
             width = D // grid.n_dp
             self.blocks = [total[:, i : i + width] for i in range(0, total.shape[1], width)]
@@ -235,10 +227,7 @@
             self.middle = self.blocks[3].shape[0] // 32 * 16
             one, two = self.blocks[3][: self.middle], self.blocks[3][self.middle :]
             self.first, self.second = grid.queued(one, outer), grid.queued(two, near)
-            self.met = (self.first, self.second)
-            return one, two
-        self.met = ()
-        return (total,)
+            self.met = tuple(came(self.first, self.second))
 
     def neighbours(self):
         grid = self.grid
@@ -247,30 +236,30 @@
         if len(inner) == 2:
             outer, near = inner
             rows, middle = self.blocks[0].shape[0], self.middle
-            first, second = self.first.astype(single), self.second.astype(single)
+            first, second = (part.astype(single) for part in self.met)
             to_near = self.blocks[1].astype(single) + jnp.pad(first, ((0, rows - middle), (0, 0)))
             to_outer = self.blocks[2].astype(single) + jnp.pad(second, ((middle, 0), (0, 0)))
             one, two = to_near.astype(bfloat), to_outer.astype(bfloat)
-            self.sums = [grid.queued(one, near), grid.queued(two, outer)]
+            self.sums = came(grid.queued(one, near), grid.queued(two, outer))
             total = self.blocks[0].astype(single)
             for part in self.sums:
                 total = total + part.astype(single)
             self.block = total.astype(bfloat)
-            return one, two
+            return
         total = jnp.stack(self.blocks)
         for bit in inner:
             middle = total.shape[0] // 2
-            away = grid.queued(total[middle:], bit)
+            away = grid.queued(total[middle:], bit).value
             total = (total[:middle].astype(single) + away.astype(single)).astype(bfloat)
         self.block = total[0]
-        return (total,)
 
     def along_line(self):
         block = self.block.T if self.turned else self.block
-        if self.grid.summed:
-            block = after(block, self.grid.summed[-1])
+        summed = self.grid.summed
+        if summed:
+            block, summed[-1].shard = lax.optimization_barrier((block, summed[-1].shard))
         self.shard = lax.psum_scatter(block, FSDP, scatter_dimension=0, tiled=True)
-        self.grid.summed.append(self.shard)
+        summed.append(self)
 
     def value(self):
         return self.shard.astype(single)
@@ -369,7 +358,7 @@
 def mix_back_kernel(*refs):
     grad_ref, *sides = refs[:9]
     qa_ref, qb_ref, k_ref, r_ref, v_ref, o_ref, p_ref, every_ref, value_gate, output_gate = refs[9:19]
-    dq_ref, dk_ref, dr_ref, dv_ref, dzv_ref, dzo_ref, du_ref, dw_ref, out_ref = refs[19:]
+    dq_ref, dk_ref, dr_ref, dv_ref, dzv_ref, dzo_ref, du_ref, dw_ref, out_ref = refs[-9:]
     query, key, value, output = (lanes(*sides[i : i + 2]) for i in range(0, 8, 2))
     back = dot(output, grad_ref[...], 1, 1)
     gate = output_gate[0]
@@ -455,7 +444,7 @@
     )(normed, rel, *(sides * 5), content, position, value_gates, output_gates)
 
 
-def mix_back(grad, sides, stored, value_gates, output_gates):
+def mix_back(grad, sides, stored, value_gates, output_gates, ties):
     outs = [
         head_rows(DH, SPAN),
         head_rows(DH, SPAN),
@@ -476,15 +465,16 @@
         + weight_blocks(sides, VALUE_ROW, EXPERT)
         + weight_blocks(sides, OUTPUT_ROW, EXPERT)
         + [head_rows(*array.shape[1:])[0] for array in stored]
-        + [head_rows(8, SPAN)[0], head_rows(8, SEG)[0]],
+        + [head_rows(8, SPAN)[0], head_rows(8, SEG)[0]]
+        + [untouched] * len(ties),
         out_specs=[spec for spec, _ in outs],
         out_shape=[shape for _, shape in outs],
         compiler_params=params,
         cost_estimate=light,
-    )(grad, *(sides * 4), *stored, value_gates, output_gates)
-
-
-ff_tile = 512
+    )(grad, *(sides * 4), *stored, value_gates, output_gates, *ties)
+
+
+ff_tile = 1024
 ff_columns = pl.BlockSpec((SEG, ff_tile), lambda i: (0, i))
 ff_weights = pl.BlockSpec((D // 2, ff_tile), lambda i: (0, i))
 ff_bias = pl.BlockSpec((1, ff_tile), lambda i: (0, i))
@@ -533,9 +523,8 @@
     )(active, *sides)
 
 
-def ff_back_kernel(
-    in_ref, slope_ref, own_down, other_down, own_up, other_up, grad_ref, bias_ref, out_ref, total
-):
+def ff_back_kernel(in_ref, slope_ref, own_down, other_down, own_up, other_up, *refs):
+    grad_ref, bias_ref, out_ref, total = refs[-4:]
     tile = pl.program_id(0)
 
     @pl.when(tile == 0)
@@ -556,11 +545,11 @@
         out_ref[...] = total[...].astype(bfloat)
 
 
-def ff_back(grad, slope, down, up):
+def ff_back(grad, slope, down, up, ties):
     return pl.pallas_call(
         ff_back_kernel,
         grid=(FF // ff_tile,),
-        in_specs=[fixed(SEG, D), ff_columns] + [ff_weights] * 4,
+        in_specs=[fixed(SEG, D), ff_columns] + [ff_weights] * 4 + [untouched] * len(ties),
         out_specs=[ff_columns, ff_bias, fixed(SEG, D)],
         out_shape=[
             jax.ShapeDtypeStruct((SEG, FF), bfloat),
@@ -570,7 +559,115 @@
         scratch_shapes=[pltpu.VMEM((SEG, D), single)],
         compiler_params=params,
         cost_estimate=light,
-    )(grad, slope, *down, *up)
+    )(grad, slope, *down, *up, *ties)
+
+
+untouched = pl.BlockSpec(memory_space=pl.ANY)
+
+
+def product_kernel(left_dim, adds, left_ref, right_ref, *refs):
+    total = dot(left_ref[...], right_ref[...], left_dim, 0)
+    if adds:
+        total = total + refs[0][...].astype(single)
+    refs[-1][...] = total.astype(bfloat)
+
+
+def ff_product(wide, other, side, came=(), ties=()):
+    return pl.pallas_call(
+        functools.partial(product_kernel, 0, len(came)),
+        grid=(FF // ff_tile,),
+        in_specs=[pl.BlockSpec((SEG, D // 2), lambda i: (0, side)), ff_columns]
+        + [ff_weights] * len(came)
+        + [untouched] * len(ties),
+        out_specs=ff_weights,
+        out_shape=jax.ShapeDtypeStruct((D // 2, FF), bfloat),
+        compiler_params=params,
+        cost_estimate=light,
+    )(wide, other, *came, *ties)
+
+
+def expert_product(wide, other, side, came=(), ties=()):
+    rows, depth = other.shape
+    tile = pl.BlockSpec((EXPERT, D // 2), lambda i: (i, 0))
+    return pl.pallas_call(
+        functools.partial(product_kernel, 1, len(came)),
+        grid=(rows // EXPERT,),
+        in_specs=[
+            pl.BlockSpec((EXPERT, depth), lambda i: (i, 0)),
+            pl.BlockSpec((depth, D // 2), lambda i: (0, side)),
+        ]
+        + [tile] * len(came)
+        + [untouched] * len(ties),
+        out_specs=tile,
+        out_shape=jax.ShapeDtypeStruct((rows, D // 2), bfloat),
+        compiler_params=params,
+        cost_estimate=light,
+    )(other, wide, *came, *ties)
+
+
+def table_product_kernel(first, adds, grad_ref, ids_ref, out_grad, in_grad, *refs):
+    rows = grad_ref.shape[1]
+    place = first + pl.program_id(0) * rows + lax.broadcasted_iota(jnp.int32, (rows, SEG), 0)
+    chosen = jnp.where(place == ids_ref[...], 1.0, 0.0).astype(bfloat)
+    total = dot(grad_ref[...], out_grad[...], 0, 0) + dot(chosen, in_grad[...], 1, 0)
+    if adds:
+        total = total + refs[0][...].astype(single)
+    refs[-1][...] = total.astype(bfloat)
+
+
+def table_product(grad_logits, ids, normed, grad_embedded, first, rows, side, came=(), ties=()):
+    half = pl.BlockSpec((SEG, D // 2), lambda i: (0, side))
+    tile = pl.BlockSpec((head_tile, D // 2), lambda i: (i, 0))
+    return pl.pallas_call(
+        functools.partial(table_product_kernel, first, len(came)),
+        grid=(rows // head_tile,),
+        in_specs=[
+            pl.BlockSpec((SEG, head_tile), lambda i: (0, first // head_tile + i)),
+            fixed(1, SEG),
+            half,
+            half,
+        ]
+        + [tile] * len(came)
+        + [untouched] * len(ties),
+        out_specs=tile,
+        out_shape=jax.ShapeDtypeStruct((rows, D // 2), bfloat),
+        compiler_params=params,
+        cost_estimate=light,
+    )(grad_logits, ids, normed, grad_embedded, *came, *ties)
+
+
+def small_product_kernel(adds, q_ref, k_ref, r_ref, gates_ref, vectors_ref, normed, rel, *refs):
+    out = refs[-1]
+
+    def put(start, value):
+        stop = start + value.shape[0]
+        if adds:
+            value = value + refs[0][start:stop, :].astype(single)
+        out[start:stop, :] = value.astype(bfloat)
+
+    put(0, dot(q_ref[...], normed[...], 1, 0))
+    put(HD, dot(k_ref[...], normed[...], 1, 0))
+    put(2 * HD, dot(r_ref[...], rel[...], 1, 0))
+    put(3 * HD, dot(gates_ref[...], normed[...], 1, 0) + vectors_ref[...])
+
+
+def small_product(grads, vectors, normed, rel, side, came=(), ties=()):
+    def half(rows):
+        return pl.BlockSpec((rows, D // 2), lambda i: (0, side))
+
+    rows = 3 * HD + LAST_ROWS
+    return pl.pallas_call(
+        functools.partial(small_product_kernel, len(came)),
+        grid=(1,),
+        in_specs=[fixed(*grad.shape) for grad in grads]
+        + [half(LAST_ROWS), half(SPAN), half(SPAN)]
+        + [fixed(rows, D // 2)] * len(came)
+        + [untouched] * len(ties),
+        out_specs=fixed(rows, D // 2),
+        out_shape=jax.ShapeDtypeStruct((rows, D // 2), bfloat),
+        compiler_params=params,
+        cost_estimate=light,
+    )(*grads, vectors, normed, rel, *came, *ties)
 
 
 def lookup_kernel(first, ids_ref, own_ref, other_ref, out_ref):
@@ -806,9 +903,8 @@
     tables[0].neighbours()
     tables[1].direct_line()
     grid.step()
+    attending.direct_line()
     opposite_and_neighbours(tables[0], tables[1])
-    attending.direct_line()
-    grid.step()
     middle = expand.shape[1]
     lines = lax.all_gather(
         after(jnp.concatenate([expanding.shard, contracting.shard], axis=1), *grid.before),
@@ -824,19 +920,16 @@
     attending.opposite()
     expanding.neighbours()
     tables[1].pair()
+    found = [lookup(ids[:, None], *tables[0].by_block(), 0)]
+    grid.step(found[0])
     tables_by_block = [part.by_block() for part in tables]
-    found = [lookup(ids[:, None], *tables_by_block[0], 0)]
-    grid.step(found[0])
     attending.pair()
     expanding.opposite()
-    contracting.neighbours()
     found.append(lookup(ids[:, None], *tables_by_block[1], part_rows))
     embedded = (found[0] + found[1]) * D**0.5
     grid.step(embedded)
-    contracting.opposite()
+    contracting.neighbours()
     expanding.pair()
-    grid.step()
-    contracting.pair()
     attention = attending.by_block()
     last_rows = jnp.concatenate(
         [side[i, GATE_ROW:] for side in attention for i in range(side.shape[0])], axis=1
@@ -863,12 +956,18 @@
         value_gates,
         output_gates,
     )
+    grid.step(mixed)
+    contracting.opposite()
     gated = gated.reshape(H * EXPERT, SEG)
     residual = embedded + mixed
     normal_mid, spread_mid = normalised(residual)
     normed_mid = (normal_mid * gains[1]).astype(bfloat)
-    up, down = (expanding.own, expanding.other), (contracting.own, contracting.other)
+    up = expanding.sides()
     active, slope = expand_forward(normed_mid, up, biases[None, 2 * HD :])
+    grid.step()
+    contracting.pair()
+    grid.step()
+    down = contracting.sides()
     final = residual + contract_forward(active, down) + gains[3]
     normal_out, spread_out = normalised(final)
     normed_out = (normal_out * gains[2]).astype(bfloat)
@@ -885,38 +984,31 @@
     grad_branch = grad_final.astype(bfloat)
     grad_bias_down = jnp.sum(grad_branch.astype(single), axis=0)
 
-    def summing(wide, other, wide_dim, other_dim):
-        def part(start):
-            side = lax.slice_in_dim(wide, start, start + half, axis=1)
-            return lambda ties: dot(after(side, *ties), other, wide_dim, other_dim)
-
-        return Reduce(grid, part(0), part(half))
+    def summing(wide, other):
+        return Reduce(grid, functools.partial(ff_product, wide, other))
 
     def summing_turned(wide, other):
-        def part(start):
-            side = lax.slice_in_dim(wide, start, start + half, axis=1)
-            return lambda ties: dot(other, after(side, *ties), 1, 0)
-
-        return Reduce(grid, part(0), part(half), True, True)
+        return Reduce(grid, functools.partial(expert_product, wide, other), True, True)
 
     grid.step()
-    contracting = summing(grad_branch, active, 0, 0)
-    tie = contracting.pair()
-    grad_hidden, grad_bias_up, grad_mid = ff_back(after(grad_branch, tie), slope, down, up)
-    expanding = summing(normed_mid, grad_hidden, 0, 0)
-    tie = expanding.pair()
-    tie_two = contracting.opposite()
-    grad_mid = after(grad_mid, tie, *tie_two)
+    contracting = summing(grad_branch, active)
+    contracting.pair()
+    grad_hidden, grad_bias_up, grad_mid = ff_back(
+        grad_branch, slope, down, up, [contracting.high]
+    )
+    expanding = summing(normed_mid, grad_hidden)
+    expanding.pair()
+    contracting.opposite(expanding.high)
+    expanding.opposite(contracting.total)
     grad_residual, grad_gain_mid = norm_gradient(
         grad_mid.astype(single), normal_mid, spread_mid, gains[1]
     )
     grad_residual = grad_residual + grad_final
     low_residual = grad_residual.astype(bfloat)
     outputting = summing_turned(low_residual, gated)
-    tie = outputting.pair()
-    tie_two = expanding.opposite()
-    tie_three = contracting.neighbours()
-    tie_four = outputting.opposite()
+    outputting.pair(expanding.total)
+    contracting.neighbours()
+    expanding.neighbours()
     (
         grad_queries,
         grad_keys,
@@ -928,14 +1020,17 @@
         grad_position,
         grad_normed,
     ) = mix_back(
-        after(low_residual, *tie_two, *tie_three, *tie_four),
+        low_residual,
         attention,
         stored,
         value_gates,
         output_gates,
-    )
-    tie = expanding.neighbours()
+        [outputting.high, *contracting.met, *expanding.met],
+    )
     grad_values = grad_values.reshape(H * EXPERT, SPAN)
+    valuing = summing_turned(normed, grad_values)
+    valuing.pair(*contracting.sums)
+    outputting.opposite(valuing.high)
     grad_gates = jnp.concatenate(
         [
             grad_value_gates[:, :NE].reshape(H * NE, SPAN),
@@ -945,10 +1040,7 @@
         axis=0,
     ).astype(bfloat)
     contracting.along_line()
-    tie = outputting.neighbours()
     grad_normed = (grad_normed + dot(grad_gates, last_rows, 0, 0)).astype(bfloat)
-    grad_normed = after(grad_normed, *expanding.sums)
-    expanding.along_line()
     grad_stream, grad_gain_in = norm_gradient(
         grad_normed.astype(single), normal_in, spread_in, gains[0]
     )
@@ -960,57 +1052,38 @@
         + [nothing] * (LAST_ROWS - GATES - 4)
     )
 
-    tokens = jnp.arange(2 * part_rows, dtype=jnp.int32)[None, :]
-    looked = (ids[:, None] == tokens).astype(bfloat)
-    table_left = jnp.concatenate([grad_logits, looked], axis=0)
-    table_right = jnp.concatenate([normed_out, grad_embedded * bfloat(D**0.5)], axis=0)
-
-    def table_summing(start):
-        side = table_left[:, start : start + part_rows]
-
-        def part(column):
-            right = table_right[:, column : column + half]
-            return lambda ties: dot(side, after(right, *ties), 0, 0)
-
-        return Reduce(grid, part(0), part(half), columns=True)
+    def table_summing(first):
+        part = functools.partial(
+            table_product,
+            grad_logits,
+            ids[None, :],
+            normed_out,
+            grad_embedded * bfloat(D**0.5),
+            first,
+            part_rows,
+        )
+        return Reduce(grid, part, True)
 
     tables = [table_summing(i) for i in (0, part_rows)]
-    valuing = summing_turned(normed, grad_values)
-
-    def small_half(start):
-        def compute(ties):
-            stop = start + half
-            side = after(normed[:, start:stop], *ties)
-            return jnp.concatenate(
-                [
-                    dot(grad_queries.reshape(HD, SPAN), side, 1, 0),
-                    dot(grad_keys.reshape(HD, SPAN), side, 1, 0),
-                    dot(grad_rel.reshape(HD, SPAN), rel_table[:, start:stop], 1, 0),
-                    dot(grad_gates, side, 1, 0) + grad_vectors[:, start:stop],
-                ],
-                axis=0,
-            )
-
-        return compute
-
-    smalling = Reduce(grid, small_half(0), small_half(half), True, True)
-    tie = tables[0].pair(contracting.shard)
-    tie = tables[1].pair(tie)
+    grads = [part.reshape(HD, SPAN) for part in (grad_queries, grad_keys, grad_rel)] + [grad_gates]
+    small = functools.partial(small_product, grads, grad_vectors, normed, rel_table)
+    smalling = Reduce(grid, small, True, True)
+    expanding.along_line()
+    outputting.neighbours()
+    tables[0].pair(outputting.total, *expanding.sums)
+    smalling.pair(tables[0].high)
+    valuing.opposite(smalling.high, *outputting.met)
     outputting.along_line()
-    tie = tables[0].opposite(tie, *outputting.sums, expanding.shard)
-    tie = (valuing.pair(*tie),)
-    tie = tables[1].opposite(*tie)
-    tie = tables[0].neighbours() + tie
-    tie = (smalling.pair(*tie, outputting.shard),)
-    tie = valuing.opposite(*tie, *tables[1].met)
-    tie = tables[1].neighbours() + tie
-    tables[0].along_line()
-    tie = smalling.opposite(*tie)
+    tables[1].pair(valuing.total, contracting.shard)
+    smalling.opposite(tables[1].high)
     valuing.neighbours()
-    tables[1].along_line()
+    tables[0].opposite(smalling.total, *valuing.met, *outputting.sums)
     smalling.neighbours()
-    valuing.along_line()
-    smalling.along_line()
+    tables[1].opposite(tables[0].total, *valuing.sums, *smalling.met)
+    tables[0].neighbours()
+    tables[1].neighbours()
+    for part in (valuing, smalling, tables[0], tables[1]):
+        part.along_line()
     sum_contract, sum_expand, sum_outputs, sum_values, sum_small = (
         part.value() for part in (contracting, expanding, outputting, valuing, smalling)
     )
@@ -1028,8 +1101,8 @@
     ]
     most_tokens = grid.count * SEG
     local_squares = jnp.zeros((), single)
-    for grad in shard_grads:
-        scaled = grad * (1.0 / most_tokens)
+    for part in tables + [contracting, expanding, outputting, valuing, smalling]:
+        scaled = part.value() * (1.0 / most_tokens)
         local_squares = local_squares + jnp.sum(scaled * scaled)
     shared = jnp.concatenate(
         [

time: 882 us -> 794 us (0.900)
  waiting for transfers between devices: 343 us -> 201 us
  Pallas kernels: 167 us -> 266 us
  matrix products: 88.4 us -> 7.96 us
  other arithmetic: 96.6 us -> 115 us
    ppermute x72, waiting for transfers between devices: 313 us -> 162 us  [swap(): return lax.ppermute(part, BOTH, [(i, i ^ flip) for i in range(self.count)])]
    pallas_call x0 -> x14, Pallas kernels: none -> 103 us  [the longest x4 40.1 us: table_product(): pl.pallas_call(functools.partial(table_product_kernel, first, len(came)),...]
    dot_general x24 -> x4, matrix products: 88.4 us -> 7.96 us  [dot(): lax.dot_general(left, right, (((left_dim,), (right_dim,)), ((), ())), pre...]
    unnamed x8 -> x11, waiting for transfers between devices: 0.13 us -> 18.8 us
    slice x7, local copies, waits for them, and re-layouts: 1.44 us -> 13.2 us  [opposite(): one, two = (self.blocks[3][:self.middle], self.blocks[3][self.middle:])]
    reduce_scatter x7 -> x4, waiting for transfers between devices: 29 us -> 19 us  [along_line(): self.shard = lax.psum_scatter(block, FSDP, scatter_dimension=0, tiled=True)]
    convert_element_type x3 -> x0, other arithmetic: 9.57 us -> none  [the longest x1 6.46 us: body(): looked = (ids[:, None] == tokens).astype(bfloat)]
    unnamed x263 -> x224, local copies, waits for them, and re-layouts: 52.7 us -> 46.3 us
  transfers between devices with their start and end apart: 80 -> 80, of which waited for: 44 -> 30; matrix products, arithmetic and copies ran while one was open for 25% -> 21% of each run, Pallas kernels for 13% -> 27%
where the time goes in v1:
time: 794 us; the launch traced here: 781 us
  Pallas kernels  266 us (34%)
  waiting for transfers between devices  201 us (25%)
  other arithmetic  115 us (14%)
  local copies, waits for them, and re-layouts  93.1 us (12%)
  starting transfers between devices  73.8 us (9%)
  between operations  25.1 us (3%)
  matrix products  7.96 us (1%)
    ppermute x72, waiting for transfers between devices, swap(): return lax.ppermute(part, BOTH, [(i, i ^ flip) for i in range(self.count)])  162 us
    ppermute x72, starting transfers between devices, swap(): return lax.ppermute(part, BOTH, [(i, i ^ flip) for i in range(self.count)])  73.2 us
    unnamed x224, local copies, waits for them, and re-layouts  46.3 us
    pallas_call x1, Pallas kernels, head(): pl.pallas_call(functools.partial(head_kernel, shard_rows, shard_half), gr...  42.6 us
    pallas_call x4, Pallas kernels, table_product(): pl.pallas_call(functools.partial(table_product_kernel, first, len(came)),...  40.1 us
    pallas_call x1, Pallas kernels, mix_back(): pl.pallas_call(mix_back_kernel, grid=(H,), in_specs=[fixed(SEG, D)] + wei...  33.4 us
    pallas_call x1, Pallas kernels, mix(): pl.pallas_call(mix_kernel, grid=(H,), in_specs=[fixed(SPAN, D), fixed(SPA...  29.6 us
    pallas_call x4, Pallas kernels, ff_product(): pl.pallas_call(functools.partial(product_kernel, 0, len(came)), grid=(FF...  27.4 us
  transfers between devices with their start and end apart: 80, of which 30 were waited for; matrix products, arithmetic and copies ran while one was open for 21% of the time, Pallas kernels for 27%

profile of v1, /device:TPU:0, one launch (start us, length us, event | category | flops | bytes accessed | tf_op | source)
XLA Modules:
  0.0 781.3 jit_solution(15165435360855183394)
XLA Ops:
  8.7 3.1 collective-permute-start
  14.5 8.1 %fusion.19 = (bf16[1024,512]{1,0:T(8,128)(2,1)S(1)}, bf16[1024,512]{1,0:T(8,128)(2,1)S(1)}) fusion(f32[512]{0:T(512)S(1)} %multiply_exponential_fusion, f32[1024]{0:T(1024)S(1)} %rev.3), kind=kLoop, calls=%fused_computation.34 | loop fusion | flops 1572864 | bytes 2103296 | tf_op jit(solution)/shard_map/convert.39
  22.7 3.7 fusion.30.refs_1_.rel
  29.1 4.0 collective-permute-done.1
  40.7 4.8 collective-permute-start.5
  49.8 4.2 collective-permute-done.5
  54.0 12.7 %collective-permute-done.6 = bf16[1024,128]{1,0:T(8,128)(2,1)S(1)} collective-permute-done((bf16[1024,128]{1,0:T(8,128)(2,1)}, bf16[1024,128]{1,0:T(8,128)(2,1)S(1)}, u32[]{:S(2)}, u32[]{:S(2)}) %collective-permute-start.6) | collective-permute-done | bytes 262176 | tf_op jit(solution)/shard_map/ppermute | solution.py:85
  81.2 5.3 collective-permute-done.10
  86.5 4.7 collective-permute-done.8
  91.3 12.6 %collective-permute-done.9 = bf16[32,5888]{1,0:T(8,128)(2,1)S(1)} collective-permute-done((bf16[32,5888]{1,0:T(8,128)(2,1)S(1)}, bf16[32,5888]{1,0:T(8,128)(2,1)S(1)}, u32[]{:S(2)}, u32[]{:S(2)}) %collective-permute-start.9) | collective-permute-done | bytes 376864 | tf_op jit(solution)/shard_map/ppermute | solution.py:85
  119.7 39.4 %collective-permute-done.14 = bf16[2048,128]{1,0:T(8,128)(2,1)S(1)} collective-permute-done((bf16[2048,128]{1,0:T(8,128)(2,1)}, bf16[2048,128]{1,0:T(8,128)(2,1)S(1)}, u32[]{:S(2)}, u32[]{:S(2)}) %collective-permute-start.14) | collective-permute-done | bytes 524320 | tf_op jit(solution)/shard_map/ppermute | solution.py:85
  165.8 4.0 constant_dynamic-update-slice_fusion.42
  179.5 9.2 %shard_map.572 = f32[512,1024]{1,0:T(8,128)} custom-call(s32[512,1]{1,0:T(8,128)} %fusion.77.ids_ref, bf16[4,4096,128]{2,1,0:T(8,128)(2,1)} %bitcast.8.own_ref.own_zero, bf16[4,4096,128]{2,1,0:T(8,128)(2,1)} %bitcast.9.other_ref.other_zero), custom_call_target="tpu_custom_call" | custom-call | flops 10000000 | bytes 100000 | tf_op jit(solution)/shard_map/pallas_call | solution.py:693
  190.3 21.0 %collective-permute-done.19 = bf16[2944,128]{1,0:T(8,128)(2,1)} collective-permute-done((bf16[2944,128]{1,0:T(8,128)(2,1)}, bf16[2944,128]{1,0:T(8,128)(2,1)}, u32[]{:S(2)}, u32[]{:S(2)}) %collective-permute-start.19) | collective-permute-done | bytes 753696 | tf_op jit(solution)/shard_map/ppermute | solution.py:85
  220.8 8.9 %shard_map.573 = f32[512,1024]{1,0:T(8,128)} custom-call(s32[512,1]{1,0:T(8,128)} %fusion.77.ids_ref, bf16[4,4096,128]{2,1,0:T(8,128)(2,1)} %bitcast.10.own_ref.own_one, bf16[4,4096,128]{2,1,0:T(8,128)(2,1)} %bitcast.12.other_ref.other_one), custom_call_target="tpu_custom_call" | custom-call | flops 10000000 | bytes 100000 | tf_op jit(solution)/shard_map/pallas_call | solution.py:693
  231.7 3.4 add_multiply_fusion
  260.3 29.6 %shard_map.574 = (bf16[4,112,512]{2,1,0:T(8,128)(2,1)}, bf16[4,112,512]{2,1,0:T(8,128)(2,1)}, bf16[4,112,1024]{2,1,0:T(8,128)(2,1)}, bf16[4,112,1024]{2,1,0:T(8,...) custom-call(bf16[1024,1024]{1,0:T(8,128)(2,1)} %copy-done.4, ...), custom_call_target="tpu_custom_call" | custom-call | flops 10000000 | bytes 100000 | tf_op jit(solution)/shard_map/pallas_call | solution.py:429
  296.7 8.2 %collective-permute-done.30 = bf16[64,4096]{1,0:T(8,128)(2,1)S(1)} collective-permute-done((bf16[64,4096]{1,0:T(8,128)(2,1)S(1)}, bf16[64,4096]{1,0:T(8,128)(2,1)S(1)}, u32[]{:S(2)}, u32[]{:S(2)}) %collective-permute-start.30) | collective-permute-done | bytes 524320 | tf_op jit(solution)/shard_map/ppermute | solution.py:85
  314.5 12.2 %shard_map.575 = (bf16[512,4096]{1,0:T(8,128)(2,1)}, bf16[512,4096]{1,0:T(8,128)(2,1)}) custom-call(bf16[512,1024]{1,0:T(8,128)(2,1)} %multiply_convert_fusion.2.in_ref.left_ref, bf16[512,4096]{1,0:T(8,128)(2,1)} %constant_dynamic-update-slice_fusion.33.own_ref.own_up, bf16[512,4096]{1,0:T(8,128)(2,1)} %collective-permute-done.28.other_ref.other_up, ...), custom_call_target="tpu_custom_call" | custom-call | flops 10000000 | bytes 100000 | tf_op jit(solution)/shard_map/pallas_call | solution.py:494
  326.7 9.2 %shard_map.576 = f32[512,1024]{1,0:T(8,128)} custom-call(bf16[512,4096]{1,0:T(8,128)(2,1)} %get-tuple-element.169.act_ref.right_ref, bf16[512,4096]{1,0:T(8,128)(2,1)} %constant_dynamic-update-slice_fusion.38.own_ref.own_down, bf16[512,4096]{1,0:T(8,128)(2,1)} %collective-permute-done.31.other_ref.other_down), custom_call_target="tpu_custom_call" | custom-call | flops 10000000 | bytes 100000 | tf_op jit(solution)/shard_map/pallas_call | solution.py:515
  339.9 42.6 %shard_map.577 = (bf16[512,8192]{1,0:T(8,128)(2,1)}, bf16[512,1024]{1,0:T(8,128)(2,1)}, f32[512,1]{1,0:T(8,128)}) custom-call(bf16[512,1024]{1,0:T(8,128)(2,1)} %multiply_convert_fusion.1.hf_ref.out_grad, s32[512,1]{1,0:T(8,128)} %fusion.81.goal_ref, f32[512,1]{1,0:T(8,128)} %fusion.91.counted_ref, bf16[4,4096,128]{2,1,0:T(8,128)(2,1)} %bitcast.8.own_ref.own_zero, ...), custom_call_target="tpu_custom_call" | custom-call | flops 10000000 | bytes 100000 | tf_op jit(solution)/shard_map/pallas_call | solution.py:803
  386.4 6.3 shard_map.578.refs_0_
  393.3 15.4 %shard_map.579 = (bf16[512,4096]{1,0:T(8,128)(2,1)}, f32[1,4096]{1,0:T(1,128)}, bf16[512,1024]{1,0:T(8,128)(2,1)}) custom-call(bf16[512,1024]{1,0:T(8,128)(2,1)} %get-tuple-element.401.left_ref.in_ref, bf16[512,4096]{1,0:T(8,128)(2,1)} %get-tuple-element.178.slope_ref, bf16[512,4096]{1,0:T(8,128)(2,1)} %constant_dynamic-update-slice_fusion.38.own_ref.own_down, ...), custom_call_target="tpu_custom_call" | custom-call | flops 10000000 | bytes 100000 | tf_op jit(solution)/shard_map/pallas_call | solution.py:549
  408.7 6.5 shard_map.580.refs_1_
  418.7 7.3 shard_map.581.refs_1_
  431.0 7.3 shard_map.582.refs_0_
  441.9 5.0 shard_map.583.refs_19_
  451.5 4.1 collective-permute-done.36.refs_22_
  461.2 33.4 %shard_map.584 = (bf16[4,112,1024]{2,1,0:T(8,128)(2,1)}, bf16[4,112,1024]{2,1,0:T(8,128)(2,1)}, bf16[4,112,1024]{2,1,0:T(8,128)(2,1)}, bf16[4,560,1024]{2,1,0:T(...) custom-call(bf16[512,1024]{1,0:T(8,128)(2,1)} %get-tuple-element.405, ...), custom_call_target="tpu_custom_call" | custom-call | flops 10000000 | bytes 100000 | tf_op jit(solution)/shard_map/pallas_call | solution.py:459
  498.6 4.0 fusion
  505.2 3.3 add_convert_fusion.7
  508.6 6.5 shard_map.585.refs_1_
  515.2 5.7 shard_map.586.refs_0_
  524.6 3.1 fusion.38.in_grad
  532.0 9.6 %shard_map.587.refs_0_ = bf16[4096,512]{1,0:T(8,128)(2,1)} custom-call(bf16[512,8192]{1,0:T(8,128)(2,1)} %get-tuple-element.194.grad_ref, s32[1,512]{1,0:T(1,128)} %get-tuple-element.403.ids_ref, bf16[512,1024]{1,0:T(8,128)(2,1)} %multiply_convert_fusion.1.hf_ref.out_grad, bf16[512,1024]{1,0:T(8,128)(2,1)} %fusion.38.in_grad, ...), custom_call_target="tpu_custom_call" | custom-call | flops 10000000 | bytes 100000 | tf_op jit(solution)/shard_map/pallas_call | solution.py:621
  541.6 5.4 shard_map.588.refs_1_
  555.2 6.6 shard_map.589.refs_0_
  568.4 9.6 %shard_map.590.refs_1_ = bf16[4096,512]{1,0:T(8,128)(2,1)} custom-call(bf16[512,8192]{1,0:T(8,128)(2,1)} %get-tuple-element.194.grad_ref, s32[1,512]{1,0:T(1,128)} %get-tuple-element.403.ids_ref, bf16[512,1024]{1,0:T(8,128)(2,1)} %multiply_convert_fusion.1.hf_ref.out_grad, bf16[512,1024]{1,0:T(8,128)(2,1)} %fusion.38.in_grad, ...), custom_call_target="tpu_custom_call" | custom-call | flops 10000000 | bytes 100000 | tf_op jit(solution)/shard_map/pallas_call | solution.py:621
  578.0 5.9 shard_map.591.refs_1_
  599.3 10.4 %shard_map.592.refs_1_ = bf16[4096,512]{1,0:T(8,128)(2,1)} custom-call(bf16[512,8192]{1,0:T(8,128)(2,1)} %get-tuple-element.194.grad_ref, s32[1,512]{1,0:T(1,128)} %get-tuple-element.403.ids_ref, bf16[512,1024]{1,0:T(8,128)(2,1)} %multiply_convert_fusion.1.hf_ref.out_grad, bf16[512,1024]{1,0:T(8,128)(2,1)} %fusion.38.in_grad, ...), custom_call_target="tpu_custom_call" | custom-call | flops 10000000 | bytes 100000 | tf_op jit(solution)/shard_map/pallas_call | solution.py:621
  616.6 7.2 reduce-scatter.22.cloned.1.call-done
  634.6 10.4 %shard_map.593 = bf16[4096,512]{1,0:T(8,128)(2,1)} custom-call(bf16[512,8192]{1,0:T(8,128)(2,1)} %get-tuple-element.194.grad_ref, s32[1,512]{1,0:T(1,128)} %get-tuple-element.403.ids_ref, bf16[512,1024]{1,0:T(8,128)(2,1)} %multiply_convert_fusion.1.hf_ref.out_grad, bf16[512,1024]{1,0:T(8,128)(2,1)} %fusion.38.in_grad, ...), custom_call_target="tpu_custom_call" | custom-call | flops 10000000 | bytes 100000 | tf_op jit(solution)/shard_map/pallas_call | solution.py:621
  650.9 5.8 collective-permute-done.62
  658.0 3.3 add_convert_fusion.1
  661.2 11.5 %reduce-scatter.26.cloned.1.call-done = bf16[32,1408]{1,0:T(8,128)(2,1)} async-done(((bf16[128,1408]{1,0:T(8,128)(2,1)}), bf16[32,1408]{1,0:T(8,128)(2,1)}) %reduce-scatter.26.cloned.1.call-update) | async-done | bytes 90128
  678.8 20.7 %collective-permute-done.58 = bf16[4096,128]{1,0:T(8,128)(2,1)S(1)} collective-permute-done((bf16[4096,128]{1,0:T(8,128)(2,1)S(1)}, bf16[4096,128]{1,0:T(8,128)(2,1)S(1)}, u32[]{:S(2)}, u32[]{:S(2)}) %collective-permute-start.58) | collective-permute-done | bytes 1048608 | tf_op jit(solution)/shard_map/ppermute | solution.py:85
  709.5 19.0 %reduce-scatter.20.cloned.1.call-done = bf16[1024,128]{1,0:T(8,128)(2,1)} async-done(((bf16[4096,128]{1,0:T(8,128)(2,1)}), bf16[1024,128]{1,0:T(8,128)(2,1)}) %reduce-scatter.20.cloned.1.call-update) | async-done | bytes 262160 | tf_op jit(solution)/shard_map/reduce_scatter | solution.py:261
  744.3 3.8 collective-permute-done.70
  (558 shorter events, 268.2 us)
Async XLA Ops:
  7.2 158.6 %all-gather.2.cloned.1.call-start = ((), (), s32[]{:S(2)}) async-start(), calls=%async_computation.7 | async-start | bytes 2621440 | tf_op jit(solution)/shard_map/all_gather | solution.py:909
  37.7 29.0 %collective-permute-start.3 = (bf16[4096,128]{1,0:T(8,128)(2,1)}, bf16[4096,128]{1,0:T(8,128)(2,1)S(1)}, u32[]{:S(2)}, u32[]{:S(2)}) collective-permute-start(bf16[4096,128]{1,0:T(8,128)(2,1)} %pad_maximum_fusion.2), channel_id=1, source_target_pairs={{0,8},{1,9},{2,10},{3,11},{4,12},{5,13},{6,14},{7,15},{8,0},{9,1},... | collective-permute-start | bytes 3145736 | tf_op jit(solution)/shard_map/ppermute | solution.py:85
  39.2 27.6 %collective-permute-start.4 = (bf16[4096,128]{1,0:T(8,128)(2,1)}, bf16[4096,128]{1,0:T(8,128)(2,1)}, u32[]{:S(2)}, u32[]{:S(2)}) collective-permute-start(bf16[4096,128]{1,0:T(8,128)(2,1)} %pad_maximum_fusion.2), channel_id=1, source_target_pairs={{0,16},{1,17},{2,18},{3,19},{4,20},{5,21},{6,22},{7,23},{8,24},{9,... | collective-permute-start | bytes 3145736 | tf_op jit(solution)/shard_map/ppermute | solution.py:85
  71.7 32.1 %collective-permute-start.12 = (bf16[6144,128]{1,0:T(8,128)(2,1)S(1)}, bf16[6144,128]{1,0:T(8,128)(2,1)S(1)}, u32[]{:S(2)}, u32[]{:S(2)}) collective-permute-start(bf16[6144,128]{1,0:T(8,128)(2,1)S(1)} %get-tuple-element.134), channel_id=1, source_target_pairs={{0,8},{1,9},{2,10},{3,11},{4,12},{5,13},{6,14},{7,15},{8,0},{9,1},... | collective-permute-start | bytes 4718600 | tf_op jit(solution)/shard_map/ppermute | solution.py:85
  72.3 31.5 %collective-permute-start.11 = (bf16[6144,128]{1,0:T(8,128)(2,1)S(1)}, bf16[6144,128]{1,0:T(8,128)(2,1)S(1)}, u32[]{:S(2)}, u32[]{:S(2)}) collective-permute-start(bf16[6144,128]{1,0:T(8,128)(2,1)S(1)} %get-tuple-element.133), channel_id=1, source_target_pairs={{0,16},{1,17},{2,18},{3,19},{4,20},{5,21},{6,22},{7,23},{8,24},{9,... | collective-permute-start | bytes 4718600 | tf_op jit(solution)/shard_map/ppermute | solution.py:85
  77.9 26.0 %collective-permute-start.9 = (bf16[32,5888]{1,0:T(8,128)(2,1)S(1)}, bf16[32,5888]{1,0:T(8,128)(2,1)S(1)}, u32[]{:S(2)}, u32[]{:S(2)}) collective-permute-start(bf16[32,5888]{1,0:T(8,128)(2,1)S(1)} %concatenate.63), channel_id=1, source_target_pairs={{0,2},{1,3},{2,0},{3,1},{4,6},{5,7},{6,4},{7,5},{8,10},{9,11},{10,... | collective-permute-start | bytes 1130504 | tf_op jit(solution)/shard_map/ppermute | solution.py:85
  106.1 54.1 %collective-permute-start.15 = (bf16[16384,128]{1,0:T(8,128)(2,1)}, bf16[16384,128]{1,0:T(8,128)(2,1)}, u32[]{:S(2)}, u32[]{:S(2)}) collective-permute-start(bf16[16384,128]{1,0:T(8,128)(2,1)} %get-tuple-element.142), channel_id=1, source_target_pairs={{0,4},{1,5},{2,6},{3,7},{4,0},{5,1},{6,2},{7,3},{8,12},{9,13},{10,... | collective-permute-start | bytes 12582920 | tf_op jit(solution)/shard_map/ppermute | solution.py:85
  112.2 48.0 %collective-permute-start.16 = (bf16[5888,128]{1,0:T(8,128)(2,1)}, bf16[5888,128]{1,0:T(8,128)(2,1)}, u32[]{:S(2)}, u32[]{:S(2)}) collective-permute-start(bf16[5888,128]{1,0:T(8,128)(2,1)} %shard_map.571), channel_id=1, source_target_pairs={{0,8},{1,9},{2,10},{3,11},{4,12},{5,13},{6,14},{7,15},{8,0},{9,1},... | collective-permute-start | bytes 4521992 | tf_op jit(solution)/shard_map/ppermute | solution.py:85
  113.7 46.6 %collective-permute-start.17 = (bf16[5888,128]{1,0:T(8,128)(2,1)}, bf16[5888,128]{1,0:T(8,128)(2,1)}, u32[]{:S(2)}, u32[]{:S(2)}) collective-permute-start(bf16[5888,128]{1,0:T(8,128)(2,1)} %shard_map.571), channel_id=1, source_target_pairs={{0,16},{1,17},{2,18},{3,19},{4,20},{5,21},{6,22},{7,23},{8,24},{9,... | collective-permute-start | bytes 4521992 | tf_op jit(solution)/shard_map/ppermute | solution.py:85
  115.1 44.0 %collective-permute-start.14 = (bf16[2048,128]{1,0:T(8,128)(2,1)}, bf16[2048,128]{1,0:T(8,128)(2,1)S(1)}, u32[]{:S(2)}, u32[]{:S(2)}) collective-permute-start(bf16[2048,128]{1,0:T(8,128)(2,1)} %get-tuple-element.141), channel_id=1, source_target_pairs={{0,8},{1,9},{2,10},{3,11},{4,12},{5,13},{6,14},{7,15},{8,0},{9,1},... | collective-permute-start | bytes 1572872 | tf_op jit(solution)/shard_map/ppermute | solution.py:85
  115.6 44.6 %collective-permute-start.13 = (bf16[2048,128]{1,0:T(8,128)(2,1)S(1)}, bf16[2048,128]{1,0:T(8,128)(2,1)S(1)}, u32[]{:S(2)}, u32[]{:S(2)}) collective-permute-start(bf16[2048,128]{1,0:T(8,128)(2,1)S(1)} %copy-done.54), channel_id=1, source_target_pairs={{0,16},{1,17},{2,18},{3,19},{4,20},{5,21},{6,22},{7,23},{8,24},{9,... | collective-permute-start | bytes 1572872 | tf_op jit(solution)/shard_map/ppermute | solution.py:85
  116.3 438.8 %reduce-scatter.14.cloned.1.call-start = ((), (), s32[]{:S(2)}) async-start(), calls=%async_computation.8 | async-start | bytes 1310720 | tf_op jit(solution)/shard_map/reduce_scatter | solution.py:261
  161.9 50.4 %collective-permute-start.22 = (bf16[16384,128]{1,0:T(8,128)(2,1)}, bf16[16384,128]{1,0:T(8,128)(2,1)}, u32[]{:S(2)}, u32[]{:S(2)}) collective-permute-start(bf16[16384,128]{1,0:T(8,128)(2,1)} %constant_dynamic-update-slice_fusion.14), channel_id=1, source_target_pairs={{0,4},{1,5},{2,6},{3,7},{4,0},{5,1},{6,2},{7,3},{8,12},{9,13},{10,... | collective-permute-start | bytes 12582920 | tf_op jit(solution)/shard_map/ppermute | solution.py:85
  169.8 42.6 %collective-permute-start.20 = (bf16[128,4096]{1,0:T(8,128)(2,1)}, bf16[128,4096]{1,0:T(8,128)(2,1)S(1)}, u32[]{:S(2)}, u32[]{:S(2)}) collective-permute-start(bf16[128,4096]{1,0:T(8,128)(2,1)} %get-tuple-element.152), channel_id=1, source_target_pairs={{0,8},{1,9},{2,10},{3,11},{4,12},{5,13},{6,14},{7,15},{8,0},{9,1},... | collective-permute-start | bytes 3145736 | tf_op jit(solution)/shard_map/ppermute | solution.py:85
  171.2 41.1 %collective-permute-start.21 = (bf16[128,4096]{1,0:T(8,128)(2,1)}, bf16[128,4096]{1,0:T(8,128)(2,1)S(1)}, u32[]{:S(2)}, u32[]{:S(2)}) collective-permute-start(bf16[128,4096]{1,0:T(8,128)(2,1)} %get-tuple-element.152), channel_id=1, source_target_pairs={{0,16},{1,17},{2,18},{3,19},{4,20},{5,21},{6,22},{7,23},{8,24},{9,... | collective-permute-start | bytes 3145736 | tf_op jit(solution)/shard_map/ppermute | solution.py:85
  176.8 34.5 %collective-permute-start.19 = (bf16[2944,128]{1,0:T(8,128)(2,1)}, bf16[2944,128]{1,0:T(8,128)(2,1)}, u32[]{:S(2)}, u32[]{:S(2)}) collective-permute-start(bf16[2944,128]{1,0:T(8,128)(2,1)} %slice.302), channel_id=1, source_target_pairs={{0,8},{1,9},{2,10},{3,11},{4,12},{5,13},{6,14},{7,15},{8,0},{9,1},... | collective-permute-start | bytes 2261000 | tf_op jit(solution)/shard_map/ppermute | solution.py:85
  177.3 35.0 %collective-permute-start.18 = (bf16[2944,128]{1,0:T(8,128)(2,1)}, bf16[2944,128]{1,0:T(8,128)(2,1)}, u32[]{:S(2)}, u32[]{:S(2)}) collective-permute-start(bf16[2944,128]{1,0:T(8,128)(2,1)} %slice.301), channel_id=1, source_target_pairs={{0,16},{1,17},{2,18},{3,19},{4,20},{5,21},{6,22},{7,23},{8,24},{9,... | collective-permute-start | bytes 2261000 | tf_op jit(solution)/shard_map/ppermute | solution.py:85
  240.1 49.9 %collective-permute-start.28 = (bf16[512,4096]{1,0:T(8,128)(2,1)}, bf16[512,4096]{1,0:T(8,128)(2,1)}, u32[]{:S(2)}, u32[]{:S(2)}) collective-permute-start(bf16[512,4096]{1,0:T(8,128)(2,1)} %constant_dynamic-update-slice_fusion.33.own_ref.own_up), channel_id=1, source_target_pairs={{0,4},{1,5},{2,6},{3,7},{4,0},{5,1},{6,2},{7,3},{8,12},{9,13},{10,... | collective-permute-start | bytes 12582920 | tf_op jit(solution)/shard_map/ppermute | solution.py:85
  248.3 41.7 %collective-permute-start.26 = (bf16[128,4096]{1,0:T(8,128)(2,1)}, bf16[128,4096]{1,0:T(8,128)(2,1)S(1)}, u32[]{:S(2)}, u32[]{:S(2)}) collective-permute-start(bf16[128,4096]{1,0:T(8,128)(2,1)} %get-tuple-element.166), channel_id=1, source_target_pairs={{0,8},{1,9},{2,10},{3,11},{4,12},{5,13},{6,14},{7,15},{8,0},{9,1},... | collective-permute-start | bytes 3145736 | tf_op jit(solution)/shard_map/ppermute | solution.py:85
  249.6 40.3 %collective-permute-start.27 = (bf16[128,4096]{1,0:T(8,128)(2,1)}, bf16[128,4096]{1,0:T(8,128)(2,1)}, u32[]{:S(2)}, u32[]{:S(2)}) collective-permute-start(bf16[128,4096]{1,0:T(8,128)(2,1)} %get-tuple-element.166), channel_id=1, source_target_pairs={{0,16},{1,17},{2,18},{3,19},{4,20},{5,21},{6,22},{7,23},{8,24},{9,... | collective-permute-start | bytes 3145736 | tf_op jit(solution)/shard_map/ppermute | solution.py:85
  392.7 25.9 %collective-permute-start.33 = (bf16[512,4096]{1,0:T(8,128)(2,1)}, bf16[512,4096]{1,0:T(8,128)(2,1)}, u32[]{:S(2)}, u32[]{:S(2)}) collective-permute-start(bf16[512,4096]{1,0:T(8,128)(2,1)} %shard_map.578.refs_0_), channel_id=1, source_target_pairs={{0,4},{1,5},{2,6},{3,7},{4,0},{5,1},{6,2},{7,3},{8,12},{9,13},{10,... | collective-permute-start | bytes 12582920 | tf_op jit(solution)/shard_map/ppermute | solution.py:85
  446.9 68.3 %collective-permute-start.41 = (bf16[2240,512]{1,0:T(8,128)(2,1)}, bf16[2240,512]{1,0:T(8,128)(2,1)}, u32[]{:S(2)}, u32[]{:S(2)}) collective-permute-start(bf16[2240,512]{1,0:T(8,128)(2,1)} %shard_map.583.refs_19_), channel_id=1, source_target_pairs={{0,4},{1,5},{2,6},{3,7},{4,0},{5,1},{6,2},{7,3},{8,12},{9,13},{10,... | collective-permute-start | bytes 6881288 | tf_op jit(solution)/shard_map/ppermute | solution.py:85
  448.7 56.5 %collective-permute-start.38 = (bf16[128,4096]{1,0:T(8,128)(2,1)}, bf16[128,4096]{1,0:T(8,128)(2,1)}, u32[]{:S(2)}, u32[]{:S(2)}) collective-permute-start(bf16[128,4096]{1,0:T(8,128)(2,1)} %get-tuple-element.440), channel_id=1, source_target_pairs={{0,8},{1,9},{2,10},{3,11},{4,12},{5,13},{6,14},{7,15},{8,0},{9,1},... | collective-permute-start | bytes 3145736 | tf_op jit(solution)/shard_map/ppermute | solution.py:85
  450.0 55.2 %collective-permute-start.39 = (bf16[128,4096]{1,0:T(8,128)(2,1)}, bf16[128,4096]{1,0:T(8,128)(2,1)}, u32[]{:S(2)}, u32[]{:S(2)}) collective-permute-start(bf16[128,4096]{1,0:T(8,128)(2,1)} %get-tuple-element.439), channel_id=1, source_target_pairs={{0,16},{1,17},{2,18},{3,19},{4,20},{5,21},{6,22},{7,23},{8,24},{9,... | collective-permute-start | bytes 3145736 | tf_op jit(solution)/shard_map/ppermute | solution.py:85
  459.1 71.9 %collective-permute-start.42 = (bf16[128,4096]{1,0:T(8,128)(2,1)}, bf16[128,4096]{1,0:T(8,128)(2,1)S(1)}, u32[]{:S(2)}, u32[]{:S(2)}) collective-permute-start(bf16[128,4096]{1,0:T(8,128)(2,1)} %get-tuple-element.438), channel_id=1, source_target_pairs={{0,8},{1,9},{2,10},{3,11},{4,12},{5,13},{6,14},{7,15},{8,0},{9,1},... | collective-permute-start | bytes 3145736 | tf_op jit(solution)/shard_map/ppermute | solution.py:85
  460.0 71.0 %collective-permute-start.43 = (bf16[128,4096]{1,0:T(8,128)(2,1)}, bf16[128,4096]{1,0:T(8,128)(2,1)}, u32[]{:S(2)}, u32[]{:S(2)}) collective-permute-start(bf16[128,4096]{1,0:T(8,128)(2,1)} %get-tuple-element.437), channel_id=1, source_target_pairs={{0,16},{1,17},{2,18},{3,19},{4,20},{5,21},{6,22},{7,23},{8,24},{9,... | collective-permute-start | bytes 3145736 | tf_op jit(solution)/shard_map/ppermute | solution.py:85
  508.6 88.4 %reduce-scatter.16.cloned.1.call-start = ((), (), s32[]{:S(2)}) async-start(), calls=%async_computation.9 | async-start | bytes 1310720 | tf_op jit(solution)/shard_map/reduce_scatter | solution.py:261
  515.2 40.0 %collective-permute-start.40 = (bf16[2240,512]{1,0:T(8,128)(2,1)}, bf16[2240,512]{1,0:T(8,128)(2,1)}, u32[]{:S(2)}, u32[]{:S(2)}) collective-permute-start(bf16[2240,512]{1,0:T(8,128)(2,1)} %shard_map.585.refs_1_), channel_id=1, source_target_pairs={{0,4},{1,5},{2,6},{3,7},{4,0},{5,1},{6,2},{7,3},{8,12},{9,13},{10,... | collective-permute-start | bytes 6881288 | tf_op jit(solution)/shard_map/ppermute | solution.py:85
  522.8 24.7 %collective-permute-start.44 = (bf16[1120,128]{1,0:T(8,128)(2,1)}, bf16[1120,128]{1,0:T(8,128)(2,1)}, u32[]{:S(2)}, u32[]{:S(2)}) collective-permute-start(bf16[1120,128]{1,0:T(8,128)(2,1)} %get-tuple-element.452), channel_id=1, source_target_pairs={{0,16},{1,17},{2,18},{3,19},{4,20},{5,21},{6,22},{7,23},{8,24},{9,... | collective-permute-start | bytes 860168 | tf_op jit(solution)/shard_map/ppermute | solution.py:85
  523.5 24.0 %collective-permute-start.45 = (bf16[1120,128]{1,0:T(8,128)(2,1)}, bf16[1120,128]{1,0:T(8,128)(2,1)}, u32[]{:S(2)}, u32[]{:S(2)}) collective-permute-start(bf16[1120,128]{1,0:T(8,128)(2,1)} %get-tuple-element.451), channel_id=1, source_target_pairs={{0,8},{1,9},{2,10},{3,11},{4,12},{5,13},{6,14},{7,15},{8,0},{9,1},... | collective-permute-start | bytes 860168 | tf_op jit(solution)/shard_map/ppermute | solution.py:85
  547.0 31.0 %collective-permute-start.48 = (bf16[1408,512]{1,0:T(8,128)(2,1)}, bf16[1408,512]{1,0:T(8,128)(2,1)}, u32[]{:S(2)}, u32[]{:S(2)}) collective-permute-start(bf16[1408,512]{1,0:T(8,128)(2,1)} %shard_map.588.refs_1_), channel_id=1, source_target_pairs={{0,4},{1,5},{2,6},{3,7},{4,0},{5,1},{6,2},{7,3},{8,12},{9,13},{10,... | collective-permute-start | bytes 4325384 | tf_op jit(solution)/shard_map/ppermute | solution.py:85
  547.0 52.1 %collective-permute-start.47 = (bf16[4096,512]{1,0:T(8,128)(2,1)}, bf16[4096,512]{1,0:T(8,128)(2,1)}, u32[]{:S(2)}, u32[]{:S(2)}) collective-permute-start(bf16[4096,512]{1,0:T(8,128)(2,1)} %shard_map.587.refs_0_), channel_id=1, source_target_pairs={{0,4},{1,5},{2,6},{3,7},{4,0},{5,1},{6,2},{7,3},{8,12},{9,13},{10,... | collective-permute-start | bytes 12582920 | tf_op jit(solution)/shard_map/ppermute | solution.py:85
  555.1 68.6 %reduce-scatter.22.cloned.1.call-start = ((), (), s32[]{:S(2)}) async-start(), calls=%async_computation.12 | async-start | bytes 737280
  562.9 24.3 %collective-permute-start.49 = (bf16[1120,128]{1,0:T(8,128)(2,1)S(1)}, bf16[1120,128]{1,0:T(8,128)(2,1)S(1)}, u32[]{:S(2)}, u32[]{:S(2)}) collective-permute-start(bf16[1120,128]{1,0:T(8,128)(2,1)S(1)} %get-tuple-element.450), channel_id=1, source_target_pairs={{0,16},{1,17},{2,18},{3,19},{4,20},{5,21},{6,22},{7,23},{8,24},{9,... | collective-permute-start | bytes 860168 | tf_op jit(solution)/shard_map/ppermute | solution.py:85
  565.0 23.6 %collective-permute-start.50 = (bf16[1120,128]{1,0:T(8,128)(2,1)S(1)}, bf16[1120,128]{1,0:T(8,128)(2,1)S(1)}, u32[]{:S(2)}, u32[]{:S(2)}) collective-permute-start(bf16[1120,128]{1,0:T(8,128)(2,1)S(1)} %get-tuple-element.449), channel_id=1, source_target_pairs={{0,8},{1,9},{2,10},{3,11},{4,12},{5,13},{6,14},{7,15},{8,0},{9,1},... | collective-permute-start | bytes 860168 | tf_op jit(solution)/shard_map/ppermute | solution.py:85
  578.0 56.6 %collective-permute-start.46 = (bf16[4096,512]{1,0:T(8,128)(2,1)}, bf16[4096,512]{1,0:T(8,128)(2,1)}, u32[]{:S(2)}, u32[]{:S(2)}) collective-permute-start(bf16[4096,512]{1,0:T(8,128)(2,1)} %shard_map.590.refs_1_), channel_id=1, source_target_pairs={{0,4},{1,5},{2,6},{3,7},{4,0},{5,1},{6,2},{7,3},{8,12},{9,13},{10,... | collective-permute-start | bytes 12582920 | tf_op jit(solution)/shard_map/ppermute | solution.py:85
  595.6 37.7 %collective-permute-start.65 = (bf16[1408,128]{1,0:T(8,128)(2,1)}, bf16[1408,128]{1,0:T(8,128)(2,1)}, u32[]{:S(2)}, u32[]{:S(2)}) collective-permute-start(bf16[1408,128]{1,0:T(8,128)(2,1)} %get-tuple-element.465), channel_id=1, source_target_pairs={{0,8},{1,9},{2,10},{3,11},{4,12},{5,13},{6,14},{7,15},{8,0},{9,1},... | collective-permute-start | bytes 1081352 | tf_op jit(solution)/shard_map/ppermute | solution.py:85
  599.1 49.3 %reduce-scatter.24.cloned.1.call-start = ((), (), s32[]{:S(2)}) async-start(), calls=%async_computation.13 | async-start | bytes 737280
  599.2 34.0 %collective-permute-start.66 = (bf16[1408,128]{1,0:T(8,128)(2,1)}, bf16[1408,128]{1,0:T(8,128)(2,1)}, u32[]{:S(2)}, u32[]{:S(2)}) collective-permute-start(bf16[1408,128]{1,0:T(8,128)(2,1)} %get-tuple-element.466), channel_id=1, source_target_pairs={{0,16},{1,17},{2,18},{3,19},{4,20},{5,21},{6,22},{7,23},{8,24},{9,... | collective-permute-start | bytes 1081352 | tf_op jit(solution)/shard_map/ppermute | solution.py:85
  627.1 45.6 %reduce-scatter.26.cloned.1.call-start = ((), (), s32[]{:S(2)}) async-start(), calls=%async_computation.14 | async-start | bytes 450560
  630.3 26.4 %collective-permute-start.62 = (bf16[4096,128]{1,0:T(8,128)(2,1)}, bf16[4096,128]{1,0:T(8,128)(2,1)}, u32[]{:S(2)}, u32[]{:S(2)}) collective-permute-start(bf16[4096,128]{1,0:T(8,128)(2,1)} %get-tuple-element.429), channel_id=1, source_target_pairs={{0,8},{1,9},{2,10},{3,11},{4,12},{5,13},{6,14},{7,15},{8,0},{9,1},... | collective-permute-start | bytes 3145736 | tf_op jit(solution)/shard_map/ppermute | solution.py:85
  631.8 26.2 %collective-permute-start.64 = (bf16[4096,128]{1,0:T(8,128)(2,1)S(1)}, bf16[4096,128]{1,0:T(8,128)(2,1)}, u32[]{:S(2)}, u32[]{:S(2)}) collective-permute-start(bf16[4096,128]{1,0:T(8,128)(2,1)S(1)} %get-tuple-element.430), channel_id=1, source_target_pairs={{0,16},{1,17},{2,18},{3,19},{4,20},{5,21},{6,22},{7,23},{8,24},{9,... | collective-permute-start | bytes 3145736 | tf_op jit(solution)/shard_map/ppermute | solution.py:85
  647.3 26.6 %collective-permute-start.57 = (bf16[2048,128]{1,0:T(8,128)(2,1)}, bf16[2048,128]{1,0:T(8,128)(2,1)S(1)}, u32[]{:S(2)}, u32[]{:S(2)}) collective-permute-start(bf16[2048,128]{1,0:T(8,128)(2,1)} %get-tuple-element.435), channel_id=1, source_target_pairs={{0,16},{1,17},{2,18},{3,19},{4,20},{5,21},{6,22},{7,23},{8,24},{9,... | collective-permute-start | bytes 1572872 | tf_op jit(solution)/shard_map/ppermute | solution.py:85
  647.9 26.0 %collective-permute-start.59 = (bf16[2048,128]{1,0:T(8,128)(2,1)}, bf16[2048,128]{1,0:T(8,128)(2,1)}, u32[]{:S(2)}, u32[]{:S(2)}) collective-permute-start(bf16[2048,128]{1,0:T(8,128)(2,1)} %get-tuple-element.436), channel_id=1, source_target_pairs={{0,8},{1,9},{2,10},{3,11},{4,12},{5,13},{6,14},{7,15},{8,0},{9,1},... | collective-permute-start | bytes 1572872 | tf_op jit(solution)/shard_map/ppermute | solution.py:85
  650.6 52.9 %reduce-scatter.18.cloned.1.call-start = ((), (), s32[]{:S(2)}) async-start(), calls=%async_computation.10 | async-start | bytes 1310720 | tf_op jit(solution)/shard_map/reduce_scatter | solution.py:261
  673.8 54.7 %reduce-scatter.20.cloned.1.call-start = ((), (), s32[]{:S(2)}) async-start(), calls=%async_computation.11 | async-start | bytes 1310720 | tf_op jit(solution)/shard_map/reduce_scatter | solution.py:261
  675.9 23.7 %collective-permute-start.58 = (bf16[4096,128]{1,0:T(8,128)(2,1)S(1)}, bf16[4096,128]{1,0:T(8,128)(2,1)S(1)}, u32[]{:S(2)}, u32[]{:S(2)}) collective-permute-start(bf16[4096,128]{1,0:T(8,128)(2,1)S(1)} %get-tuple-element.433), channel_id=1, source_target_pairs={{0,8},{1,9},{2,10},{3,11},{4,12},{5,13},{6,14},{7,15},{8,0},{9,1},... | collective-permute-start | bytes 3145736 | tf_op jit(solution)/shard_map/ppermute | solution.py:85
  677.3 23.5 %collective-permute-start.60 = (bf16[4096,128]{1,0:T(8,128)(2,1)S(1)}, bf16[4096,128]{1,0:T(8,128)(2,1)S(1)}, u32[]{:S(2)}, u32[]{:S(2)}) collective-permute-start(bf16[4096,128]{1,0:T(8,128)(2,1)S(1)} %get-tuple-element.434), channel_id=1, source_target_pairs={{0,16},{1,17},{2,18},{3,19},{4,20},{5,21},{6,22},{7,23},{8,24},{9,... | collective-permute-start | bytes 3145736 | tf_op jit(solution)/shard_map/ppermute | solution.py:85
  (126 other events, 1585.9 us)
Sparse Core Ops, SparseCore 0:
  116.4 49.3 all-gather.1
  508.7 29.7 reduce-scatter.13
  555.2 29.5 reduce-scatter.15
  599.2 24.4 reduce-scatter.21
  627.3 20.3 reduce-scatter.23
  650.7 21.9 reduce-scatter.25
  675.0 25.2 reduce-scatter.17
  703.6 24.8 reduce-scatter.19

commit v2 on v1

--- a/solution.py
+++ b/solution.py
@@ -205,7 +205,7 @@
 class Reduce:
     def __init__(self, grid, part, columns=False, turned=False):
         self.grid, self.part = grid, part
-        self.met = self.sums = ()
+        self.met = self.sums = self.away = ()
         self.columns, self.turned = columns, turned
 
     def pair(self, *ties):
@@ -239,7 +239,7 @@
             first, second = (part.astype(single) for part in self.met)
             to_near = self.blocks[1].astype(single) + jnp.pad(first, ((0, rows - middle), (0, 0)))
             to_outer = self.blocks[2].astype(single) + jnp.pad(second, ((middle, 0), (0, 0)))
-            one, two = to_near.astype(bfloat), to_outer.astype(bfloat)
+            one, two = self.away = (to_near.astype(bfloat), to_outer.astype(bfloat))
             self.sums = came(grid.queued(one, near), grid.queued(two, outer))
             total = self.blocks[0].astype(single)
             for part in self.sums:
@@ -670,6 +670,24 @@
     )(*grads, vectors, normed, rel, *came, *ties)
 
 
+def rows_kernel(own_ref, other_ref, out_ref):
+    out_ref[...] = lanes(own_ref, other_ref)
+
+
+def rows_of(sides, start, rows):
+    blocks, _, width = sides[0].shape
+    block = pl.BlockSpec((blocks, rows, width), lambda i: (0, start // rows, 0))
+    return pl.pallas_call(
+        rows_kernel,
+        grid=(1,),
+        in_specs=[block, block],
+        out_specs=fixed(rows, D),
+        out_shape=jax.ShapeDtypeStruct((rows, D), bfloat),
+        compiler_params=params,
+        cost_estimate=light,
+    )(*sides)
+
+
 def lookup_kernel(first, ids_ref, own_ref, other_ref, out_ref):
     tile = pl.program_id(0)
     rows = own_ref.shape[1]
@@ -931,9 +949,7 @@
     contracting.neighbours()
     expanding.pair()
     attention = attending.by_block()
-    last_rows = jnp.concatenate(
-        [side[i, GATE_ROW:] for side in attention for i in range(side.shape[0])], axis=1
-    )
+    last_rows = rows_of(attention, GATE_ROW, LAST_ROWS)
     gains = last_rows[GATES : GATES + 4].astype(single)
 
     stream = jnp.concatenate([memory_rows, embedded], axis=0)
@@ -1025,7 +1041,7 @@
         stored,
         value_gates,
         output_gates,
-        [outputting.high, *contracting.met, *expanding.met],
+        [outputting.high, *contracting.away, *expanding.away],
     )
     grad_values = grad_values.reshape(H * EXPERT, SPAN)
     valuing = summing_turned(normed, grad_values)
@@ -1045,11 +1061,9 @@
         grad_normed.astype(single), normal_in, spread_in, gains[0]
     )
     grad_embedded = (grad_residual + grad_stream[MEM:]).astype(bfloat)
-    nothing = jnp.zeros((D,), single)
-    grad_vectors = jnp.stack(
-        [nothing] * GATES
-        + [grad_gain_in, grad_gain_mid, grad_gain_out, grad_bias_down]
-        + [nothing] * (LAST_ROWS - GATES - 4)
+    grad_vectors = jnp.pad(
+        jnp.stack([grad_gain_in, grad_gain_mid, grad_gain_out, grad_bias_down]),
+        ((GATES, LAST_ROWS - GATES - 4), (0, 0)),
     )
 
     def table_summing(first):

time: 794 us -> 787 us (level)
    unnamed x224 -> x205, local copies, waits for them, and re-layouts: 46.3 us -> 45.7 us
  transfers between devices with their start and end apart: 80 -> 80, of which waited for: 30 -> 29; matrix products, arithmetic and copies ran while one was open for 21% -> 20% of each run, Pallas kernels for 27% -> 27%
where the time goes in v2:
time: 787 us; the launch traced here: 775 us
  Pallas kernels  267 us (34%)
  waiting for transfers between devices  201 us (26%)
  other arithmetic  109 us (14%)
  local copies, waits for them, and re-layouts  90.2 us (11%)
  starting transfers between devices  74.2 us (9%)
  between operations  25.1 us (3%)
  matrix products  7.91 us (1%)
    ppermute x72, waiting for transfers between devices, swap(): return lax.ppermute(part, BOTH, [(i, i ^ flip) for i in range(self.count)])  162 us
    ppermute x72, starting transfers between devices, swap(): return lax.ppermute(part, BOTH, [(i, i ^ flip) for i in range(self.count)])  73.6 us
    unnamed x205, local copies, waits for them, and re-layouts  45.7 us
    pallas_call x1, Pallas kernels, head(): pl.pallas_call(functools.partial(head_kernel, shard_rows, shard_half), gr...  42.6 us
    pallas_call x4, Pallas kernels, table_product(): pl.pallas_call(functools.partial(table_product_kernel, first, len(came)),...  40.1 us
    pallas_call x1, Pallas kernels, mix_back(): pl.pallas_call(mix_back_kernel, grid=(H,), in_specs=[fixed(SEG, D)] + wei...  33.2 us
    pallas_call x1, Pallas kernels, mix(): pl.pallas_call(mix_kernel, grid=(H,), in_specs=[fixed(SPAN, D), fixed(SPA...  29.6 us
    pallas_call x4, Pallas kernels, ff_product(): pl.pallas_call(functools.partial(product_kernel, 0, len(came)), grid=(FF...  27.4 us
  transfers between devices with their start and end apart: 80, of which 29 were waited for; matrix products, arithmetic and copies ran while one was open for 20% of the time, Pallas kernels for 27%

profile of v2, /device:TPU:0, one launch (start us, length us, event | category | flops | bytes accessed | tf_op | source)
XLA Modules:
  0.0 774.6 jit_solution(313978438766554261)
XLA Ops:
  8.7 3.1 collective-permute-start
  14.5 8.1 %fusion.19 = (bf16[1024,512]{1,0:T(8,128)(2,1)S(1)}, bf16[1024,512]{1,0:T(8,128)(2,1)S(1)}) fusion(f32[512]{0:T(512)S(1)} %multiply_exponential_fusion, f32[1024]{0:T(1024)S(1)} %rev.3), kind=kLoop, calls=%fused_computation.34 | loop fusion | flops 1572864 | bytes 2103296 | tf_op jit(solution)/shard_map/convert.39
  22.7 3.7 fusion.30.refs_1_.rel
  29.0 4.1 collective-permute-done.1
  40.7 4.8 collective-permute-start.5
  49.8 4.2 collective-permute-done.5
  54.0 12.7 %collective-permute-done.6 = bf16[1024,128]{1,0:T(8,128)(2,1)S(1)} collective-permute-done((bf16[1024,128]{1,0:T(8,128)(2,1)}, bf16[1024,128]{1,0:T(8,128)(2,1)S(1)}, u32[]{:S(2)}, u32[]{:S(2)}) %collective-permute-start.6) | collective-permute-done | bytes 262176 | tf_op jit(solution)/shard_map/ppermute | solution.py:85
  81.0 5.3 collective-permute-done.10
  86.3 4.8 collective-permute-done.8
  91.0 12.6 %collective-permute-done.9 = bf16[32,5888]{1,0:T(8,128)(2,1)S(1)} collective-permute-done((bf16[32,5888]{1,0:T(8,128)(2,1)S(1)}, bf16[32,5888]{1,0:T(8,128)(2,1)S(1)}, u32[]{:S(2)}, u32[]{:S(2)}) %collective-permute-start.9) | collective-permute-done | bytes 376864 | tf_op jit(solution)/shard_map/ppermute | solution.py:85
  119.4 38.1 %collective-permute-done.14 = bf16[2048,128]{1,0:T(8,128)(2,1)S(1)} collective-permute-done((bf16[2048,128]{1,0:T(8,128)(2,1)}, bf16[2048,128]{1,0:T(8,128)(2,1)S(1)}, u32[]{:S(2)}, u32[]{:S(2)}) %collective-permute-start.14) | collective-permute-done | bytes 524320 | tf_op jit(solution)/shard_map/ppermute | solution.py:85
  166.5 4.0 constant_dynamic-update-slice_fusion.34
  177.6 9.1 %shard_map.572 = f32[512,1024]{1,0:T(8,128)} custom-call(s32[512,1]{1,0:T(8,128)} %fusion.77.ids_ref, bf16[4,4096,128]{2,1,0:T(8,128)(2,1)} %bitcast.8.own_ref.own_zero, bf16[4,4096,128]{2,1,0:T(8,128)(2,1)} %bitcast.9.other_ref.other_zero), custom_call_target="tpu_custom_call" | custom-call | flops 10000000 | bytes 100000 | tf_op jit(solution)/shard_map/pallas_call | solution.py:711
  188.3 24.1 %collective-permute-done.19 = bf16[2944,128]{1,0:T(8,128)(2,1)} collective-permute-done((bf16[2944,128]{1,0:T(8,128)(2,1)}, bf16[2944,128]{1,0:T(8,128)(2,1)}, u32[]{:S(2)}, u32[]{:S(2)}) %collective-permute-start.19) | collective-permute-done | bytes 753696 | tf_op jit(solution)/shard_map/ppermute | solution.py:85
  222.7 9.0 %shard_map.573 = f32[512,1024]{1,0:T(8,128)} custom-call(s32[512,1]{1,0:T(8,128)} %fusion.77.ids_ref, bf16[4,4096,128]{2,1,0:T(8,128)(2,1)} %bitcast.10.own_ref.own_one, bf16[4,4096,128]{2,1,0:T(8,128)(2,1)} %bitcast.12.other_ref.other_one), custom_call_target="tpu_custom_call" | custom-call | flops 10000000 | bytes 100000 | tf_op jit(solution)/shard_map/pallas_call | solution.py:711
  236.2 3.1 constant_dynamic-update-slice_fusion.27
  261.0 29.6 %shard_map.575 = (bf16[4,112,512]{2,1,0:T(8,128)(2,1)}, bf16[4,112,512]{2,1,0:T(8,128)(2,1)}, bf16[4,112,1024]{2,1,0:T(8,128)(2,1)}, bf16[4,112,1024]{2,1,0:T(8,...) custom-call(bf16[1024,1024]{1,0:T(8,128)(2,1)} %copy-done.4, ...), custom_call_target="tpu_custom_call" | custom-call | flops 10000000 | bytes 100000 | tf_op jit(solution)/shard_map/pallas_call | solution.py:429
  298.0 7.5 collective-permute-done.30
  315.9 12.2 %shard_map.576 = (bf16[512,4096]{1,0:T(8,128)(2,1)}, bf16[512,4096]{1,0:T(8,128)(2,1)}) custom-call(bf16[512,1024]{1,0:T(8,128)(2,1)} %multiply_convert_fusion.2.in_ref.left_ref, bf16[512,4096]{1,0:T(8,128)(2,1)} %constant_dynamic-update-slice_fusion.25.own_ref.own_up, bf16[512,4096]{1,0:T(8,128)(2,1)} %collective-permute-done.28.other_ref.other_up, ...), custom_call_target="tpu_custom_call" | custom-call | flops 10000000 | bytes 100000 | tf_op jit(solution)/shard_map/pallas_call | solution.py:494
  328.0 9.2 %shard_map.577 = f32[512,1024]{1,0:T(8,128)} custom-call(bf16[512,4096]{1,0:T(8,128)(2,1)} %get-tuple-element.169.act_ref.right_ref, bf16[512,4096]{1,0:T(8,128)(2,1)} %constant_dynamic-update-slice_fusion.30.own_ref.own_down, bf16[512,4096]{1,0:T(8,128)(2,1)} %collective-permute-done.31.other_ref.other_down), custom_call_target="tpu_custom_call" | custom-call | flops 10000000 | bytes 100000 | tf_op jit(solution)/shard_map/pallas_call | solution.py:515
  341.2 42.6 %shard_map.578 = (bf16[512,8192]{1,0:T(8,128)(2,1)}, bf16[512,1024]{1,0:T(8,128)(2,1)}, f32[512,1]{1,0:T(8,128)}) custom-call(bf16[512,1024]{1,0:T(8,128)(2,1)} %multiply_convert_fusion.1.hf_ref.out_grad, s32[512,1]{1,0:T(8,128)} %fusion.81.goal_ref, f32[512,1]{1,0:T(8,128)} %fusion.91.counted_ref, bf16[4,4096,128]{2,1,0:T(8,128)(2,1)} %bitcast.8.own_ref.own_zero, ...), custom_call_target="tpu_custom_call" | custom-call | flops 10000000 | bytes 100000 | tf_op jit(solution)/shard_map/pallas_call | solution.py:821
  387.7 6.3 shard_map.579.refs_0_
  394.5 15.4 %shard_map.580 = (bf16[512,4096]{1,0:T(8,128)(2,1)}, f32[1,4096]{1,0:T(1,128)}, bf16[512,1024]{1,0:T(8,128)(2,1)}) custom-call(bf16[512,1024]{1,0:T(8,128)(2,1)} %get-tuple-element.401.left_ref.in_ref, bf16[512,4096]{1,0:T(8,128)(2,1)} %get-tuple-element.178.slope_ref, bf16[512,4096]{1,0:T(8,128)(2,1)} %constant_dynamic-update-slice_fusion.30.own_ref.own_down, ...), custom_call_target="tpu_custom_call" | custom-call | flops 10000000 | bytes 100000 | tf_op jit(solution)/shard_map/pallas_call | solution.py:549
  410.0 6.5 shard_map.581.refs_1_
  420.0 7.4 shard_map.582.refs_1_
  431.7 7.3 shard_map.583.refs_0_
  443.2 5.0 shard_map.584.refs_19_
  448.3 3.1 add_convert_fusion.11
  461.4 33.2 %shard_map.585 = (bf16[4,112,1024]{2,1,0:T(8,128)(2,1)}, bf16[4,112,1024]{2,1,0:T(8,128)(2,1)}, bf16[4,112,1024]{2,1,0:T(8,128)(2,1)}, bf16[4,560,1024]{2,1,0:T(...) custom-call(bf16[512,1024]{1,0:T(8,128)(2,1)} %get-tuple-element.405, ...), custom_call_target="tpu_custom_call" | custom-call | flops 10000000 | bytes 100000 | tf_op jit(solution)/shard_map/pallas_call | solution.py:459
  498.6 4.0 fusion
  504.7 3.3 add_convert_fusion.7
  508.0 6.6 shard_map.586.refs_1_
  514.6 5.3 shard_map.587.refs_0_
  524.3 9.6 %shard_map.588.refs_0_ = bf16[4096,512]{1,0:T(8,128)(2,1)} custom-call(bf16[512,8192]{1,0:T(8,128)(2,1)} %get-tuple-element.194.grad_ref, s32[1,512]{1,0:T(1,128)} %get-tuple-element.403.ids_ref, bf16[512,1024]{1,0:T(8,128)(2,1)} %multiply_convert_fusion.1.hf_ref.out_grad, bf16[512,1024]{1,0:T(8,128)(2,1)} %fusion.38.in_grad, ...), custom_call_target="tpu_custom_call" | custom-call | flops 10000000 | bytes 100000 | tf_op jit(solution)/shard_map/pallas_call | solution.py:621
  534.0 5.5 shard_map.589.refs_1_
  543.5 3.3 add_convert_fusion.8
  546.9 6.6 shard_map.590.refs_0_
  558.4 9.6 %shard_map.591.refs_1_ = bf16[4096,512]{1,0:T(8,128)(2,1)} custom-call(bf16[512,8192]{1,0:T(8,128)(2,1)} %get-tuple-element.194.grad_ref, s32[1,512]{1,0:T(1,128)} %get-tuple-element.403.ids_ref, bf16[512,1024]{1,0:T(8,128)(2,1)} %multiply_convert_fusion.1.hf_ref.out_grad, bf16[512,1024]{1,0:T(8,128)(2,1)} %fusion.38.in_grad, ...), custom_call_target="tpu_custom_call" | custom-call | flops 10000000 | bytes 100000 | tf_op jit(solution)/shard_map/pallas_call | solution.py:621
  568.1 5.9 shard_map.592.refs_1_
  589.6 10.4 %shard_map.593.refs_1_ = bf16[4096,512]{1,0:T(8,128)(2,1)} custom-call(bf16[512,8192]{1,0:T(8,128)(2,1)} %get-tuple-element.194.grad_ref, s32[1,512]{1,0:T(1,128)} %get-tuple-element.403.ids_ref, bf16[512,1024]{1,0:T(8,128)(2,1)} %multiply_convert_fusion.1.hf_ref.out_grad, bf16[512,1024]{1,0:T(8,128)(2,1)} %fusion.38.in_grad, ...), custom_call_target="tpu_custom_call" | custom-call | flops 10000000 | bytes 100000 | tf_op jit(solution)/shard_map/pallas_call | solution.py:621
  605.6 8.0 %reduce-scatter.22.cloned.1.call-done = bf16[32,2240]{1,0:T(8,128)(2,1)} async-done(((bf16[128,2240]{1,0:T(8,128)(2,1)}), bf16[32,2240]{1,0:T(8,128)(2,1)}) %reduce-scatter.22.cloned.1.call-update) | async-done | bytes 143376
  624.3 10.4 %shard_map.594 = bf16[4096,512]{1,0:T(8,128)(2,1)} custom-call(bf16[512,8192]{1,0:T(8,128)(2,1)} %get-tuple-element.194.grad_ref, s32[1,512]{1,0:T(1,128)} %get-tuple-element.403.ids_ref, bf16[512,1024]{1,0:T(8,128)(2,1)} %multiply_convert_fusion.1.hf_ref.out_grad, bf16[512,1024]{1,0:T(8,128)(2,1)} %fusion.38.in_grad, ...), custom_call_target="tpu_custom_call" | custom-call | flops 10000000 | bytes 100000 | tf_op jit(solution)/shard_map/pallas_call | solution.py:621
  640.4 6.1 collective-permute-done.62
  647.8 3.3 add_convert_fusion.1
  651.0 11.8 %reduce-scatter.26.cloned.1.call-done = bf16[32,1408]{1,0:T(8,128)(2,1)} async-done(((bf16[128,1408]{1,0:T(8,128)(2,1)}), bf16[32,1408]{1,0:T(8,128)(2,1)}) %reduce-scatter.26.cloned.1.call-update) | async-done | bytes 90128
  669.3 20.2 %collective-permute-done.58 = bf16[4096,128]{1,0:T(8,128)(2,1)S(1)} collective-permute-done((bf16[4096,128]{1,0:T(8,128)(2,1)S(1)}, bf16[4096,128]{1,0:T(8,128)(2,1)S(1)}, u32[]{:S(2)}, u32[]{:S(2)}) %collective-permute-start.58) | collective-permute-done | bytes 1048608 | tf_op jit(solution)/shard_map/ppermute | solution.py:85
  699.4 19.3 %reduce-scatter.20.cloned.1.call-done = bf16[1024,128]{1,0:T(8,128)(2,1)} async-done(((bf16[4096,128]{1,0:T(8,128)(2,1)}), bf16[1024,128]{1,0:T(8,128)(2,1)}) %reduce-scatter.20.cloned.1.call-update) | async-done | bytes 262160 | tf_op jit(solution)/shard_map/reduce_scatter | solution.py:261
  734.5 3.8 collective-permute-done.70
  (535 shorter events, 260.7 us)
Async XLA Ops:
  7.2 159.2 %all-gather.2.cloned.1.call-start = ((), (), s32[]{:S(2)}) async-start(), calls=%async_computation.7 | async-start | bytes 2621440 | tf_op jit(solution)/shard_map/all_gather | solution.py:927
  11.7 21.4 %collective-permute-start.1 = (bf16[1024,128]{1,0:T(8,128)(2,1)S(1)}, bf16[1024,128]{1,0:T(8,128)(2,1)S(1)}, u32[]{:S(2)}, u32[]{:S(2)}) collective-permute-start(bf16[1024,128]{1,0:T(8,128)(2,1)S(1)} %slice.344), channel_id=1, source_target_pairs={{0,2},{1,3},{2,0},{3,1},{4,6},{5,7},{6,4},{7,5},{8,10},{9,11},{10,... | collective-permute-start | bytes 786440 | tf_op jit(solution)/shard_map/ppermute | solution.py:85
  37.7 29.0 %collective-permute-start.3 = (bf16[4096,128]{1,0:T(8,128)(2,1)}, bf16[4096,128]{1,0:T(8,128)(2,1)S(1)}, u32[]{:S(2)}, u32[]{:S(2)}) collective-permute-start(bf16[4096,128]{1,0:T(8,128)(2,1)} %pad_maximum_fusion.2), channel_id=1, source_target_pairs={{0,8},{1,9},{2,10},{3,11},{4,12},{5,13},{6,14},{7,15},{8,0},{9,1},... | collective-permute-start | bytes 3145736 | tf_op jit(solution)/shard_map/ppermute | solution.py:85
  39.1 27.5 %collective-permute-start.4 = (bf16[4096,128]{1,0:T(8,128)(2,1)}, bf16[4096,128]{1,0:T(8,128)(2,1)}, u32[]{:S(2)}, u32[]{:S(2)}) collective-permute-start(bf16[4096,128]{1,0:T(8,128)(2,1)} %pad_maximum_fusion.2), channel_id=1, source_target_pairs={{0,16},{1,17},{2,18},{3,19},{4,20},{5,21},{6,22},{7,23},{8,24},{9,... | collective-permute-start | bytes 3145736 | tf_op jit(solution)/shard_map/ppermute | solution.py:85
  71.5 32.1 %collective-permute-start.12 = (bf16[6144,128]{1,0:T(8,128)(2,1)S(1)}, bf16[6144,128]{1,0:T(8,128)(2,1)S(1)}, u32[]{:S(2)}, u32[]{:S(2)}) collective-permute-start(bf16[6144,128]{1,0:T(8,128)(2,1)S(1)} %get-tuple-element.134), channel_id=1, source_target_pairs={{0,8},{1,9},{2,10},{3,11},{4,12},{5,13},{6,14},{7,15},{8,0},{9,1},... | collective-permute-start | bytes 4718600 | tf_op jit(solution)/shard_map/ppermute | solution.py:85
  72.1 31.5 %collective-permute-start.11 = (bf16[6144,128]{1,0:T(8,128)(2,1)S(1)}, bf16[6144,128]{1,0:T(8,128)(2,1)S(1)}, u32[]{:S(2)}, u32[]{:S(2)}) collective-permute-start(bf16[6144,128]{1,0:T(8,128)(2,1)S(1)} %get-tuple-element.133), channel_id=1, source_target_pairs={{0,16},{1,17},{2,18},{3,19},{4,20},{5,21},{6,22},{7,23},{8,24},{9,... | collective-permute-start | bytes 4718600 | tf_op jit(solution)/shard_map/ppermute | solution.py:85
  77.6 26.0 %collective-permute-start.9 = (bf16[32,5888]{1,0:T(8,128)(2,1)S(1)}, bf16[32,5888]{1,0:T(8,128)(2,1)S(1)}, u32[]{:S(2)}, u32[]{:S(2)}) collective-permute-start(bf16[32,5888]{1,0:T(8,128)(2,1)S(1)} %concatenate.60), channel_id=1, source_target_pairs={{0,2},{1,3},{2,0},{3,1},{4,6},{5,7},{6,4},{7,5},{8,10},{9,11},{10,... | collective-permute-start | bytes 1130504 | tf_op jit(solution)/shard_map/ppermute | solution.py:85
  105.9 52.9 %collective-permute-start.15 = (bf16[16384,128]{1,0:T(8,128)(2,1)}, bf16[16384,128]{1,0:T(8,128)(2,1)}, u32[]{:S(2)}, u32[]{:S(2)}) collective-permute-start(bf16[16384,128]{1,0:T(8,128)(2,1)} %get-tuple-element.142), channel_id=1, source_target_pairs={{0,4},{1,5},{2,6},{3,7},{4,0},{5,1},{6,2},{7,3},{8,12},{9,13},{10,... | collective-permute-start | bytes 12582920 | tf_op jit(solution)/shard_map/ppermute | solution.py:85
  110.7 48.1 %collective-permute-start.16 = (bf16[5888,128]{1,0:T(8,128)(2,1)}, bf16[5888,128]{1,0:T(8,128)(2,1)S(1)}, u32[]{:S(2)}, u32[]{:S(2)}) collective-permute-start(bf16[5888,128]{1,0:T(8,128)(2,1)} %shard_map.571), channel_id=1, source_target_pairs={{0,8},{1,9},{2,10},{3,11},{4,12},{5,13},{6,14},{7,15},{8,0},{9,1},... | collective-permute-start | bytes 4521992 | tf_op jit(solution)/shard_map/ppermute | solution.py:85
  112.1 46.7 %collective-permute-start.17 = (bf16[5888,128]{1,0:T(8,128)(2,1)}, bf16[5888,128]{1,0:T(8,128)(2,1)}, u32[]{:S(2)}, u32[]{:S(2)}) collective-permute-start(bf16[5888,128]{1,0:T(8,128)(2,1)} %shard_map.571), channel_id=1, source_target_pairs={{0,16},{1,17},{2,18},{3,19},{4,20},{5,21},{6,22},{7,23},{8,24},{9,... | collective-permute-start | bytes 4521992 | tf_op jit(solution)/shard_map/ppermute | solution.py:85
  113.5 44.0 %collective-permute-start.14 = (bf16[2048,128]{1,0:T(8,128)(2,1)}, bf16[2048,128]{1,0:T(8,128)(2,1)S(1)}, u32[]{:S(2)}, u32[]{:S(2)}) collective-permute-start(bf16[2048,128]{1,0:T(8,128)(2,1)} %get-tuple-element.141), channel_id=1, source_target_pairs={{0,8},{1,9},{2,10},{3,11},{4,12},{5,13},{6,14},{7,15},{8,0},{9,1},... | collective-permute-start | bytes 1572872 | tf_op jit(solution)/shard_map/ppermute | solution.py:85
  114.0 44.7 %collective-permute-start.13 = (bf16[2048,128]{1,0:T(8,128)(2,1)}, bf16[2048,128]{1,0:T(8,128)(2,1)}, u32[]{:S(2)}, u32[]{:S(2)}) collective-permute-start(bf16[2048,128]{1,0:T(8,128)(2,1)} %get-tuple-element.140), channel_id=1, source_target_pairs={{0,16},{1,17},{2,18},{3,19},{4,20},{5,21},{6,22},{7,23},{8,24},{9,... | collective-permute-start | bytes 1572872 | tf_op jit(solution)/shard_map/ppermute | solution.py:85
  114.7 432.1 %reduce-scatter.14.cloned.1.call-start = ((), (), s32[]{:S(2)}) async-start(), calls=%async_computation.8 | async-start | bytes 1310720 | tf_op jit(solution)/shard_map/reduce_scatter | solution.py:261
  161.5 51.3 %collective-permute-start.22 = (bf16[16384,128]{1,0:T(8,128)(2,1)}, bf16[16384,128]{1,0:T(8,128)(2,1)}, u32[]{:S(2)}, u32[]{:S(2)}) collective-permute-start(bf16[16384,128]{1,0:T(8,128)(2,1)} %constant_dynamic-update-slice_fusion.14), channel_id=1, source_target_pairs={{0,4},{1,5},{2,6},{3,7},{4,0},{5,1},{6,2},{7,3},{8,12},{9,13},{10,... | collective-permute-start | bytes 12582920 | tf_op jit(solution)/shard_map/ppermute | solution.py:85
  170.4 42.4 %collective-permute-start.20 = (bf16[128,4096]{1,0:T(8,128)(2,1)}, bf16[128,4096]{1,0:T(8,128)(2,1)}, u32[]{:S(2)}, u32[]{:S(2)}) collective-permute-start(bf16[128,4096]{1,0:T(8,128)(2,1)} %get-tuple-element.152), channel_id=1, source_target_pairs={{0,8},{1,9},{2,10},{3,11},{4,12},{5,13},{6,14},{7,15},{8,0},{9,1},... | collective-permute-start | bytes 3145736 | tf_op jit(solution)/shard_map/ppermute | solution.py:85
  171.0 41.8 %collective-permute-start.21 = (bf16[128,4096]{1,0:T(8,128)(2,1)}, bf16[128,4096]{1,0:T(8,128)(2,1)}, u32[]{:S(2)}, u32[]{:S(2)}) collective-permute-start(bf16[128,4096]{1,0:T(8,128)(2,1)} %get-tuple-element.152), channel_id=1, source_target_pairs={{0,16},{1,17},{2,18},{3,19},{4,20},{5,21},{6,22},{7,23},{8,24},{9,... | collective-permute-start | bytes 3145736 | tf_op jit(solution)/shard_map/ppermute | solution.py:85
  175.3 37.1 %collective-permute-start.19 = (bf16[2944,128]{1,0:T(8,128)(2,1)}, bf16[2944,128]{1,0:T(8,128)(2,1)}, u32[]{:S(2)}, u32[]{:S(2)}) collective-permute-start(bf16[2944,128]{1,0:T(8,128)(2,1)} %slice.278), channel_id=1, source_target_pairs={{0,8},{1,9},{2,10},{3,11},{4,12},{5,13},{6,14},{7,15},{8,0},{9,1},... | collective-permute-start | bytes 2261000 | tf_op jit(solution)/shard_map/ppermute | solution.py:85
  176.8 36.0 %collective-permute-start.18 = (bf16[2944,128]{1,0:T(8,128)(2,1)}, bf16[2944,128]{1,0:T(8,128)(2,1)}, u32[]{:S(2)}, u32[]{:S(2)}) collective-permute-start(bf16[2944,128]{1,0:T(8,128)(2,1)} %slice.277), channel_id=1, source_target_pairs={{0,16},{1,17},{2,18},{3,19},{4,20},{5,21},{6,22},{7,23},{8,24},{9,... | collective-permute-start | bytes 2261000 | tf_op jit(solution)/shard_map/ppermute | solution.py:85
  215.2 24.1 %collective-permute-start.23 = (bf16[23552,128]{1,0:T(8,128)(2,1)S(1)}, bf16[23552,128]{1,0:T(8,128)(2,1)}, u32[]{:S(2)}, u32[]{:S(2)}) collective-permute-start(bf16[23552,128]{1,0:T(8,128)(2,1)S(1)} %constant_dynamic-update-slice_fusion.20), channel_id=1, source_target_pairs={{0,4},{1,5},{2,6},{3,7},{4,0},{5,1},{6,2},{7,3},{8,12},{9,13},{10,... | collective-permute-start | bytes 18087944 | tf_op jit(solution)/shard_map/ppermute | solution.py:85
  243.1 47.5 %collective-permute-start.28 = (bf16[512,4096]{1,0:T(8,128)(2,1)}, bf16[512,4096]{1,0:T(8,128)(2,1)}, u32[]{:S(2)}, u32[]{:S(2)}) collective-permute-start(bf16[512,4096]{1,0:T(8,128)(2,1)} %constant_dynamic-update-slice_fusion.25.own_ref.own_up), channel_id=1, source_target_pairs={{0,4},{1,5},{2,6},{3,7},{4,0},{5,1},{6,2},{7,3},{8,12},{9,13},{10,... | collective-permute-start | bytes 12582920 | tf_op jit(solution)/shard_map/ppermute | solution.py:85
  250.0 40.6 %collective-permute-start.26 = (bf16[128,4096]{1,0:T(8,128)(2,1)}, bf16[128,4096]{1,0:T(8,128)(2,1)S(1)}, u32[]{:S(2)}, u32[]{:S(2)}) collective-permute-start(bf16[128,4096]{1,0:T(8,128)(2,1)} %get-tuple-element.166), channel_id=1, source_target_pairs={{0,8},{1,9},{2,10},{3,11},{4,12},{5,13},{6,14},{7,15},{8,0},{9,1},... | collective-permute-start | bytes 3145736 | tf_op jit(solution)/shard_map/ppermute | solution.py:85
  250.6 40.0 %collective-permute-start.27 = (bf16[128,4096]{1,0:T(8,128)(2,1)}, bf16[128,4096]{1,0:T(8,128)(2,1)}, u32[]{:S(2)}, u32[]{:S(2)}) collective-permute-start(bf16[128,4096]{1,0:T(8,128)(2,1)} %get-tuple-element.166), channel_id=1, source_target_pairs={{0,16},{1,17},{2,18},{3,19},{4,20},{5,21},{6,22},{7,23},{8,24},{9,... | collective-permute-start | bytes 3145736 | tf_op jit(solution)/shard_map/ppermute | solution.py:85
  394.0 26.0 %collective-permute-start.33 = (bf16[512,4096]{1,0:T(8,128)(2,1)}, bf16[512,4096]{1,0:T(8,128)(2,1)}, u32[]{:S(2)}, u32[]{:S(2)}) collective-permute-start(bf16[512,4096]{1,0:T(8,128)(2,1)} %shard_map.579.refs_0_), channel_id=1, source_target_pairs={{0,4},{1,5},{2,6},{3,7},{4,0},{5,1},{6,2},{7,3},{8,12},{9,13},{10,... | collective-permute-start | bytes 12582920 | tf_op jit(solution)/shard_map/ppermute | solution.py:85
  448.2 66.4 %collective-permute-start.41 = (bf16[2240,512]{1,0:T(8,128)(2,1)}, bf16[2240,512]{1,0:T(8,128)(2,1)}, u32[]{:S(2)}, u32[]{:S(2)}) collective-permute-start(bf16[2240,512]{1,0:T(8,128)(2,1)} %shard_map.584.refs_19_), channel_id=1, source_target_pairs={{0,4},{1,5},{2,6},{3,7},{4,0},{5,1},{6,2},{7,3},{8,12},{9,13},{10,... | collective-permute-start | bytes 6881288 | tf_op jit(solution)/shard_map/ppermute | solution.py:85
  451.3 53.3 %collective-permute-start.38 = (bf16[128,4096]{1,0:T(8,128)(2,1)}, bf16[128,4096]{1,0:T(8,128)(2,1)}, u32[]{:S(2)}, u32[]{:S(2)}) collective-permute-start(bf16[128,4096]{1,0:T(8,128)(2,1)} %get-tuple-element.442.refs_20_), channel_id=1, source_target_pairs={{0,8},{1,9},{2,10},{3,11},{4,12},{5,13},{6,14},{7,15},{8,0},{9,1},... | collective-permute-start | bytes 3145736 | tf_op jit(solution)/shard_map/ppermute | solution.py:85
  452.0 52.7 %collective-permute-start.39 = (bf16[128,4096]{1,0:T(8,128)(2,1)}, bf16[128,4096]{1,0:T(8,128)(2,1)}, u32[]{:S(2)}, u32[]{:S(2)}) collective-permute-start(bf16[128,4096]{1,0:T(8,128)(2,1)} %get-tuple-element.441.refs_21_), channel_id=1, source_target_pairs={{0,16},{1,17},{2,18},{3,19},{4,20},{5,21},{6,22},{7,23},{8,24},{9,... | collective-permute-start | bytes 3145736 | tf_op jit(solution)/shard_map/ppermute | solution.py:85
  459.0 65.4 %collective-permute-start.42 = (bf16[128,4096]{1,0:T(8,128)(2,1)}, bf16[128,4096]{1,0:T(8,128)(2,1)}, u32[]{:S(2)}, u32[]{:S(2)}) collective-permute-start(bf16[128,4096]{1,0:T(8,128)(2,1)} %get-tuple-element.438.refs_22_), channel_id=1, source_target_pairs={{0,8},{1,9},{2,10},{3,11},{4,12},{5,13},{6,14},{7,15},{8,0},{9,1},... | collective-permute-start | bytes 3145736 | tf_op jit(solution)/shard_map/ppermute | solution.py:85
  460.0 64.4 %collective-permute-start.43 = (bf16[128,4096]{1,0:T(8,128)(2,1)}, bf16[128,4096]{1,0:T(8,128)(2,1)}, u32[]{:S(2)}, u32[]{:S(2)}) collective-permute-start(bf16[128,4096]{1,0:T(8,128)(2,1)} %get-tuple-element.437.refs_23_), channel_id=1, source_target_pairs={{0,16},{1,17},{2,18},{3,19},{4,20},{5,21},{6,22},{7,23},{8,24},{9,... | collective-permute-start | bytes 3145736 | tf_op jit(solution)/shard_map/ppermute | solution.py:85
  508.0 77.6 %reduce-scatter.16.cloned.1.call-start = ((), (), s32[]{:S(2)}) async-start(), calls=%async_computation.9 | async-start | bytes 1310720 | tf_op jit(solution)/shard_map/reduce_scatter | solution.py:261
  514.6 32.3 %collective-permute-start.40 = (bf16[2240,512]{1,0:T(8,128)(2,1)}, bf16[2240,512]{1,0:T(8,128)(2,1)}, u32[]{:S(2)}, u32[]{:S(2)}) collective-permute-start(bf16[2240,512]{1,0:T(8,128)(2,1)} %shard_map.586.refs_1_), channel_id=1, source_target_pairs={{0,4},{1,5},{2,6},{3,7},{4,0},{5,1},{6,2},{7,3},{8,12},{9,13},{10,... | collective-permute-start | bytes 6881288 | tf_op jit(solution)/shard_map/ppermute | solution.py:85
  539.5 28.6 %collective-permute-start.48 = (bf16[1408,512]{1,0:T(8,128)(2,1)}, bf16[1408,512]{1,0:T(8,128)(2,1)}, u32[]{:S(2)}, u32[]{:S(2)}) collective-permute-start(bf16[1408,512]{1,0:T(8,128)(2,1)} %shard_map.589.refs_1_), channel_id=1, source_target_pairs={{0,4},{1,5},{2,6},{3,7},{4,0},{5,1},{6,2},{7,3},{8,12},{9,13},{10,... | collective-permute-start | bytes 4325384 | tf_op jit(solution)/shard_map/ppermute | solution.py:85
  539.5 48.3 %collective-permute-start.47 = (bf16[4096,512]{1,0:T(8,128)(2,1)}, bf16[4096,512]{1,0:T(8,128)(2,1)}, u32[]{:S(2)}, u32[]{:S(2)}) collective-permute-start(bf16[4096,512]{1,0:T(8,128)(2,1)} %shard_map.588.refs_0_), channel_id=1, source_target_pairs={{0,4},{1,5},{2,6},{3,7},{4,0},{5,1},{6,2},{7,3},{8,12},{9,13},{10,... | collective-permute-start | bytes 12582920 | tf_op jit(solution)/shard_map/ppermute | solution.py:85
  546.9 66.7 %reduce-scatter.22.cloned.1.call-start = ((), (), s32[]{:S(2)}) async-start(), calls=%async_computation.12 | async-start | bytes 737280
  554.7 22.4 %collective-permute-start.49 = (bf16[1120,128]{1,0:T(8,128)(2,1)S(1)}, bf16[1120,128]{1,0:T(8,128)(2,1)S(1)}, u32[]{:S(2)}, u32[]{:S(2)}) collective-permute-start(bf16[1120,128]{1,0:T(8,128)(2,1)S(1)} %get-tuple-element.450), channel_id=1, source_target_pairs={{0,16},{1,17},{2,18},{3,19},{4,20},{5,21},{6,22},{7,23},{8,24},{9,... | collective-permute-start | bytes 860168 | tf_op jit(solution)/shard_map/ppermute | solution.py:85
  568.0 56.3 %collective-permute-start.46 = (bf16[4096,512]{1,0:T(8,128)(2,1)}, bf16[4096,512]{1,0:T(8,128)(2,1)}, u32[]{:S(2)}, u32[]{:S(2)}) collective-permute-start(bf16[4096,512]{1,0:T(8,128)(2,1)} %shard_map.591.refs_1_), channel_id=1, source_target_pairs={{0,4},{1,5},{2,6},{3,7},{4,0},{5,1},{6,2},{7,3},{8,12},{9,13},{10,... | collective-permute-start | bytes 12582920 | tf_op jit(solution)/shard_map/ppermute | solution.py:85
  578.3 23.9 %collective-permute-start.53 = (bf16[2240,128]{1,0:T(8,128)(2,1)}, bf16[2240,128]{1,0:T(8,128)(2,1)S(1)}, u32[]{:S(2)}, u32[]{:S(2)}) collective-permute-start(bf16[2240,128]{1,0:T(8,128)(2,1)} %get-tuple-element.446), channel_id=1, source_target_pairs={{0,8},{1,9},{2,10},{3,11},{4,12},{5,13},{6,14},{7,15},{8,0},{9,1},... | collective-permute-start | bytes 1720328 | tf_op jit(solution)/shard_map/ppermute | solution.py:85
  585.5 37.5 %collective-permute-start.65 = (bf16[1408,128]{1,0:T(8,128)(2,1)}, bf16[1408,128]{1,0:T(8,128)(2,1)}, u32[]{:S(2)}, u32[]{:S(2)}) collective-permute-start(bf16[1408,128]{1,0:T(8,128)(2,1)} %get-tuple-element.465), channel_id=1, source_target_pairs={{0,8},{1,9},{2,10},{3,11},{4,12},{5,13},{6,14},{7,15},{8,0},{9,1},... | collective-permute-start | bytes 1081352 | tf_op jit(solution)/shard_map/ppermute | solution.py:85
  587.8 50.4 %reduce-scatter.24.cloned.1.call-start = ((), (), s32[]{:S(2)}) async-start(), calls=%async_computation.13 | async-start | bytes 737280
  587.8 35.2 %collective-permute-start.66 = (bf16[1408,128]{1,0:T(8,128)(2,1)}, bf16[1408,128]{1,0:T(8,128)(2,1)}, u32[]{:S(2)}, u32[]{:S(2)}) collective-permute-start(bf16[1408,128]{1,0:T(8,128)(2,1)} %get-tuple-element.466), channel_id=1, source_target_pairs={{0,16},{1,17},{2,18},{3,19},{4,20},{5,21},{6,22},{7,23},{8,24},{9,... | collective-permute-start | bytes 1081352 | tf_op jit(solution)/shard_map/ppermute | solution.py:85
  616.9 45.9 %reduce-scatter.26.cloned.1.call-start = ((), (), s32[]{:S(2)}) async-start(), calls=%async_computation.14 | async-start | bytes 450560
  620.0 26.4 %collective-permute-start.62 = (bf16[4096,128]{1,0:T(8,128)(2,1)}, bf16[4096,128]{1,0:T(8,128)(2,1)}, u32[]{:S(2)}, u32[]{:S(2)}) collective-permute-start(bf16[4096,128]{1,0:T(8,128)(2,1)} %get-tuple-element.429), channel_id=1, source_target_pairs={{0,8},{1,9},{2,10},{3,11},{4,12},{5,13},{6,14},{7,15},{8,0},{9,1},... | collective-permute-start | bytes 3145736 | tf_op jit(solution)/shard_map/ppermute | solution.py:85
  621.6 26.2 %collective-permute-start.64 = (bf16[4096,128]{1,0:T(8,128)(2,1)S(1)}, bf16[4096,128]{1,0:T(8,128)(2,1)}, u32[]{:S(2)}, u32[]{:S(2)}) collective-permute-start(bf16[4096,128]{1,0:T(8,128)(2,1)S(1)} %get-tuple-element.430), channel_id=1, source_target_pairs={{0,16},{1,17},{2,18},{3,19},{4,20},{5,21},{6,22},{7,23},{8,24},{9,... | collective-permute-start | bytes 3145736 | tf_op jit(solution)/shard_map/ppermute | solution.py:85
  637.0 27.3 %collective-permute-start.57 = (bf16[2048,128]{1,0:T(8,128)(2,1)}, bf16[2048,128]{1,0:T(8,128)(2,1)S(1)}, u32[]{:S(2)}, u32[]{:S(2)}) collective-permute-start(bf16[2048,128]{1,0:T(8,128)(2,1)} %get-tuple-element.435), channel_id=1, source_target_pairs={{0,16},{1,17},{2,18},{3,19},{4,20},{5,21},{6,22},{7,23},{8,24},{9,... | collective-permute-start | bytes 1572872 | tf_op jit(solution)/shard_map/ppermute | solution.py:85
  637.6 26.6 %collective-permute-start.59 = (bf16[2048,128]{1,0:T(8,128)(2,1)}, bf16[2048,128]{1,0:T(8,128)(2,1)}, u32[]{:S(2)}, u32[]{:S(2)}) collective-permute-start(bf16[2048,128]{1,0:T(8,128)(2,1)} %get-tuple-element.436), channel_id=1, source_target_pairs={{0,8},{1,9},{2,10},{3,11},{4,12},{5,13},{6,14},{7,15},{8,0},{9,1},... | collective-permute-start | bytes 1572872 | tf_op jit(solution)/shard_map/ppermute | solution.py:85
  640.3 53.1 %reduce-scatter.18.cloned.1.call-start = ((), (), s32[]{:S(2)}) async-start(), calls=%async_computation.10 | async-start | bytes 1310720 | tf_op jit(solution)/shard_map/reduce_scatter | solution.py:261
  663.9 54.8 %reduce-scatter.20.cloned.1.call-start = ((), (), s32[]{:S(2)}) async-start(), calls=%async_computation.11 | async-start | bytes 1310720 | tf_op jit(solution)/shard_map/reduce_scatter | solution.py:261
  666.3 23.2 %collective-permute-start.58 = (bf16[4096,128]{1,0:T(8,128)(2,1)S(1)}, bf16[4096,128]{1,0:T(8,128)(2,1)S(1)}, u32[]{:S(2)}, u32[]{:S(2)}) collective-permute-start(bf16[4096,128]{1,0:T(8,128)(2,1)S(1)} %get-tuple-element.433), channel_id=1, source_target_pairs={{0,8},{1,9},{2,10},{3,11},{4,12},{5,13},{6,14},{7,15},{8,0},{9,1},... | collective-permute-start | bytes 3145736 | tf_op jit(solution)/shard_map/ppermute | solution.py:85
  667.7 23.0 %collective-permute-start.60 = (bf16[4096,128]{1,0:T(8,128)(2,1)S(1)}, bf16[4096,128]{1,0:T(8,128)(2,1)S(1)}, u32[]{:S(2)}, u32[]{:S(2)}) collective-permute-start(bf16[4096,128]{1,0:T(8,128)(2,1)S(1)} %get-tuple-element.434), channel_id=1, source_target_pairs={{0,16},{1,17},{2,18},{3,19},{4,20},{5,21},{6,22},{7,23},{8,24},{9,... | collective-permute-start | bytes 3145736 | tf_op jit(solution)/shard_map/ppermute | solution.py:85
  (120 other events, 1454.3 us)
Sparse Core Ops, SparseCore 0:
  114.9 49.1 all-gather.1
  508.1 29.4 reduce-scatter.13
  547.0 29.4 reduce-scatter.15
  587.9 25.6 reduce-scatter.21
  617.0 20.2 reduce-scatter.23
  640.5 22.2 reduce-scatter.25
  665.1 25.2 reduce-scatter.17
  693.5 25.1 reduce-scatter.19
